TPU v7x, 32 devices: a whole 2x2x4 slice. The times are simulated.
32 devices in a mesh: blk: 4 (over y, core), head: 4 (over z), dp: 2 (over x).
Axes of the slice: x: 2, y: 2, z: 4, core: 2. Of those that a mesh axis runs over, the one named last changes fastest.
Arguments:
- atoms: float32 [2, 1024, 512], P('dp', 'blk'), may hold values from -6 to 6
- pair: float32 [2, 64, 1024, 1024], P('dp', 'head', 'blk'), may hold values from -6 to 6
- mol_ids: int32 [2, 1024], P('dp', 'blk'), may hold values from 0 to 1023, as said below
- ln1_gain: float32 [512], replicated, may hold values from 0.25 to 1.75
- ln1_bias: float32 [512], replicated, may hold values from -3 to 3
- w_query: float32 [512, 512], P(None, 'head'), may hold values from -0.25 to 0.25
- b_query: float32 [512], P('head'), may hold values from -3 to 3
- w_key: float32 [512, 512], P(None, 'head'), may hold values from -0.25 to 0.25
- w_value: float32 [512, 512], P(None, 'head'), may hold values from -0.25 to 0.25
- b_value: float32 [512], P('head'), may hold values from -3 to 3
- w_out: float32 [512, 512], P('head'), may hold values from -2 to 2
- b_out: float32 [512], replicated, may hold values from -3 to 3
- ln2_gain: float32 [512], replicated, may hold values from 0.25 to 1.75
- ln2_bias: float32 [512], replicated, may hold values from -3 to 3
- w_up: float32 [512, 2048], P(None, 'head'), may hold values from -0.25 to 0.25
- b_up: float32 [2048], P('head'), may hold values from -3 to 3
- w_down: float32 [2048, 512], P('head'), may hold values from -0.125 to 0.125
- b_down: float32 [512], replicated, may hold values from -3 to 3
- cot_atoms: float32 [2, 1024, 512], P('dp', 'blk'), may hold values from -6 to 6
- cot_pair: float32 [2, 64, 1024, 1024], P('dp', 'head', 'blk'), may hold values from -6 to 6
Outputs:
- out_atoms: float32 [2, 1024, 512], P('dp', 'blk')
- out_pair: float32 [2, 64, 1024, 1024], P('dp', 'head', 'blk')
- aux_penalty: float32 [], replicated
- grad_atoms: float32 [2, 1024, 512], P('dp', 'blk')
- grad_pair: float32 [2, 64, 1024, 1024], P('dp', 'head', 'blk')
- grad_ln1_gain: float32 [512], replicated
- grad_ln1_bias: float32 [512], replicated
- grad_w_query: float32 [512, 512], P(None, 'head')
- grad_b_query: float32 [512], P('head')
- grad_w_key: float32 [512, 512], P(None, 'head')
- grad_w_value: float32 [512, 512], P(None, 'head')
- grad_b_value: float32 [512], P('head')
- grad_w_out: float32 [512, 512], P('head')
- grad_b_out: float32 [512], replicated
- grad_ln2_gain: float32 [512], replicated
- grad_ln2_bias: float32 [512], replicated
- grad_w_up: float32 [512, 2048], P(None, 'head')
- grad_b_up: float32 [2048], P('head')
- grad_w_down: float32 [2048, 512], P('head')
- grad_b_down: float32 [512], replicated
Inputs may be any that keep to these rules, and one draw needn't show every extreme that they name: `mol_ids`: non-decreasing by steps of one along the atoms of a group, the last atom numbered 1024 - 1; atoms with equal numbers form one molecule of consecutive atoms; every molecule has at most 768 atoms, and in every group one molecule has exactly 768.
All inputs are finite; a program needn't handle non-finite values.
Results may differ from a plain program's by a relative error of at most 0.0003.
Values sent between devices are 32-bit elements; how exact they have to be, the bound alone decides.
A program may use at most 192 MiB of HBM per device.

v0:
```python
import math

import jax
import jax.numpy as jnp
from jax import lax
from jax.sharding import PartitionSpec as P

H = 64
DH = 8


NORM_EPS = 1e-05
MASK_FILL = -1e30
FULL_PRECISION = lax.Precision.HIGHEST


def from_behind(value, axis, steps):
    count = lax.axis_size(axis)
    pairs = [(source, (source + steps) % count) for source in range(count)]
    return lax.ppermute(value, axis, pairs)


def layer_norm(inputs, scale_gain, shift_bias):
    average = jnp.mean(inputs, -1, keepdims=True)
    centred = inputs - average
    variance = jnp.mean(centred * centred, -1, keepdims=True)
    return centred * lax.rsqrt(variance + NORM_EPS) * scale_gain + shift_bias


def gelu_exact(inputs):
    return jax.nn.gelu(inputs, approximate=False)


def matmul_full(left, right):
    return jnp.dot(left, right, precision=FULL_PRECISION)


def local(
    atoms,
    pair,
    mol_ids,
    ln1_gain,
    ln1_bias,
    w_query,
    b_query,
    w_key,
    w_value,
    b_value,
    w_out,
    b_out,
    ln2_gain,
    ln2_bias,
    w_up,
    b_up,
    w_down,
    b_down,
    cot_atoms,
    cot_pair,
):
    inputs = atoms[0]
    bias_pair = pair[0]
    own_ids = mol_ids[0]
    grad_output = cot_atoms[0]
    grad_cols = cot_pair[0]
    row_count = inputs.shape[0]
    head_count = bias_pair.shape[0]
    feat_width = w_query.shape[1]
    scaling = DH ** (-0.5)
    normed = layer_norm(inputs, ln1_gain, ln1_bias)
    queries = ((matmul_full(normed, w_query) + b_query) * scaling).reshape(
        row_count, head_count, DH
    )
    key_rows = matmul_full(normed, w_key)
    value_rows = matmul_full(normed, w_value) + b_value
    run_max = jnp.full((head_count, row_count), MASK_FILL, jnp.float32)
    weighted = jnp.zeros((row_count, head_count, DH), jnp.float32)
    part_keys = lax.all_gather(key_rows, "blk", axis=0, tiled=True)
    part_values = lax.all_gather(value_rows, "blk", axis=0, tiled=True)
    part_ids = lax.all_gather(own_ids, "blk", axis=0, tiled=True)
    col_count = part_keys.shape[0]
    key_heads = part_keys.reshape(col_count, head_count, DH)
    value_heads = part_values.reshape(col_count, head_count, DH)
    scores = jnp.einsum("rhd,nhd->hrn", queries, key_heads, precision=FULL_PRECISION)
    logits = scores + bias_pair
    same_mol = own_ids[:, None] == part_ids[None, :]
    masked = jnp.where(same_mol[None], logits, MASK_FILL)
    new_max = jnp.maximum(run_max, jnp.max(masked, -1))
    factor = jnp.exp(run_max - new_max)
    weights = jnp.where(same_mol[None], jnp.exp(masked - new_max[:, :, None]), 0.0)
    run_total = jnp.sum(weights, -1)
    weighted = weighted * factor.T[:, :, None] + jnp.einsum(
        "hrn,nhd->rhd", weights, value_heads, precision=FULL_PRECISION
    )
    logits_all = logits
    squares_all = jnp.sum(scores * scores, 0)
    valid_all = same_mol.astype(jnp.float32)
    run_max, run_total, weighted, out_pair, squares, valid = (
        new_max,
        run_total,
        weighted,
        logits_all,
        squares_all,
        valid_all,
    )
    log_total = run_max + jnp.log(run_total)
    mixed = weighted / run_total.T[:, :, None]
    mixed_flat = mixed.reshape(row_count, feat_width)
    attn_part = matmul_full(mixed_flat, w_out)
    attn_sum, square_sum = lax.psum((attn_part, squares), "head")
    hidden = inputs + attn_sum + b_out
    norms = jnp.sqrt(square_sum + 1.0)
    numer = jnp.sum(valid * jnp.log1p(jnp.exp(norms - math.sqrt(H))))
    numer_all, count_all = lax.psum((numer, jnp.sum(valid)), ("blk", "dp"))
    penalty = numer_all / count_all
    normed_two = layer_norm(hidden, ln2_gain, ln2_bias)
    pre_act = matmul_full(normed_two, w_up) + b_up
    activated = gelu_exact(pre_act)
    down_part = matmul_full(activated, w_down)
    ffn_out = lax.psum(down_part, "head")
    result_atoms = hidden + ffn_out + b_down
    g_b_down = jnp.sum(grad_output, 0)
    g_w_down = matmul_full(activated.T, grad_output)
    d_act = matmul_full(grad_output, w_down.T)
    gelu_unused, gelu_pull = jax.vjp(gelu_exact, pre_act)
    d_pre = gelu_pull(d_act)[0]
    g_b_up = jnp.sum(d_pre, 0)
    g_w_up = matmul_full(normed_two.T, d_pre)
    d_normed_two = lax.psum(matmul_full(d_pre, w_up.T), "head")
    norm_unused, norm_two_pull = jax.vjp(layer_norm, hidden, ln2_gain, ln2_bias)
    d_hidden_norm, g_ln2_gain, g_ln2_bias = norm_two_pull(d_normed_two)
    d_hidden = grad_output + d_hidden_norm
    g_b_out = jnp.sum(d_hidden, 0)
    g_w_out = matmul_full(mixed_flat.T, d_hidden)
    d_mixed = matmul_full(d_hidden, w_out.T).reshape(row_count, head_count, DH)
    delta = jnp.sum(d_mixed * mixed, -1).T

    def back_block(part_keys, part_values, part_ids, col_start):
        col_count = part_keys.shape[0]
        key_heads = part_keys.reshape(col_count, head_count, DH)
        value_heads = part_values.reshape(col_count, head_count, DH)
        scores = jnp.einsum("rhd,nhd->hrn", queries, key_heads, precision=FULL_PRECISION)
        logits = scores + lax.dynamic_slice_in_dim(bias_pair, col_start, col_count, 2)
        same_mol = own_ids[:, None] == part_ids[None, :]
        probs = jnp.where(same_mol[None], jnp.exp(logits - log_total[:, :, None]), 0.0)
        d_probs = jnp.einsum("rhd,nhd->hrn", d_mixed, value_heads, precision=FULL_PRECISION)
        d_logits = probs * (d_probs - delta[:, :, None])
        d_cols = d_logits + lax.dynamic_slice_in_dim(grad_cols, col_start, col_count, 2)
        d_query_add = jnp.einsum("hrn,nhd->rhd", d_cols, key_heads, precision=FULL_PRECISION)
        d_key_part = jnp.einsum("hrn,rhd->nhd", d_cols, queries, precision=FULL_PRECISION)
        d_value_part = jnp.einsum("hrn,rhd->nhd", probs, d_mixed, precision=FULL_PRECISION)
        return (
            d_query_add,
            d_key_part.reshape(col_count, feat_width),
            d_value_part.reshape(col_count, feat_width),
            d_cols,
        )

    block_total = lax.axis_size("blk")
    d_query_zero = jnp.zeros((row_count, head_count, DH), jnp.float32)
    position = lax.axis_index("blk")

    def turn_step(turn_index, state):
        d_query_acc, grad_pair_acc, current, partials = state
        source = (position - turn_index) % block_total
        col_start = source * row_count
        d_query_add, d_key_part, d_value_part, d_cols = back_block(
            current[0], current[1], current[2], col_start
        )
        grad_pair_acc = lax.dynamic_update_slice_in_dim(grad_pair_acc, d_cols, col_start, 2)
        moved = from_behind((current[0], current[1], current[2]), "blk", 1)
        carried = from_behind((partials[0] + d_key_part, partials[1] + d_value_part), "blk", 1)
        return (d_query_acc + d_query_add, grad_pair_acc, moved, carried)

    start_turn = (
        d_query_zero,
        jnp.zeros_like(bias_pair),
        (key_rows, value_rows, own_ids),
        (jnp.zeros_like(key_rows), jnp.zeros_like(value_rows)),
    )
    d_query_acc, grad_pair_local, kept_blocks, partials = lax.fori_loop(
        0, block_total, turn_step, start_turn
    )
    d_keys, d_values = partials
    d_queries = d_query_acc.reshape(row_count, feat_width) * scaling
    g_w_query = matmul_full(normed.T, d_queries)
    g_b_query = jnp.sum(d_queries, 0)
    g_w_key = matmul_full(normed.T, d_keys)
    g_w_value = matmul_full(normed.T, d_values)
    g_b_value = jnp.sum(d_values, 0)
    d_normed_part = (
        matmul_full(d_queries, w_query.T)
        + matmul_full(d_keys, w_key.T)
        + matmul_full(d_values, w_value.T)
    )
    d_normed = lax.psum(d_normed_part, "head")
    first_unused, norm_one_pull = jax.vjp(layer_norm, inputs, ln1_gain, ln1_bias)
    d_inputs_norm, g_ln1_gain, g_ln1_bias = norm_one_pull(d_normed)
    grad_inputs = d_hidden + d_inputs_norm
    (
        g_ln1_gain,
        g_ln1_bias,
        g_w_query,
        g_b_query,
        g_w_key,
        g_w_value,
        g_b_value,
        g_w_out,
        g_b_out,
        g_ln2_gain,
        g_ln2_bias,
        g_w_up,
        g_b_up,
        g_w_down,
        g_b_down,
    ) = lax.psum(
        (
            g_ln1_gain,
            g_ln1_bias,
            g_w_query,
            g_b_query,
            g_w_key,
            g_w_value,
            g_b_value,
            g_w_out,
            g_b_out,
            g_ln2_gain,
            g_ln2_bias,
            g_w_up,
            g_b_up,
            g_w_down,
            g_b_down,
        ),
        ("blk", "dp"),
    )
    return (
        result_atoms[None],
        out_pair[None],
        penalty,
        grad_inputs[None],
        grad_pair_local[None],
        g_ln1_gain,
        g_ln1_bias,
        g_w_query,
        g_b_query,
        g_w_key,
        g_w_value,
        g_b_value,
        g_w_out,
        g_b_out,
        g_ln2_gain,
        g_ln2_bias,
        g_w_up,
        g_b_up,
        g_w_down,
        g_b_down,
    )


def solution(mesh):
    return jax.shard_map(
        local,
        mesh=mesh,
        in_specs=(
            P("dp", "blk", None),
            P("dp", "head", "blk", None),
            P("dp", "blk"),
            P(),
            P(),
            P(None, "head"),
            P("head"),
            P(None, "head"),
            P(None, "head"),
            P("head"),
            P("head", None),
            P(),
            P(),
            P(),
            P(None, "head"),
            P("head"),
            P("head", None),
            P(),
            P("dp", "blk", None),
            P("dp", "head", "blk", None),
        ),
        out_specs=(
            P("dp", "blk", None),
            P("dp", "head", "blk", None),
            P(),
            P("dp", "blk", None),
            P("dp", "head", "blk", None),
            P(),
            P(),
            P(None, "head"),
            P("head"),
            P(None, "head"),
            P(None, "head"),
            P("head"),
            P("head", None),
            P(),
            P(),
            P(),
            P(None, "head"),
            P("head"),
            P("head", None),
            P(),
        ),
        check_vma=False,
    )
```

profile of v0, /device:TPU:0, one launch (start us, length us, event | category | flops | bytes accessed | tf_op | source)
XLA Modules:
  0.0 513.7 jit_solution(2404550093489830399)
XLA Ops:
  10.3 6.3 %all-gather = s32[1,1024]{1,0:T(1,128)S(1)} all-gather(s32[1,256]{1,0:T(1,128)} %param.24), channel_id=2, replica_groups=mesh['blk'=4,'head'=4,'dp'=2] {'blk'}, dimensions={1}, use_global_device_ids=true | all-gather | bytes 5120 | tf_op jit(solution)/shard_map/all_gather | solution.py:79
  19.1 7.6 %all_gather.10 = f32[1024,128]{1,0:T(8,128)S(1)} all-gather(f32[256,128]{1,0:T(8,128)S(1)} %fusion.76), channel_id=1, replica_groups=mesh['blk'=4,'head'=4,'dp'=2] {'blk'}, dimensions={0}, use_global_device_ids=true | all-gather | bytes 655360 | tf_op jit(solution)/shard_map/all_gather | solution.py:77
  30.1 7.3 %all_gather.11 = f32[1024,128]{1,0:T(8,128)S(1)} all-gather(f32[256,128]{1,0:T(8,128)S(1)} %convolution_add_fusion.3), channel_id=1, replica_groups=mesh['blk'=4,'head'=4,'dp'=2] {'blk'}, dimensions={0}, use_global_device_ids=true | all-gather | bytes 655360 | tf_op jit(solution)/shard_map/all_gather | solution.py:78
  38.4 2.5 fusion.13
  42.6 31.5 %select_reduce_fusion = (f32[16,256]{1,0:T(8,128)}, f32[16,256,1024]{2,1,0:T(8,128)S(1)}, f32[256,1024]{1,0:T(8,128)}) fusion(pred[256,1024]{1,0:T(8,128)(4,1)} %broadcast_compare_fusion.1, f32[1,16,256,1024]{3,2,1,0:T(8,128)} %param.23, f32[256,16,8]{0,2,1:T(8,128)} %fusion.13, f32[1024,128]{0,1:T(8,128)} %copy.44), kind=kOutput, calls=%fused_computation.15 | convolution fusion | flops 423358464 | bytes 35536896 | tf_op jit(solution)/shard_map/rhd,nhd->hrn/dot_general | solution.py:83
  74.9 6.5 %fusion.6 = f32[16,256]{1,0:T(8,128)S(1)} fusion(f32[16,256,1024]{2,1,0:T(8,128)S(1)} %get-tuple-element.554, f32[16,256]{1,0:T(8,128)S(1)} %broadcast_maximum_fusion, pred[256,1024]{1,0:T(8,128)(4,1)} %broadcast_compare_fusion.1), kind=kLoop, calls=%fused_computation.16 | loop fusion | flops 16773120 | bytes 17072128 | tf_op jit(solution)/shard_map/reduce_sum | solution.py:90
  82.1 15.9 %fusion.16 = f32[256,16,8]{0,2,1:T(8,128)S(1)} fusion(f32[16,256,1024]{2,1,0:T(8,128)S(1)} %get-tuple-element.554, f32[16,256]{1,0:T(8,128)S(1)} %broadcast_maximum_fusion, pred[256,1024]{1,0:T(8,128)(4,1)S(1)} %copy-done.10, f32[1024,128]{0,1:T(8,128)S(1)} %copy-done.19, f32[256,16]{0,1:T(8,128)S(1)} %bitcast.172, f32[256,16]{0,1:T(8,128)S(1)} %get-tuple-element.559), kind=kOutput, calls=%fused_computation.32 | convolution fusion | flops 415301632 | bytes 17743872 | tf_op jit(solution)/shard_map/hrn,nhd->rhd/dot_general | solution.py:91
  100.2 39.7 %all-reduce.8.cloned.1.call-done = f32[256,512]{1,0:T(8,128)} async-done(((f32[256,512]{1,0:T(8,128)}), f32[256,512]{1,0:T(8,128)}) %all-reduce.8.cloned.1.call-update) | async-done | bytes 524304 | tf_op jit(solution)/shard_map/psum | solution.py:109
  142.0 2.9 fusion.17
  145.7 3.2 fusion.82
  151.9 3.3 fusion.54
  155.2 34.8 %all-reduce.10.cloned.1.call-done = f32[256,512]{1,0:T(8,128)} async-done(((f32[256,512]{1,0:T(8,128)}), f32[256,512]{1,0:T(8,128)}) %all-reduce.10.cloned.1.call-update) | async-done | bytes 524304 | tf_op jit(solution)/shard_map/psum | solution.py:128
  196.3 8.3 %broadcast_in_dim.119 = f32[16,256,1024]{2,1,0:T(8,128)} broadcast(f32[]{:T(128)} %constant.132.clone.1), dimensions={} | broadcast | bytes 16777220 | tf_op jit(solution)/shard_map/jit(_where)/broadcast_in_dim | solution.py:89
  204.6 119.6 %while.28 = (s32[]{:T(128)}, f32[256,16,8]{0,2,1:T(8,128)S(1)}, f32[16,256,1024]{2,1,0:T(8,128)}, f32[256,128]{0,1:T(8,128)S(1)}, f32[256,128]{0,1:T(8,128)S(1)}...) while((s32[]{:T(128)}, f32[256,16,8]{0,2,1:T(8,128)S(1)}, ...), condition=%wide.region_19.20_spmd.clone, body=%wide.region_18.19_spmd.clone.sunk | while | flops 509804544 | bytes 59023968 | solution.py:180
  207.4 6.2 %exponential_select_fusion.10 = f32[16,256,256]{2,1,0:T(8,128)S(1)} fusion(f32[16,256,1024]{2,1,0:T(8,128)} %get-tuple-element.724, s32[]{:T(128)S(6)} %select_n.82, f32[256,16,8]{0,2,1:T(8,128)S(1)} %get-tuple-element.722, f32[16,256]{1,0:T(8,128)S(1)} %get-tuple-element.725, pred[256,256]{1,0:T(8,128)(4,1)S(1)} %broadcast_compare_fusion.3, ...), kind=kOutput, calls=%fused_computation.1.clone.1 | convolution fusion | flops 103809024 | bytes 8732676 | tf_op jit(solution)/shard_map/while/body/eval_jaxpr/rhd,nhd->hrn/dot_general | solution.py:141
  213.6 2.3 fusion.135
  216.5 7.5 %constant_dynamic-update-slice_fusion.2 = (f32[16,256,1024]{2,1,0:T(8,128)}, f32[16,256,256]{2,1,0:T(8,128)S(1)}) fusion(f32[16,256,1024]{2,1,0:T(8,128)} %get-tuple-element.693, s32[]{:T(128)S(6)} %select_n.82, f32[16,256,1024]{2,1,0:T(8,128)} %get-tuple-element.728, f32[16,256,256]{2,1,0:T(8,128)S(1)} %exponential_select_fusion.10, ...), kind=kOutput, calls=%fused_computation.12.clone.1 | convolution fusion | flops 103809024 | bytes 17055748 | tf_op jit(solution)/shard_map/while/body/eval_jaxpr/rhd,nhd->hrn/dot_general | solution.py:145
  225.9 2.3 fusion.134
  228.3 5.8 %fusion.133 = f32[256,16,8]{0,2,1:T(8,128)S(1)} fusion(f32[16,256,256]{2,1,0:T(8,128)} %copy-done.2, f32[256,128]{0,1:T(8,128)S(1)} %copy.62, f32[256,16,8]{0,2,1:T(8,128)S(1)} %get-tuple-element.692, pred[]{:T(512)S(6)} %compare.4), kind=kOutput, calls=%fused_computation.5.clone.1 | convolution fusion | flops 100728832 | bytes 4587521 | tf_op jit(solution)/shard_map/while/body/eval_jaxpr/hrn,nhd->rhd/dot_general | solution.py:148
  237.3 6.2 %exponential_select_fusion.10 = f32[16,256,256]{2,1,0:T(8,128)S(1)} fusion(f32[16,256,1024]{2,1,0:T(8,128)} %get-tuple-element.724, s32[]{:T(128)S(6)} %select_n.82, f32[256,16,8]{0,2,1:T(8,128)S(1)} %get-tuple-element.722, f32[16,256]{1,0:T(8,128)S(1)} %get-tuple-element.725, pred[256,256]{1,0:T(8,128)(4,1)S(1)} %broadcast_compare_fusion.3, ...), kind=kOutput, calls=%fused_computation.1.clone.1 | convolution fusion | flops 103809024 | bytes 8732676 | tf_op jit(solution)/shard_map/while/body/eval_jaxpr/rhd,nhd->hrn/dot_general | solution.py:141
  243.5 2.3 fusion.135
  245.8 7.5 %constant_dynamic-update-slice_fusion.2 = (f32[16,256,1024]{2,1,0:T(8,128)}, f32[16,256,256]{2,1,0:T(8,128)S(1)}) fusion(f32[16,256,1024]{2,1,0:T(8,128)} %get-tuple-element.693, s32[]{:T(128)S(6)} %select_n.82, f32[16,256,1024]{2,1,0:T(8,128)} %get-tuple-element.728, f32[16,256,256]{2,1,0:T(8,128)S(1)} %exponential_select_fusion.10, ...), kind=kOutput, calls=%fused_computation.12.clone.1 | convolution fusion | flops 103809024 | bytes 17055748 | tf_op jit(solution)/shard_map/while/body/eval_jaxpr/rhd,nhd->hrn/dot_general | solution.py:145
  255.2 2.3 fusion.134
  259.0 5.8 %fusion.133 = f32[256,16,8]{0,2,1:T(8,128)S(1)} fusion(f32[16,256,256]{2,1,0:T(8,128)} %copy-done.2, f32[256,128]{0,1:T(8,128)S(1)} %copy.62, f32[256,16,8]{0,2,1:T(8,128)S(1)} %get-tuple-element.692, pred[]{:T(512)S(6)} %compare.4), kind=kOutput, calls=%fused_computation.5.clone.1 | convolution fusion | flops 100728832 | bytes 4587521 | tf_op jit(solution)/shard_map/while/body/eval_jaxpr/hrn,nhd->rhd/dot_general | solution.py:148
  266.6 6.2 %exponential_select_fusion.10 = f32[16,256,256]{2,1,0:T(8,128)S(1)} fusion(f32[16,256,1024]{2,1,0:T(8,128)} %get-tuple-element.724, s32[]{:T(128)S(6)} %select_n.82, f32[256,16,8]{0,2,1:T(8,128)S(1)} %get-tuple-element.722, f32[16,256]{1,0:T(8,128)S(1)} %get-tuple-element.725, pred[256,256]{1,0:T(8,128)(4,1)S(1)} %broadcast_compare_fusion.3, ...), kind=kOutput, calls=%fused_computation.1.clone.1 | convolution fusion | flops 103809024 | bytes 8732676 | tf_op jit(solution)/shard_map/while/body/eval_jaxpr/rhd,nhd->hrn/dot_general | solution.py:141
  272.8 2.3 fusion.135
  276.6 7.5 %constant_dynamic-update-slice_fusion.2 = (f32[16,256,1024]{2,1,0:T(8,128)}, f32[16,256,256]{2,1,0:T(8,128)S(1)}) fusion(f32[16,256,1024]{2,1,0:T(8,128)} %get-tuple-element.693, s32[]{:T(128)S(6)} %select_n.82, f32[16,256,1024]{2,1,0:T(8,128)} %get-tuple-element.728, f32[16,256,256]{2,1,0:T(8,128)S(1)} %exponential_select_fusion.10, ...), kind=kOutput, calls=%fused_computation.12.clone.1 | convolution fusion | flops 103809024 | bytes 17055748 | tf_op jit(solution)/shard_map/while/body/eval_jaxpr/rhd,nhd->hrn/dot_general | solution.py:145
  286.0 2.3 fusion.134
  288.3 5.8 %fusion.133 = f32[256,16,8]{0,2,1:T(8,128)S(1)} fusion(f32[16,256,256]{2,1,0:T(8,128)} %copy-done.2, f32[256,128]{0,1:T(8,128)S(1)} %copy.62, f32[256,16,8]{0,2,1:T(8,128)S(1)} %get-tuple-element.692, pred[]{:T(512)S(6)} %compare.4), kind=kOutput, calls=%fused_computation.5.clone.1 | convolution fusion | flops 100728832 | bytes 4587521 | tf_op jit(solution)/shard_map/while/body/eval_jaxpr/hrn,nhd->rhd/dot_general | solution.py:148
  297.4 6.2 %exponential_select_fusion.10 = f32[16,256,256]{2,1,0:T(8,128)S(1)} fusion(f32[16,256,1024]{2,1,0:T(8,128)} %get-tuple-element.724, s32[]{:T(128)S(6)} %select_n.82, f32[256,16,8]{0,2,1:T(8,128)S(1)} %get-tuple-element.722, f32[16,256]{1,0:T(8,128)S(1)} %get-tuple-element.725, pred[256,256]{1,0:T(8,128)(4,1)S(1)} %broadcast_compare_fusion.3, ...), kind=kOutput, calls=%fused_computation.1.clone.1 | convolution fusion | flops 103809024 | bytes 8732676 | tf_op jit(solution)/shard_map/while/body/eval_jaxpr/rhd,nhd->hrn/dot_general | solution.py:141
  303.5 2.3 fusion.135
  305.9 7.5 %constant_dynamic-update-slice_fusion.2 = (f32[16,256,1024]{2,1,0:T(8,128)}, f32[16,256,256]{2,1,0:T(8,128)S(1)}) fusion(f32[16,256,1024]{2,1,0:T(8,128)} %get-tuple-element.693, s32[]{:T(128)S(6)} %select_n.82, f32[16,256,1024]{2,1,0:T(8,128)} %get-tuple-element.728, f32[16,256,256]{2,1,0:T(8,128)S(1)} %exponential_select_fusion.10, ...), kind=kOutput, calls=%fused_computation.12.clone.1 | convolution fusion | flops 103809024 | bytes 17055748 | tf_op jit(solution)/shard_map/while/body/eval_jaxpr/rhd,nhd->hrn/dot_general | solution.py:145
  315.3 2.3 fusion.134
  318.2 5.8 %fusion.133 = f32[256,16,8]{0,2,1:T(8,128)S(1)} fusion(f32[16,256,256]{2,1,0:T(8,128)} %copy-done.2, f32[256,128]{0,1:T(8,128)S(1)} %copy.62, f32[256,16,8]{0,2,1:T(8,128)S(1)} %get-tuple-element.692, pred[]{:T(512)S(6)} %compare.4), kind=kOutput, calls=%fused_computation.5.clone.1 | convolution fusion | flops 100728832 | bytes 4587521 | tf_op jit(solution)/shard_map/while/body/eval_jaxpr/hrn,nhd->rhd/dot_general | solution.py:148
  327.6 2.4 convolution_add_fusion.1
  330.1 3.2 fusion.39
  333.3 3.4 fusion.20
  336.8 2.0 fusion.58
  338.8 2.5 fusion.75
  341.3 2.5 fusion.18
  343.8 2.5 fusion.74
  347.7 70.1 %all-reduce.14.cloned.1.call-done = (f32[256,512]{1,0:T(8,128)}, f32[256,1024]{1,0:T(8,128)}, f32[256,512]{1,0:T(8,128)}) async-done(((f32[256,512]{1,0:T(8,128)}, f32[256,1024]{1,0:T(8,128)}, f32[256,512]{1,0:T(8,128)}), (f32[256,512]{1,0:T(8,128)}, f32[256,1024]{1,0:T(8,128)}, f32[256,512]{1,0:T(8,128)})) %all-reduce.14.cloned.1.call-update) | async-done | bytes 2097168 | tf_op jit(solution)/shard_map/psum | solution.py:119
  419.1 2.7 convert_reduce_fusion
  421.8 25.7 %all-reduce = (f32[]{:T(128)}, f32[]{:T(128)}, f32[512]{0:T(512)}, f32[512]{0:T(512)}, f32[128]{0:T(128)}, /*index=5*/f32[128]{0:T(128)}, f32[512]{0:T(512)}, f3...) all-reduce(f32[]{:T(128)} %get-tuple-element.492, ...), channel_id=1, replica_groups=mesh['blk'=4,'head'=4,'dp'=2] {'blk','dp'}, use_global_device_ids=true, to_apply=%region_11.12 | all-reduce | flops 3842 | bytes 30736 | tf_op jit(solution)/shard_map/psum | solution.py:113
  450.2 2.2 add_bitcast_fusion
  452.4 42.0 %all-reduce.12.cloned.1.call-done = (f32[512,128]{1,0:T(8,128)}, f32[512,128]{1,0:T(8,128)}, f32[512,128]{1,0:T(8,128)}, f32[128,512]{1,0:T(8,128)}, f32[512,512]{1,0:T(8,128)}, /*index=5*/f32[512,512]{1,0:T(8,128)}) async-done(((f32[512,128]{1,0:T(8,128)}, f32[512,128]{1,0:T(8,128)}, f32[512,128]{1,0:T(8,128)}, f32[128,512]{1,0:T(8,128)}, f32[512,512]{1,0:T(8,128)}, /*index=5*/f32[512,512]{1,0:T(8,128)}), ...) | async-done | bytes 3145744 | tf_op jit(solution)/shard_map/psum | solution.py:215
  501.1 2.3 copy.91
  503.3 2.3 copy.92
  (199 shorter events, 64.3 us)
Async XLA Ops:
  7.2 134.8 %copy-start = (f32[512,512]{1,0:T(8,128)S(1)}, f32[512,512]{1,0:T(8,128)}, u32[]{:S(2)}) copy-start(f32[512,512]{1,0:T(8,128)} %param.36) | copy-start | bytes 3145732
  7.2 132.7 %all-reduce.8.cloned.1.call-start = ((), (), s32[]{:S(2)}) async-start(), calls=%async_computation | async-start | bytes 1048576 | tf_op jit(solution)/shard_map/psum | solution.py:109
  81.4 58.5 %copy-start.40 = (f32[512]{0:T(512)S(1)}, f32[512]{0:T(512)}, u32[]{:S(2)}) copy-start(f32[512]{0:T(512)} %param.33) | copy-start | bytes 6148
  81.4 60.6 %copy-start.29 = (f32[512]{0:T(512)S(1)}, f32[512]{0:T(512)}, u32[]{:S(2)}) copy-start(f32[512]{0:T(512)} %param.34) | copy-start | bytes 6148
  81.4 60.6 %copy-start.41 = (f32[512]{0:T(512)S(1)}, f32[512]{0:T(512)}, u32[]{:S(2)}) copy-start(f32[512]{0:T(512)} %param.35) | copy-start | bytes 6148
  100.1 51.5 %copy-start.26 = (s32[1,256]{1,0:T(1,128)S(1)}, s32[1,256]{1,0:T(1,128)}, u32[]{:S(2)}) copy-start(s32[1,256]{1,0:T(1,128)} %param.24) | copy-start | bytes 3076
  100.1 51.6 %copy-start.14 = (f32[256,128]{1,0:T(8,128)S(1)}, f32[256,128]{1,0:T(8,128)}, u32[]{:S(2)}) copy-start(f32[256,128]{1,0:T(8,128)} %copy-done.13) | copy-start | bytes 393220
  100.1 51.7 %copy-start.12 = (f32[256,128]{1,0:T(8,128)S(1)}, f32[256,128]{1,0:T(8,128)}, u32[]{:S(2)}) copy-start(f32[256,128]{1,0:T(8,128)} %copy-done.11) | copy-start | bytes 393220
  100.1 93.8 %copy-start.6 = (f32[1,256,512]{2,1,0:T(8,128)S(1)}, f32[1,256,512]{2,1,0:T(8,128)}, u32[]{:S(2)}) copy-start(f32[1,256,512]{2,1,0:T(8,128)} %param.40) | copy-start | bytes 1572868
  100.1 94.6 %copy-start.16 = (f32[256,16,8]{0,2,1:T(8,128)S(1)}, f32[256,16,8]{0,2,1:T(8,128)}, u32[]{:S(2)}) copy-start(f32[256,16,8]{0,2,1:T(8,128)} %copy-done.15) | copy-start | bytes 393220
  100.1 89.9 %all-reduce.10.cloned.1.call-start = ((), (), s32[]{:S(2)}) async-start(), calls=%async_computation.1 | async-start | bytes 1048576 | tf_op jit(solution)/shard_map/psum | solution.py:128
  144.9 59.7 %copy-start.5 = (f32[256,16,8]{0,2,1:T(8,128)S(1)}, f32[256,16,8]{0,2,1:T(8,128)}, u32[]{:S(2)}) copy-start(f32[256,16,8]{0,2,1:T(8,128)} %fusion.13) | copy-start | bytes 393220
  144.9 59.7 %copy-start.18 = (f32[16,256]{1,0:T(8,128)S(1)}, f32[16,256]{1,0:T(8,128)}, u32[]{:S(2)}) copy-start(f32[16,256]{1,0:T(8,128)} %get-tuple-element.681) | copy-start | bytes 49156
  151.6 266.3 %all-reduce.14.cloned.1.call-start = ((), (), s32[]{:S(2)}) async-start(), calls=%async_computation.3 | async-start | bytes 4194304 | tf_op jit(solution)/shard_map/psum | solution.py:119
  204.6 134.2 %copy-start.4 = (f32[1,256,512]{2,1,0:T(8,128)S(1)}, f32[1,256,512]{2,1,0:T(8,128)}, u32[]{:S(2)}) copy-start(f32[1,256,512]{2,1,0:T(8,128)} %param.22) | copy-start | bytes 1572868
  204.8 29.2 %collective-permute-start.2 = (s32[256]{0:T(256)S(1)}, s32[256]{0:T(256)S(1)}, u32[]{:S(2)}, u32[]{:S(2)}) collective-permute-start(s32[256]{0:T(256)S(1)} %copy.64), channel_id=1, source_target_pairs={{0,8},{8,16},{16,24},{24,0},{1,9},{9,17},{17,25},{25,1},{2,10},{10... | collective-permute-start | bytes 3080 | tf_op jit(solution)/shard_map/while/body/eval_jaxpr/ppermute | solution.py:20
  204.9 29.1 %collective-permute-start.1 = (f32[256,128]{0,1:T(8,128)S(1)}, f32[256,128]{0,1:T(8,128)S(1)}, u32[]{:S(2)}, u32[]{:S(2)}) collective-permute-start(f32[256,128]{0,1:T(8,128)S(1)} %copy.63), channel_id=1, source_target_pairs={{0,8},{8,16},{16,24},{24,0},{1,9},{9,17},{17,25},{25,1},{2,10},{10... | collective-permute-start | bytes 393224 | tf_op jit(solution)/shard_map/while/body/eval_jaxpr/ppermute | solution.py:20
  206.6 27.5 %collective-permute-start = (f32[256,128]{0,1:T(8,128)S(1)}, f32[256,128]{0,1:T(8,128)S(1)}, u32[]{:S(2)}, u32[]{:S(2)}) collective-permute-start(f32[256,128]{0,1:T(8,128)S(1)} %copy.62), channel_id=1, source_target_pairs={{0,8},{8,16},{16,24},{24,0},{1,9},{9,17},{17,25},{25,1},{2,10},{10... | collective-permute-start | bytes 393224 | tf_op jit(solution)/shard_map/while/body/eval_jaxpr/ppermute | solution.py:20
  215.9 18.2 %collective-permute-start.4 = (f32[256,128]{0,1:T(8,128)S(1)}, f32[256,128]{0,1:T(8,128)S(1)}, u32[]{:S(2)}, u32[]{:S(2)}) collective-permute-start(f32[256,128]{0,1:T(8,128)S(1)} %fusion.135), channel_id=1, source_target_pairs={{0,8},{8,16},{16,24},{24,0},{1,9},{9,17},{17,25},{25,1},{2,10},{10... | collective-permute-start | bytes 393224 | tf_op jit(solution)/shard_map/while/body/eval_jaxpr/ppermute | solution.py:20
  228.2 5.9 %collective-permute-start.3 = (f32[256,128]{0,1:T(8,128)S(1)}, f32[256,128]{0,1:T(8,128)S(1)}, u32[]{:S(2)}, u32[]{:S(2)}) collective-permute-start(f32[256,128]{0,1:T(8,128)S(1)} %fusion.134), channel_id=1, source_target_pairs={{0,8},{8,16},{16,24},{24,0},{1,9},{9,17},{17,25},{25,1},{2,10},{10... | collective-permute-start | bytes 393224 | tf_op jit(solution)/shard_map/while/body/eval_jaxpr/ppermute | solution.py:20
  234.1 30.7 %collective-permute-start.2 = (s32[256]{0:T(256)S(1)}, s32[256]{0:T(256)S(1)}, u32[]{:S(2)}, u32[]{:S(2)}) collective-permute-start(s32[256]{0:T(256)S(1)} %copy.64), channel_id=1, source_target_pairs={{0,8},{8,16},{16,24},{24,0},{1,9},{9,17},{17,25},{25,1},{2,10},{10... | collective-permute-start | bytes 3080 | tf_op jit(solution)/shard_map/while/body/eval_jaxpr/ppermute | solution.py:20
  235.7 29.1 %collective-permute-start.1 = (f32[256,128]{0,1:T(8,128)S(1)}, f32[256,128]{0,1:T(8,128)S(1)}, u32[]{:S(2)}, u32[]{:S(2)}) collective-permute-start(f32[256,128]{0,1:T(8,128)S(1)} %copy.63), channel_id=1, source_target_pairs={{0,8},{8,16},{16,24},{24,0},{1,9},{9,17},{17,25},{25,1},{2,10},{10... | collective-permute-start | bytes 393224 | tf_op jit(solution)/shard_map/while/body/eval_jaxpr/ppermute | solution.py:20
  235.8 29.0 %collective-permute-start = (f32[256,128]{0,1:T(8,128)S(1)}, f32[256,128]{0,1:T(8,128)S(1)}, u32[]{:S(2)}, u32[]{:S(2)}) collective-permute-start(f32[256,128]{0,1:T(8,128)S(1)} %copy.62), channel_id=1, source_target_pairs={{0,8},{8,16},{16,24},{24,0},{1,9},{9,17},{17,25},{25,1},{2,10},{10... | collective-permute-start | bytes 393224 | tf_op jit(solution)/shard_map/while/body/eval_jaxpr/ppermute | solution.py:20
  245.8 19.1 %collective-permute-start.4 = (f32[256,128]{0,1:T(8,128)S(1)}, f32[256,128]{0,1:T(8,128)S(1)}, u32[]{:S(2)}, u32[]{:S(2)}) collective-permute-start(f32[256,128]{0,1:T(8,128)S(1)} %fusion.135), channel_id=1, source_target_pairs={{0,8},{8,16},{16,24},{24,0},{1,9},{9,17},{17,25},{25,1},{2,10},{10... | collective-permute-start | bytes 393224 | tf_op jit(solution)/shard_map/while/body/eval_jaxpr/ppermute | solution.py:20
  257.5 7.4 %collective-permute-start.3 = (f32[256,128]{0,1:T(8,128)S(1)}, f32[256,128]{0,1:T(8,128)S(1)}, u32[]{:S(2)}, u32[]{:S(2)}) collective-permute-start(f32[256,128]{0,1:T(8,128)S(1)} %fusion.134), channel_id=1, source_target_pairs={{0,8},{8,16},{16,24},{24,0},{1,9},{9,17},{17,25},{25,1},{2,10},{10... | collective-permute-start | bytes 393224 | tf_op jit(solution)/shard_map/while/body/eval_jaxpr/ppermute | solution.py:20
  264.9 29.2 %collective-permute-start.2 = (s32[256]{0:T(256)S(1)}, s32[256]{0:T(256)S(1)}, u32[]{:S(2)}, u32[]{:S(2)}) collective-permute-start(s32[256]{0:T(256)S(1)} %copy.64), channel_id=1, source_target_pairs={{0,8},{8,16},{16,24},{24,0},{1,9},{9,17},{17,25},{25,1},{2,10},{10... | collective-permute-start | bytes 3080 | tf_op jit(solution)/shard_map/while/body/eval_jaxpr/ppermute | solution.py:20
  265.0 29.1 %collective-permute-start.1 = (f32[256,128]{0,1:T(8,128)S(1)}, f32[256,128]{0,1:T(8,128)S(1)}, u32[]{:S(2)}, u32[]{:S(2)}) collective-permute-start(f32[256,128]{0,1:T(8,128)S(1)} %copy.63), channel_id=1, source_target_pairs={{0,8},{8,16},{16,24},{24,0},{1,9},{9,17},{17,25},{25,1},{2,10},{10... | collective-permute-start | bytes 393224 | tf_op jit(solution)/shard_map/while/body/eval_jaxpr/ppermute | solution.py:20
  265.7 28.4 %collective-permute-start = (f32[256,128]{0,1:T(8,128)S(1)}, f32[256,128]{0,1:T(8,128)S(1)}, u32[]{:S(2)}, u32[]{:S(2)}) collective-permute-start(f32[256,128]{0,1:T(8,128)S(1)} %copy.62), channel_id=1, source_target_pairs={{0,8},{8,16},{16,24},{24,0},{1,9},{9,17},{17,25},{25,1},{2,10},{10... | collective-permute-start | bytes 393224 | tf_op jit(solution)/shard_map/while/body/eval_jaxpr/ppermute | solution.py:20
  275.0 19.1 %collective-permute-start.4 = (f32[256,128]{0,1:T(8,128)S(1)}, f32[256,128]{0,1:T(8,128)S(1)}, u32[]{:S(2)}, u32[]{:S(2)}) collective-permute-start(f32[256,128]{0,1:T(8,128)S(1)} %fusion.135), channel_id=1, source_target_pairs={{0,8},{8,16},{16,24},{24,0},{1,9},{9,17},{17,25},{25,1},{2,10},{10... | collective-permute-start | bytes 393224 | tf_op jit(solution)/shard_map/while/body/eval_jaxpr/ppermute | solution.py:20
  288.3 5.9 %collective-permute-start.3 = (f32[256,128]{0,1:T(8,128)S(1)}, f32[256,128]{0,1:T(8,128)S(1)}, u32[]{:S(2)}, u32[]{:S(2)}) collective-permute-start(f32[256,128]{0,1:T(8,128)S(1)} %fusion.134), channel_id=1, source_target_pairs={{0,8},{8,16},{16,24},{24,0},{1,9},{9,17},{17,25},{25,1},{2,10},{10... | collective-permute-start | bytes 393224 | tf_op jit(solution)/shard_map/while/body/eval_jaxpr/ppermute | solution.py:20
  294.2 29.8 %collective-permute-start.2 = (s32[256]{0:T(256)S(1)}, s32[256]{0:T(256)S(1)}, u32[]{:S(2)}, u32[]{:S(2)}) collective-permute-start(s32[256]{0:T(256)S(1)} %copy.64), channel_id=1, source_target_pairs={{0,8},{8,16},{16,24},{24,0},{1,9},{9,17},{17,25},{25,1},{2,10},{10... | collective-permute-start | bytes 3080 | tf_op jit(solution)/shard_map/while/body/eval_jaxpr/ppermute | solution.py:20
  294.9 29.1 %collective-permute-start.1 = (f32[256,128]{0,1:T(8,128)S(1)}, f32[256,128]{0,1:T(8,128)S(1)}, u32[]{:S(2)}, u32[]{:S(2)}) collective-permute-start(f32[256,128]{0,1:T(8,128)S(1)} %copy.63), channel_id=1, source_target_pairs={{0,8},{8,16},{16,24},{24,0},{1,9},{9,17},{17,25},{25,1},{2,10},{10... | collective-permute-start | bytes 393224 | tf_op jit(solution)/shard_map/while/body/eval_jaxpr/ppermute | solution.py:20
  295.0 29.0 %collective-permute-start = (f32[256,128]{0,1:T(8,128)S(1)}, f32[256,128]{0,1:T(8,128)S(1)}, u32[]{:S(2)}, u32[]{:S(2)}) collective-permute-start(f32[256,128]{0,1:T(8,128)S(1)} %copy.62), channel_id=1, source_target_pairs={{0,8},{8,16},{16,24},{24,0},{1,9},{9,17},{17,25},{25,1},{2,10},{10... | collective-permute-start | bytes 393224 | tf_op jit(solution)/shard_map/while/body/eval_jaxpr/ppermute | solution.py:20
  305.8 18.2 %collective-permute-start.4 = (f32[256,128]{0,1:T(8,128)S(1)}, f32[256,128]{0,1:T(8,128)S(1)}, u32[]{:S(2)}, u32[]{:S(2)}) collective-permute-start(f32[256,128]{0,1:T(8,128)S(1)} %fusion.135), channel_id=1, source_target_pairs={{0,8},{8,16},{16,24},{24,0},{1,9},{9,17},{17,25},{25,1},{2,10},{10... | collective-permute-start | bytes 393224 | tf_op jit(solution)/shard_map/while/body/eval_jaxpr/ppermute | solution.py:20
  317.5 6.5 %collective-permute-start.3 = (f32[256,128]{0,1:T(8,128)S(1)}, f32[256,128]{0,1:T(8,128)S(1)}, u32[]{:S(2)}, u32[]{:S(2)}) collective-permute-start(f32[256,128]{0,1:T(8,128)S(1)} %fusion.134), channel_id=1, source_target_pairs={{0,8},{8,16},{16,24},{24,0},{1,9},{9,17},{17,25},{25,1},{2,10},{10... | collective-permute-start | bytes 393224 | tf_op jit(solution)/shard_map/while/body/eval_jaxpr/ppermute | solution.py:20
  324.3 93.6 %copy-start.21 = (f32[512]{0:T(512)S(1)}, f32[512]{0:T(512)}, u32[]{:S(2)}) copy-start(f32[512]{0:T(512)} %param.25) | copy-start | bytes 6148
  324.3 93.5 %copy-start.23 = (f32[256]{0:T(256)S(1)}, f32[256]{0:T(256)}, u32[]{:S(2)}) copy-start(f32[256]{0:T(256)} %copy-done.22) | copy-start | bytes 3076
  324.3 93.5 %copy-start.25 = (f32[256]{0:T(256)S(1)}, f32[256]{0:T(256)}, u32[]{:S(2)}) copy-start(f32[256]{0:T(256)} %copy-done.24) | copy-start | bytes 3076
  324.3 94.8 %copy-start.27 = (s32[1,256]{1,0:T(1,128)S(1)}, s32[1,256]{1,0:T(1,128)}, u32[]{:S(2)}) copy-start(s32[1,256]{1,0:T(1,128)} %get-tuple-element.811) | copy-start | bytes 3076
  324.3 94.8 %copy-start.32 = (s32[1,1024]{1,0:T(1,128)S(1)}, s32[1,1024]{1,0:T(1,128)}, u32[]{:S(2)}) copy-start(s32[1,1024]{1,0:T(1,128)} %copy-done.31) | copy-start | bytes 12292
  324.3 97.5 %copy-start.36 = (f32[512]{0:T(512)S(1)}, f32[512]{0:T(512)}, u32[]{:S(2)}) copy-start(f32[512]{0:T(512)} %get-tuple-element.485) | copy-start | bytes 6148
  324.3 97.5 %copy-start.37 = (f32[512]{0:T(512)S(1)}, f32[512]{0:T(512)}, u32[]{:S(2)}) copy-start(f32[512]{0:T(512)} %get-tuple-element.489) | copy-start | bytes 6148
  324.4 97.5 %copy-start.38 = (f32[512]{0:T(512)S(1)}, f32[512]{0:T(512)}, u32[]{:S(2)}) copy-start(f32[512]{0:T(512)} %get-tuple-element.547) | copy-start | bytes 6148
  324.4 97.5 %copy-start.39 = (f32[512]{0:T(512)S(1)}, f32[512]{0:T(512)}, u32[]{:S(2)}) copy-start(f32[512]{0:T(512)} %get-tuple-element.564) | copy-start | bytes 6148
  324.4 124.5 %copy-start.34 = (f32[256]{0:T(256)S(1)}, f32[256]{0:T(256)}, u32[]{:S(2)}) copy-start(f32[256]{0:T(256)} %copy-done.33) | copy-start | bytes 3076
  324.4 125.9 %copy-start.42 = (f32[512]{0:T(512)S(1)}, f32[512]{0:T(512)}, u32[]{:S(2)}) copy-start(f32[512]{0:T(512)} %param.39) | copy-start | bytes 6148
  324.4 181.2 %copy-start.1 = (f32[512,512]{1,0:T(8,128)S(1)}, f32[512,512]{1,0:T(8,128)}, u32[]{:S(2)}) copy-start(f32[512,512]{1,0:T(8,128)} %param.36) | copy-start | bytes 3145732
  330.1 164.3 %all-reduce.12.cloned.1.call-start = ((), (), s32[]{:S(2)}) async-start(), calls=%async_computation.2 | async-start | bytes 6291456 | tf_op jit(solution)/shard_map/psum | solution.py:215
  (22 other events, 233.8 us)
Sparse Core Ops, SparseCore 0:
  100.2 39.6 all-reduce.7
  151.7 38.2 all-reduce.9
  330.2 87.5 all-reduce.13
  423.9 70.4 all-reduce.11
where the time goes:
time: 523 us; the launch traced here: 514 us
  waiting for transfers between devices  187 us (36%)
  matrix products  185 us (35%)
  blocking collectives  46.9 us (9%)
  local copies, waits for them, and re-layouts  34.4 us (7%)
  other arithmetic  30.1 us (6%)
  between operations  17.3 us (3%)
  starting transfers between devices  12.1 us (2%)
    psum x1, waiting for transfers between devices, local(): ffn_out = lax.psum(down_part, 'head')  70.1 us
    dot_general x18, matrix products, matmul_full(): return jnp.dot(left, right, precision=FULL_PRECISION)  42.1 us
    psum x1, waiting for transfers between devices, local(): lax.psum((g_ln1_gain, g_ln1_bias, g_w_query, g_b_query, g_w_key, g_w_valu...  42 us
    psum x1, waiting for transfers between devices, local(): attn_sum, square_sum = lax.psum((attn_part, squares), 'head')  39.7 us
    psum x1, waiting for transfers between devices, local(): d_normed_two = lax.psum(matmul_full(d_pre, w_up.T), 'head')  34.8 us
    dot_general x1, matrix products, local(): jnp.einsum('rhd,nhd->hrn', queries, key_heads, precision=FULL_PRECISION)  31.5 us
    dot_general x4, matrix products, back_block(): jnp.einsum('rhd,nhd->hrn', d_mixed, value_heads, precision=FULL_PRECISION)  29.9 us
    psum x1, blocking collectives, local(): numer_all, count_all = lax.psum((numer, jnp.sum(valid)), ('blk', 'dp'))  25.7 us
  transfers between devices with their start and end apart: 24, of which 4 were waited for; matrix products, arithmetic and copies ran while one was open for 25% of the time, Pallas kernels for 0%

commit v1 on v0

v1 whole, which is shorter than its diff:
```python
import functools
import math

import jax
import jax.numpy as jnp
from jax import lax
from jax.experimental import pallas as pl
from jax.experimental.pallas import tpu as pltpu
from jax.sharding import PartitionSpec as P

DH = 8
LANES = 128
STRIP = 16
CHUNK = 256
GROUP = 2
NORM_EPS = 1e-05
MASK_FILL = -1e30
F32 = jnp.float32
BF16 = jnp.bfloat16
MESH = pl.DeviceIdType.MESH
NN = (((1,), (0,)), ((), ()))
NT = (((1,), (1,)), ((), ()))
TN = (((0,), (0,)), ((), ()))
VMEM = pl.BlockSpec(memory_space=pltpu.VMEM)


def dot(left, right, dims=NN):
    return lax.dot_general(left, right, dims, preferred_element_type=F32)


def halves(value):
    high = value.astype(BF16)
    return high, (value - high.astype(F32)).astype(BF16)


def dot_halves(left, right, dims=NN):
    return dot(left[0], right[0], dims) + (
        dot(left[0], right[1], dims) + dot(left[1], right[0], dims)
    )


def dot_full(left, right, dims=NN):
    return dot_halves(halves(left), halves(right), dims)


def normalize(inputs):
    centred = inputs - jnp.mean(inputs, -1, keepdims=True)
    rate = lax.rsqrt(jnp.mean(centred * centred, -1, keepdims=True) + NORM_EPS)
    return centred * rate, rate


def normalize_back(grad, gain, normal, rate):
    scaled = grad * gain
    return rate * (
        scaled
        - jnp.mean(scaled, -1, keepdims=True)
        - normal * jnp.mean(scaled * normal, -1, keepdims=True)
    )


def column_sum(value):
    return jnp.sum(value, 0, keepdims=True)


def send(src, dst, send_sem, recv_sem, target):
    copy = pltpu.make_async_remote_copy(
        src_ref=src,
        dst_ref=dst,
        send_sem=send_sem,
        recv_sem=recv_sem,
        device_id=target,
        device_id_type=MESH,
    )
    copy.start()
    return copy


def arrived(ref, sem):
    pltpu.make_async_remote_copy(
        src_ref=ref, dst_ref=ref, send_sem=sem, recv_sem=sem, device_id={}, device_id_type=MESH
    ).wait_recv()


def meet(targets):
    barrier = pltpu.get_barrier_semaphore()
    for target in targets:
        pl.semaphore_signal(barrier, inc=1, device_id=target, device_id_type=MESH)
    pl.semaphore_wait(barrier, len(targets))


def others(index, count):
    return [lax.rem(index + step, count) for step in range(1, count)]


def project_kernel(
    atoms, ids, gain, bias, w_query, b_query, w_key, w_value, b_value,
    queries, kept, id_column, send_sem, recv_sem,
):
    blocks, feats = kept.shape[0], w_query.shape[1]
    rows = atoms.shape[0]
    chips = blocks // 2
    blk = lax.axis_index("blk")
    core, chip = lax.rem(blk, 2), lax.div(blk, 2)
    sibling = blk + 1 - 2 * core
    far = [step * 2 + core for step in others(chip, chips)]
    meet([{"blk": peer} for peer in [sibling] + far])
    normal, _ = normalize(atoms[...])
    normed = halves(normal * gain[...] + bias[...])
    kept[blk, 0:feats, :] = dot_halves(normed, halves(w_key[...])).T
    kept[blk, feats : 2 * feats, :] = (dot_halves(normed, halves(w_value[...])) + b_value[...]).T
    id_row = ids[...].astype(F32)
    kept[blk, 2 * feats : 2 * feats + 8, :] = jnp.broadcast_to(id_row, (8, rows))
    copies = [
        send(kept.at[blk], kept.at[blk], send_sem.at[place], recv_sem.at[blk], {"blk": peer})
        for place, peer in enumerate([sibling] + far)
    ]
    id_column[...] = jnp.broadcast_to(id_row, (LANES, rows)).T
    queries[...] = (
        (dot_halves(normed, halves(w_query[...])) + b_query[...]) * (DH ** (-0.5))
    ).T
    for place, source in enumerate(far):
        arrived(kept.at[source], recv_sem.at[source])
        copies.append(
            send(
                kept.at[source], kept.at[source], send_sem.at[chips + place], recv_sem.at[source],
                {"blk": sibling},
            )
        )
    for source in [sibling] + [peer + 1 - 2 * core for peer in far]:
        arrived(kept.at[source], recv_sem.at[source])
    for copy in copies:
        copy.wait_send()


def project(blocks, atoms, ids, gain, bias, w_query, b_query, w_key, w_value, b_value):
    rows, feats = atoms.shape[0], w_query.shape[1]
    return pl.pallas_call(
        project_kernel,
        out_shape=[
            jax.ShapeDtypeStruct((feats, rows), F32),
            jax.ShapeDtypeStruct((blocks, 2 * feats + 8, rows), F32),
            jax.ShapeDtypeStruct((rows, LANES), F32),
        ],
        in_specs=[VMEM] * 9,
        out_specs=[VMEM] * 3,
        scratch_shapes=[
            pltpu.SemaphoreType.DMA((blocks,)),
            pltpu.SemaphoreType.DMA((blocks,)),
        ],
        compiler_params=pltpu.CompilerParams(
            collective_id=0, has_side_effects=True, vmem_limit_bytes=32 << 20
        ),
        name="project",
    )(atoms, ids, gain, bias, w_query, b_query, w_key, w_value, b_value)


def whole_row(ref, low, count):
    return jnp.concatenate([ref[n, low : low + count, :] for n in range(ref.shape[0])], axis=1)


def stacked(parts):
    return jnp.concatenate(parts, axis=0).astype(BF16)


def wide_halves(value):
    high = value.astype(BF16).astype(F32)
    return high, value - high


def attend_kernel(
    pair, queries, keys, values, ids, id_column,
    mixed, log_sums, squares, id_row, score, high, low,
):
    group, rows, cols = score.shape
    strips = rows // STRIP
    chunk = min(CHUNK, cols)

    @pl.when(pl.program_id(0) == 0)
    def _():
        squares[...] = jnp.zeros_like(squares)
        one = whole_row(ids, 0, 8)
        id_row[...] = jnp.concatenate([one, one], axis=0)

    for g in range(group):
        head = slice(8 * g, 8 * g + 8)
        q_high, q_low = wide_halves(queries[head, :])
        k_high, k_low = wide_halves(whole_row(keys, 8 * g, 8))
        v_high, v_low = wide_halves(whole_row(values, 8 * g, 8))
        ones = jnp.ones_like(v_high)
        q_pack = stacked([q_high, q_high, q_low, q_low])
        k_pack = stacked([k_high, k_low, k_high, k_low])
        v_pack = stacked([v_high, v_low, ones, jnp.zeros_like(ones)])
        tops = [None] * strips
        for start in range(0, cols, chunk):
            part = slice(start, start + chunk)
            score[g, :, part] = dot(q_pack, k_pack[:, part], TN)
            for s in range(strips):
                line = pl.ds(s * STRIP, STRIP)
                own = id_column[line, :]
                for j in range(start, start + chunk, LANES):
                    tile = pl.ds(j, LANES)
                    value = score[g, line, tile]
                    squares[line, tile] += value * value
                    value = jnp.where(own == id_row[:, tile], pair[0, g, line, tile] + value, MASK_FILL)
                    score[g, line, tile] = value
                    tops[s] = value if tops[s] is None else jnp.maximum(tops[s], value)
        tops = [
            jnp.broadcast_to(jnp.max(top, axis=1, keepdims=True), (STRIP, LANES)) for top in tops
        ]
        totals = [None] * strips
        gathered = None
        for start in range(0, cols, chunk):
            part = slice(start, start + chunk)
            for s in range(strips):
                line = pl.ds(s * STRIP, STRIP)
                for j in range(start, start + chunk, LANES):
                    tile = pl.ds(j, LANES)
                    weight = jnp.exp(score[g, line, tile] - tops[s])
                    high[g, line, tile], low[g, line, tile] = halves(weight)
                    totals[s] = weight if totals[s] is None else totals[s] + weight
            term = dot(v_pack[:, part], high[g, :, part], NT) + dot(
                v_pack[:, part], low[g, :, part], NT
            )
            gathered = term if gathered is None else gathered + term
        for s in range(strips):
            total = jnp.sum(totals[s], axis=1, keepdims=True)
            log_sums[g, pl.ds(s * STRIP, STRIP), :] = tops[s] + jnp.log(total)
        mixed[head, :] = (gathered[0:8] + gathered[8:16]) / gathered[16:17]


def head_specs(kept_shape, feats, group):
    blocks, _, rows = kept_shape
    first = feats // (8 * group)
    return (
        pl.BlockSpec((blocks, 8 * group, rows), lambda h: (0, h, 0)),
        pl.BlockSpec((blocks, 8 * group, rows), lambda h: (0, first + h, 0)),
        pl.BlockSpec((blocks, 8, rows), lambda h: (0, 2 * feats // 8, 0)),
    )


def attend(pair, queries, kept, id_column):
    _, heads, rows, cols = pair.shape
    group = GROUP
    feats = heads * DH
    keys, values, ids = head_specs(kept.shape, feats, group)
    return pl.pallas_call(
        attend_kernel,
        grid=(heads // group,),
        in_specs=[
            pl.BlockSpec((1, group, rows, cols), lambda h: (0, h, 0, 0)),
            pl.BlockSpec((8 * group, rows), lambda h: (h, 0)),
            keys,
            values,
            ids,
            pl.BlockSpec((rows, LANES), lambda h: (0, 0)),
        ],
        out_specs=[
            pl.BlockSpec((8 * group, rows), lambda h: (h, 0)),
            pl.BlockSpec((group, rows, LANES), lambda h: (h, 0, 0)),
            pl.BlockSpec((rows, cols), lambda h: (0, 0)),
            pl.BlockSpec((STRIP, cols), lambda h: (0, 0)),
        ],
        out_shape=[
            jax.ShapeDtypeStruct((feats, rows), F32),
            jax.ShapeDtypeStruct((heads, rows, LANES), F32),
            jax.ShapeDtypeStruct((rows, cols), F32),
            jax.ShapeDtypeStruct((STRIP, cols), F32),
        ],
        scratch_shapes=[
            pltpu.VMEM((group, rows, cols), F32),
            pltpu.VMEM((group, rows, cols), BF16),
            pltpu.VMEM((group, rows, cols), BF16),
        ],
        compiler_params=pltpu.CompilerParams(vmem_limit_bytes=48 << 20),
        cost_estimate=pl.CostEstimate(
            flops=2 * 200 * heads * rows * cols,
            bytes_accessed=4 * heads * rows * cols,
            transcendentals=heads * rows * cols,
        ),
        name="attend",
    )(pair, queries, kept, kept, kept, id_column)


def attend_back_kernel(
    pair, cot, queries, keys, values, mixed, d_mixed, log_sums, id_column, id_row,
    out_pair, grad_pair, d_queries, d_keys, d_values, score, d_prob, p_high, p_low, g_high, g_low,
):
    group, rows, cols = score.shape
    blocks = d_keys.shape[0] * 2
    chunk = min(CHUNK, cols)
    place = lax.broadcasted_iota(jnp.int32, (8, rows), 0)

    def both(left, high, low, dims):
        value = dot(left, high, dims) + dot(left, low, dims)
        return value[0:8] + value[8:16]

    for g in range(group):
        head = slice(8 * g, 8 * g + 8)
        q_high, q_low = wide_halves(queries[head, :])
        k_high, k_low = wide_halves(whole_row(keys, 8 * g, 8))
        v_high, v_low = wide_halves(whole_row(values, 8 * g, 8))
        m_high, m_low = wide_halves(d_mixed[head, :])
        first = -column_sum(mixed[head, :] * d_mixed[head, :])
        delta_high, second = wide_halves(first)
        delta_mid, delta_low = wide_halves(second)
        deltas = jnp.where(
            place == 0, delta_high, jnp.where(place == 1, delta_mid, jnp.where(place == 2, delta_low, 0.0))
        )
        q_pack = stacked([q_high, q_high, q_low, q_low])
        k_pack = stacked([k_high, k_low, k_high, k_low])
        m_pack = stacked([m_high, m_high, m_low, deltas])
        v_pack = stacked([v_high, v_low, v_high, jnp.ones_like(v_high)])
        q_pair = stacked([q_high, q_low])
        k_pair = stacked([k_high, k_low])
        m_pair = stacked([m_high, m_low])
        d_query = None
        for start in range(0, cols, chunk):
            part = slice(start, start + chunk)
            score[g, :, part] = dot(q_pack, k_pack[:, part], TN)
            d_prob[g, :, part] = dot(m_pack, v_pack[:, part], TN)
            for s in range(rows // STRIP):
                line = pl.ds(s * STRIP, STRIP)
                own = id_column[line, :]
                log_sum = log_sums[g, line, :]
                for j in range(start, start + chunk, LANES):
                    tile = pl.ds(j, LANES)
                    value = pair[0, g, line, tile] + score[g, line, tile]
                    out_pair[0, g, line, tile] = value
                    prob = jnp.exp(jnp.where(own == id_row[:, tile], value - log_sum, MASK_FILL))
                    p_high[g, line, tile], p_low[g, line, tile] = halves(prob)
                    grad = prob * d_prob[g, line, tile] + cot[0, g, line, tile]
                    grad_pair[0, g, line, tile] = grad
                    g_high[g, line, tile], g_low[g, line, tile] = halves(grad)
            d_value = both(m_pair, p_high[g, :, part], p_low[g, :, part], NN)
            d_key = both(q_pair, g_high[g, :, part], g_low[g, :, part], NN)
            for n in range(start // rows, (start + chunk) // rows):
                span = slice(n * rows - start, (n + 1) * rows - start)
                d_keys[n // 2, n % 2, head, :] = d_key[:, span]
                d_values[n // 2, n % 2, head, :] = d_value[:, span]
            term = both(k_pair[:, part], g_high[g, :, part], g_low[g, :, part], NT)
            d_query = term if d_query is None else d_query + term
        d_queries[head, :] = d_query * (DH ** (-0.5))


def attend_back(pair, cot, queries, kept, mixed, d_mixed, log_sums, id_column, id_row):
    _, heads, rows, cols = pair.shape
    group = GROUP
    feats = heads * DH
    blocks = kept.shape[0]
    keys, values, _ = head_specs(kept.shape, feats, group)
    big = pl.BlockSpec((1, group, rows, cols), lambda h: (0, h, 0, 0))
    flat = pl.BlockSpec((8 * group, rows), lambda h: (h, 0))
    split = pl.BlockSpec((blocks // 2, 2, 8 * group, rows), lambda h: (0, 0, h, 0))
    return pl.pallas_call(
        attend_back_kernel,
        grid=(heads // group,),
        in_specs=[
            big, big, flat, keys, values, flat, flat,
            pl.BlockSpec((group, rows, LANES), lambda h: (h, 0, 0)),
            pl.BlockSpec((rows, LANES), lambda h: (0, 0)),
            pl.BlockSpec((STRIP, cols), lambda h: (0, 0)),
        ],
        out_specs=[big, big, flat, split, split],
        out_shape=[
            jax.ShapeDtypeStruct(pair.shape, F32),
            jax.ShapeDtypeStruct(pair.shape, F32),
            jax.ShapeDtypeStruct((feats, rows), F32),
            jax.ShapeDtypeStruct((blocks // 2, 2, feats, rows), F32),
            jax.ShapeDtypeStruct((blocks // 2, 2, feats, rows), F32),
        ],
        scratch_shapes=[pltpu.VMEM((group, rows, cols), F32)] * 2
        + [pltpu.VMEM((group, rows, cols), BF16)] * 4,
        compiler_params=pltpu.CompilerParams(vmem_limit_bytes=56 << 20),
        cost_estimate=pl.CostEstimate(
            flops=2 * 400 * heads * rows * cols,
            bytes_accessed=16 * heads * rows * cols,
            transcendentals=heads * rows * cols,
        ),
        name="attend_back",
    )(pair, cot, queries, kept, kept, mixed, d_mixed, log_sums, id_column, id_row)


SMALL_LN1_GAIN, SMALL_LN1_BIAS, SMALL_LN2_GAIN, SMALL_LN2_BIAS = 0, 1, 2, 3
SMALL_B_OUT, SMALL_B_DOWN, SMALL_PENALTY = 4, 5, 6
SMALL_B_QUERY, SMALL_B_VALUE, SMALL_B_UP = 8, 9, 10
SMALL_ROWS = 16


def feed_kernel(
    mixed, atoms, w_out, b_out, gain, bias, w_up, b_up, w_down, cot,
    d_mixed, hidden, down, d_hidden, grad_up, grad_down, small,
    mixed_all, normal_two, rate_two, part, landed, back, back_landed,
    mix_send, mix_recv, part_send, part_recv, back_send, back_recv,
):
    zs, feats, rows = mixed_all.shape
    piece = rows // zs
    width = atoms.shape[1]
    z = lax.axis_index("head")
    peers = others(z, zs)
    meet([{"head": peer} for peer in peers])
    mixed_all[z] = mixed[...]
    copies = [
        send(mixed_all.at[z], mixed_all.at[z], mix_send.at[n], mix_recv.at[z], {"head": peer})
        for n, peer in enumerate(peers)
    ]
    mine = pl.ds(pl.multiple_of(z * piece, 8), piece)
    small[...] = jnp.zeros_like(small)
    small[SMALL_B_DOWN : SMALL_B_DOWN + 1, :] = column_sum(cot[mine, :])
    cots = halves(cot[...])
    downs = halves(w_down[...])
    d_act = dot_halves(cots, downs, NT)
    ups = halves(w_up[...])
    outs = halves(w_out[...])
    for peer in peers:
        arrived(mixed_all.at[peer], mix_recv.at[peer])
    mixed_rows = mixed_all[...].reshape(zs * feats, rows).T
    hidden_rows = atoms[...] + dot_halves(halves(mixed_rows), outs) + b_out[...]
    hidden[...] = hidden_rows
    normal, rate = normalize(hidden_rows)
    normal_two[...] = normal
    rate_two[...] = jnp.broadcast_to(rate, rate_two.shape)
    normed = normal * gain[...] + bias[...]
    pre = dot_halves(halves(normed), ups) + b_up[...]
    phi = 0.5 * (1.0 + lax.erf(pre * math.sqrt(0.5)))
    act = pre * phi
    d_pre = d_act * (phi + pre * jnp.exp(-0.5 * pre * pre) * (1.0 / math.sqrt(2.0 * math.pi)))
    d_pres = halves(d_pre)
    part[...] = dot_halves(d_pres, ups, NT).reshape(zs, piece, width)
    copies += [
        send(part.at[peer], landed.at[z], part_send.at[n], part_recv.at[z], {"head": peer})
        for n, peer in enumerate(peers)
    ]
    landed[z] = part[z]
    down[...] = dot_halves(halves(act), downs)
    grad_up[...] = dot_halves(halves(normed.T), d_pres)
    grad_down[...] = dot_halves(halves(act.T), cots)
    small[SMALL_B_UP : SMALL_B_UP + 1, 0 : d_pre.shape[1]] = column_sum(d_pre)
    for peer in peers:
        arrived(landed.at[peer], part_recv.at[peer])
    d_normed = functools.reduce(jnp.add, [landed[n] for n in range(zs)])
    normal = normal_two[mine, :]
    small[SMALL_LN2_GAIN : SMALL_LN2_GAIN + 1, :] = column_sum(d_normed * normal)
    small[SMALL_LN2_BIAS : SMALL_LN2_BIAS + 1, :] = column_sum(d_normed)
    d_rows = cot[mine, :] + normalize_back(d_normed, gain[...], normal, rate_two[mine, 0:1])
    d_hidden[...] = d_rows
    small[SMALL_B_OUT : SMALL_B_OUT + 1, :] = column_sum(d_rows)
    d_halves = halves(d_rows)
    for n in range(zs):
        some = slice(n * feats, (n + 1) * feats)
        back[n] = dot_halves(d_halves, (outs[0][some], outs[1][some]), NT)
    copies += [
        send(back.at[peer], back_landed.at[z], back_send.at[n], back_recv.at[z], {"head": peer})
        for n, peer in enumerate(peers)
    ]
    back_landed[z] = back[z]
    for peer in peers:
        arrived(back_landed.at[peer], back_recv.at[peer])
    d_mixed[...] = back_landed[...].reshape(rows, feats).T
    for copy in copies:
        copy.wait_send()


def feed(zs, mixed, atoms, w_out, b_out, gain, bias, w_up, b_up, w_down, cot):
    feats, rows = mixed.shape
    width = atoms.shape[1]
    units = w_up.shape[1]
    piece = rows // zs
    return pl.pallas_call(
        feed_kernel,
        out_shape=[
            jax.ShapeDtypeStruct((feats, rows), F32),
            jax.ShapeDtypeStruct((rows, width), F32),
            jax.ShapeDtypeStruct((rows, width), F32),
            jax.ShapeDtypeStruct((piece, width), F32),
            jax.ShapeDtypeStruct((width, units), F32),
            jax.ShapeDtypeStruct((units, width), F32),
            jax.ShapeDtypeStruct((SMALL_ROWS, width), F32),
        ],
        in_specs=[VMEM] * 10,
        out_specs=[VMEM] * 7,
        scratch_shapes=[
            pltpu.VMEM((zs, feats, rows), F32),
            pltpu.VMEM((rows, width), F32),
            pltpu.VMEM((rows, LANES), F32),
            pltpu.VMEM((zs, piece, width), F32),
            pltpu.VMEM((zs, piece, width), F32),
            pltpu.VMEM((zs, piece, feats), F32),
            pltpu.VMEM((zs, piece, feats), F32),
        ]
        + [pltpu.SemaphoreType.DMA((zs,))] * 6,
        compiler_params=pltpu.CompilerParams(
            collective_id=1, has_side_effects=True, vmem_limit_bytes=48 << 20
        ),
        name="feed",
    )(mixed, atoms, w_out, b_out, gain, bias, w_up, b_up, w_down, cot)


def finish_kernel(
    d_queries, d_keys, d_values, mixed, atoms, d_hidden, d_hidden_all, w_query, w_key, w_value,
    gain, bias, squares, id_column, id_row, small_in,
    grad_atoms, grad_query, grad_key, grad_value, grad_out, small, penalty,
    sib_keys, sib_values, go_keys, go_values, got_keys, got_values,
    part, landed, grads, sib_grads, go_grads, got_grads, total_grads, small_z, small_all,
    sib_send, sib_recv, kv_send, kv_recv, part_send, part_recv, back_send, back_recv,
    g_send, g_recv, t_send, t_recv, f_send, small_z_send, small_z_recv, small_send, small_recv,
):
    chips, _, feats, rows = d_keys.shape
    zs, piece, width = part.shape
    teams, _, share, _ = grads.shape
    blk, z, dp = lax.axis_index("blk"), lax.axis_index("head"), lax.axis_index("dp")
    core, chip = lax.rem(blk, 2), lax.div(blk, 2)
    other_core = 1 - core
    sibling = {"blk": blk + 1 - 2 * core}
    peers = others(z, zs)
    team = dp * chips + chip
    far_teams = others(team, teams)
    far_chips = others(chip, chips)
    place = team * 2 + core
    far_places = others(place, teams * 2)

    def of_team(value, kind):
        return {"dp": lax.div(value, chips), "blk": lax.rem(value, chips) * 2 + kind}

    plane = [of_team(lax.div(value, 2), lax.rem(value, 2)) for value in far_places]
    meet([{"head": peer} for peer in peers] + plane)
    copies = [
        send(d_keys.at[:, other_core], sib_keys, sib_send.at[0], sib_recv.at[0], sibling),
        send(d_values.at[:, other_core], sib_values, sib_send.at[1], sib_recv.at[1], sibling),
    ]
    normal, rate = normalize(atoms[...])
    normed = halves(normal * gain[...] + bias[...])
    dq_rows = d_queries[...].T
    d_normed = dot_full(dq_rows, w_query[...], NT)
    grad_q = dot_halves(halves(d_queries[...]), normed)
    grad_o = dot_full(mixed[...], d_hidden_all[...])
    mine = pl.ds(pl.multiple_of(z * piece, 8), piece)
    own = id_column[mine, 0:1]
    same = own == id_row[0:1, :]
    norms = jnp.sqrt(squares[...] + 1.0)
    terms = jnp.where(same, jnp.log1p(jnp.exp(norms - math.sqrt(zs * feats // DH))), 0.0)
    number = jnp.where(same, 1.0, 0.0)

    def total(value):
        return jnp.sum(jnp.sum(value, axis=1, keepdims=True), axis=0, keepdims=True)

    lane = lax.broadcasted_iota(jnp.int32, (1, width), 1)
    small_z[z] = small_in[0:8, :]
    small_z[z, SMALL_PENALTY : SMALL_PENALTY + 1, :] = jnp.where(
        lane == 0, total(terms), jnp.where(lane == 1, total(number), 0.0)
    )
    arrived(sib_keys, sib_recv.at[0])
    arrived(sib_values, sib_recv.at[1])
    go_keys[...] = sib_keys[...] + d_keys[:, core]
    go_values[...] = sib_values[...] + d_values[:, core]
    for n, peer in enumerate(far_chips):
        target = {"blk": peer * 2 + core}
        copies.append(send(go_keys.at[peer], got_keys.at[chip], kv_send.at[0, n], kv_recv.at[0, chip], target))
        copies.append(
            send(go_values.at[peer], got_values.at[chip], kv_send.at[1, n], kv_recv.at[1, chip], target)
        )
    got_keys[chip] = go_keys[chip]
    got_values[chip] = go_values[chip]
    for peer in far_chips:
        arrived(got_keys.at[peer], kv_recv.at[0, peer])
        arrived(got_values.at[peer], kv_recv.at[1, peer])
    dk = functools.reduce(jnp.add, [got_keys[n] for n in range(chips)])
    dv = functools.reduce(jnp.add, [got_values[n] for n in range(chips)])
    dv_rows = dv.T
    d_normed = (
        d_normed + dot_full(dk.T, w_key[...], NT) + dot_full(dv_rows, w_value[...], NT)
    )
    part[...] = d_normed.reshape(zs, piece, width)
    copies += [
        send(part.at[peer], landed.at[z], part_send.at[n], part_recv.at[z], {"head": peer})
        for n, peer in enumerate(peers)
    ]
    landed[z] = part[z]
    grad_k = dot_halves(halves(dk), normed)
    grad_v = dot_halves(halves(dv), normed)
    grads[...] = jnp.concatenate([grad_q, grad_k, grad_v, grad_o], axis=0).reshape(grads.shape)
    copies.append(send(grads.at[:, other_core], sib_grads, sib_send.at[2], sib_recv.at[2], sibling))
    arrived(sib_grads, sib_recv.at[2])
    go_grads[...] = sib_grads[...] + grads[:, core]
    copies += [
        send(go_grads.at[peer], got_grads.at[team], g_send.at[n], g_recv.at[team], of_team(peer, core))
        for n, peer in enumerate(far_teams)
    ]
    got_grads[team] = go_grads[team]
    for peer in peers:
        arrived(landed.at[peer], part_recv.at[peer])
    d_normed = functools.reduce(jnp.add, [landed[n] for n in range(zs)])
    normal, rate = normalize(atoms[mine, :])
    small_z[z, SMALL_LN1_GAIN : SMALL_LN1_GAIN + 1, :] = column_sum(d_normed * normal)
    small_z[z, SMALL_LN1_BIAS : SMALL_LN1_BIAS + 1, :] = column_sum(d_normed)
    grad_atoms[mine, :] = d_hidden[...] + normalize_back(d_normed, gain[...], normal, rate)
    copies += [
        send(small_z.at[z], small_z.at[z], small_z_send.at[n], small_z_recv.at[z], {"head": peer})
        for n, peer in enumerate(peers)
    ]
    copies += [
        send(grad_atoms.at[mine], grad_atoms.at[mine], back_send.at[n], back_recv.at[z], {"head": peer})
        for n, peer in enumerate(peers)
    ]
    for peer in far_teams:
        arrived(got_grads.at[peer], g_recv.at[peer])
    total_grads[team, core] = functools.reduce(jnp.add, [got_grads[n] for n in range(teams)])
    ready = total_grads.at[team, core]
    copies.append(send(ready, ready, t_send.at[0], t_recv.at[team, core], sibling))
    copies += [
        send(ready, ready, t_send.at[n + 1], t_recv.at[team, core], of_team(peer, core))
        for n, peer in enumerate(far_teams)
    ]
    for peer in peers:
        arrived(small_z.at[peer], small_z_recv.at[peer])
    small_all[place, 0:8, :] = functools.reduce(jnp.add, [small_z[n] for n in range(zs)])
    small_all[place, 8:16, :] = small_in[8:16, :]
    small_all[place, SMALL_B_QUERY : SMALL_B_QUERY + 1, 0:feats] = column_sum(dq_rows)
    small_all[place, SMALL_B_VALUE : SMALL_B_VALUE + 1, 0:feats] = column_sum(dv_rows)
    copies += [
        send(small_all.at[place], small_all.at[place], small_send.at[n], small_recv.at[place], target)
        for n, target in enumerate(plane)
    ]
    for n, peer in enumerate(far_teams):
        ready = total_grads.at[peer, core]
        arrived(ready, t_recv.at[peer, core])
        copies.append(send(ready, ready, f_send.at[n], t_recv.at[peer, core], sibling))
    for source in far_places:
        arrived(small_all.at[source], small_recv.at[source])
    summed = functools.reduce(jnp.add, [small_all[n] for n in range(2 * teams)])
    small[...] = summed
    ends = summed[SMALL_PENALTY : SMALL_PENALTY + 1, :]
    penalty[...] = ends[:, 0:1] / ends[:, 1:2]
    for peer in [team] + far_teams:
        ready = total_grads.at[peer, other_core]
        arrived(ready, t_recv.at[peer, other_core])
    done = total_grads[...].reshape(4 * feats, width)
    grad_query[...] = done[0:feats].T
    grad_key[...] = done[feats : 2 * feats].T
    grad_value[...] = done[2 * feats : 3 * feats].T
    grad_out[...] = done[3 * feats :]
    for peer in peers:
        there = pl.ds(pl.multiple_of(peer * piece, 8), piece)
        arrived(grad_atoms.at[there], back_recv.at[peer])
    for copy in copies:
        copy.wait_send()


def finish(zs, dps, *operands):
    d_queries, d_keys, atoms = operands[0], operands[1], operands[4]
    chips, _, feats, rows = d_keys.shape
    width = atoms.shape[1]
    piece = rows // zs
    teams = dps * chips
    share = 4 * feats // (2 * teams)
    some = pltpu.VMEM((chips, feats, rows), F32)
    slab = pltpu.VMEM((zs, piece, width), F32)
    both = pltpu.VMEM((teams, 2, share, width), F32)
    one = pltpu.VMEM((teams, share, width), F32)
    dma = pltpu.SemaphoreType.DMA
    return pl.pallas_call(
        finish_kernel,
        out_shape=[
            jax.ShapeDtypeStruct((rows, width), F32),
            jax.ShapeDtypeStruct((width, feats), F32),
            jax.ShapeDtypeStruct((width, feats), F32),
            jax.ShapeDtypeStruct((width, feats), F32),
            jax.ShapeDtypeStruct((feats, width), F32),
            jax.ShapeDtypeStruct((SMALL_ROWS, width), F32),
            jax.ShapeDtypeStruct((1, 1), F32),
        ],
        in_specs=[VMEM] * len(operands),
        out_specs=[VMEM] * 7,
        scratch_shapes=[some] * 6
        + [slab, slab, both, one, one, one, both]
        + [
            pltpu.VMEM((zs, 8, width), F32),
            pltpu.VMEM((2 * teams, SMALL_ROWS, width), F32),
            dma((3,)), dma((3,)),
            dma((2, chips)), dma((2, chips)),
            dma((zs,)), dma((zs,)),
            dma((zs,)), dma((zs,)),
            dma((teams,)), dma((teams,)),
            dma((teams,)), dma((teams, 2)), dma((teams,)),
            dma((zs,)), dma((zs,)),
            dma((2 * teams,)), dma((2 * teams,)),
        ],
        compiler_params=pltpu.CompilerParams(
            collective_id=2, has_side_effects=True, vmem_limit_bytes=56 << 20
        ),
        name="finish",
    )(*operands)


def local(
    zs, dps,
    atoms, pair, mol_ids, ln1_gain, ln1_bias, w_query, b_query, w_key, w_value, b_value, w_out, b_out,
    ln2_gain, ln2_bias, w_up, b_up, w_down, b_down, cot_atoms, cot_pair,
):
    blocks = pair.shape[3] // pair.shape[2]
    inputs, cot = atoms[0], cot_atoms[0]

    def line(value):
        return value.reshape(1, -1)

    queries, kept, id_column = project(
        blocks, inputs, mol_ids, line(ln1_gain), line(ln1_bias), w_query, line(b_query), w_key, w_value,
        line(b_value),
    )
    w_out_all = lax.all_gather(w_out, "head", axis=0, tiled=True)
    mixed, log_sums, squares, id_row = attend(pair, queries, kept, id_column)
    squares = lax.psum_scatter(squares, "head", scatter_dimension=0, tiled=True)
    d_mixed, hidden, down, d_hidden, grad_up, grad_down, small = feed(
        zs, mixed, inputs, w_out_all, line(b_out), line(ln2_gain), line(ln2_bias), w_up, line(b_up), w_down, cot
    )
    down = lax.psum(down, "head")
    out_atoms = hidden + down + b_down
    d_hidden_all = lax.all_gather(d_hidden, "head", axis=0, tiled=True)
    grad_up, grad_down = lax.psum((grad_up, grad_down), ("blk", "dp"))
    out_pair, grad_pair, d_queries, d_keys, d_values = attend_back(
        pair, cot_pair, queries, kept, mixed, d_mixed, log_sums, id_column, id_row
    )
    grad_atoms, grad_query, grad_key, grad_value, grad_out, small, penalty = finish(
        zs, dps,
        d_queries, d_keys, d_values, mixed, inputs, d_hidden, d_hidden_all, w_query, w_key, w_value,
        line(ln1_gain), line(ln1_bias), squares, id_column, id_row, small,
    )
    feats, units = w_query.shape[1], w_up.shape[1]
    return (
        out_atoms[None],
        out_pair,
        penalty[0, 0],
        grad_atoms[None],
        grad_pair,
        small[SMALL_LN1_GAIN],
        small[SMALL_LN1_BIAS],
        grad_query,
        small[SMALL_B_QUERY, :feats],
        grad_key,
        grad_value,
        small[SMALL_B_VALUE, :feats],
        grad_out,
        small[SMALL_B_OUT],
        small[SMALL_LN2_GAIN],
        small[SMALL_LN2_BIAS],
        grad_up,
        small[SMALL_B_UP, :units],
        grad_down,
        small[SMALL_B_DOWN],
    )


def solution(mesh):
    rows, pairs = P("dp", "blk", None), P("dp", "head", "blk", None)
    columns = P(None, "head")
    return jax.shard_map(
        functools.partial(local, mesh.shape["head"], mesh.shape["dp"]),
        mesh=mesh,
        in_specs=(
            rows, pairs, P("dp", "blk"), P(), P(), columns, P("head"), columns, columns, P("head"),
            P("head", None), P(), P(), P(), columns, P("head"), P("head", None), P(), rows, pairs,
        ),
        out_specs=(
            rows, pairs, P(), rows, pairs, P(), P(), columns, P("head"), columns, columns, P("head"),
            P("head", None), P(), P(), P(), columns, P("head"), P("head", None), P(),
        ),
        check_vma=False,
    )
```

time: 523 us -> 239 us (0.46); the launches traced: 514 us -> 238 us
  matrix products: 185 us -> 0 us
  waiting for transfers between devices: 187 us -> 15.7 us
  Pallas kernels: 0 us -> 156 us
  other arithmetic: 30.1 us -> 1.93 us
  blocking collectives: 46.9 us -> 19.7 us
  starting transfers between devices: 12.1 us -> 0.16 us
  local copies, waits for them, and re-layouts: 34.4 us -> 28.4 us
    dot_general x40 -> x0, matrix products: 185 us -> none  [the longest x18 42.1 us: matmul_full(): return jnp.dot(left, right, precision=FULL_PRECISION)]
    psum x4 -> x2, waiting for transfers between devices: 187 us -> 14.4 us  [the longest x1 14.4 us: local(): grad_up, grad_down = lax.psum((grad_up, grad_down), ('blk', 'dp'))]
    pallas_call x0 -> x5, Pallas kernels: none -> 156 us  [the longest x1 53 us: feed(): pl.pallas_call(feed_kernel, out_shape=[jax.ShapeDtypeStruct((feats, rows)...]
    psum x1 -> x0, blocking collectives: 25.7 us -> none  [local(): numer_all, count_all = lax.psum((numer, jnp.sum(valid)), ('blk', 'dp'))]
    reduce_sum x14 -> x0, other arithmetic: 21 us -> none  [the longest x1 6.5 us: local(): run_total = jnp.sum(weights, -1)]
    ppermute x20 -> x0, starting transfers between devices: 12 us -> none  [from_behind(): return lax.ppermute(value, axis, pairs)]
    unnamed x93 -> x61, local copies, waits for them, and re-layouts: 16.2 us -> 25.6 us
    broadcast_in_dim x1 -> x0, local copies, waits for them, and re-layouts: 8.31 us -> none  [local(): jnp.where(same_mol[None], jnp.exp(masked - new_max[:, :, None]), 0.0)]
  transfers between devices with their start and end apart: 24 -> 4, of which waited for: 4 -> 1; matrix products, arithmetic and copies ran while one was open for 25% -> 2% of each run, Pallas kernels for 0% -> 66%
where the time goes in v1:
time: 239 us; the launch traced here: 238 us
  Pallas kernels  156 us (65%)
  local copies, waits for them, and re-layouts  28.4 us (12%)
  blocking collectives  19.7 us (8%)
  between operations  15.8 us (7%)
  waiting for transfers between devices  15.7 us (7%)
    pallas_call x1, Pallas kernels, feed(): pl.pallas_call(feed_kernel, out_shape=[jax.ShapeDtypeStruct((feats, rows)...  53 us
    pallas_call x1, Pallas kernels, finish(): pl.pallas_call(finish_kernel, out_shape=[jax.ShapeDtypeStruct((rows, widt...  41.5 us
    pallas_call x1, Pallas kernels, attend_back(): pl.pallas_call(attend_back_kernel, grid=(heads // group,), in_specs=[big,...  32.6 us
    unnamed x61, local copies, waits for them, and re-layouts  25.6 us
    all_gather x1, blocking collectives, local(): d_hidden_all = lax.all_gather(d_hidden, 'head', axis=0, tiled=True)  19.7 us
    pallas_call x1, Pallas kernels, attend(): pl.pallas_call(attend_kernel, grid=(heads // group,), in_specs=[pl.BlockS...  17.1 us
    psum x1, waiting for transfers between devices, local(): grad_up, grad_down = lax.psum((grad_up, grad_down), ('blk', 'dp'))  14.4 us
    pallas_call x1, Pallas kernels, project(): pl.pallas_call(project_kernel, out_shape=[jax.ShapeDtypeStruct((feats, ro...  12.2 us
  transfers between devices with their start and end apart: 4, of which 1 were waited for; matrix products, arithmetic and copies ran while one was open for 2% of the time, Pallas kernels for 66%

profile of v1, /device:TPU:0, one launch (start us, length us, event | category | flops | bytes accessed | tf_op | source)
XLA Modules:
  0.0 238.1 jit_solution(652824914659206581)
XLA Ops:
  7.2 0.0 all-gather.2.cloned.1.call-start
  7.3 0.7 all-gather.2.cloned.1.call-update
  8.0 0.0 reduce-scatter.2.cloned.1.call-start
  8.0 0.0 copy-start.1
  8.0 1.0 copy-done.1
  9.1 0.9 copy-done.6
  10.0 0.9 copy-done.7
  11.0 0.9 copy-done.8
  11.9 0.7 copy-done.17
  12.6 0.7 copy-done.18
  13.3 0.7 copy-done.23
  14.0 0.7 copy-done.24
  14.6 0.7 copy-done.25
  15.3 12.2 %project.1 = (f32[128,256]{1,0:T(8,128)S(1)}, f32[4,264,256]{2,1,0:T(8,128)S(1)}, f32[256,128]{1,0:T(8,128)S(1)}) custom-call(f32[256,512]{1,0:T(8,128)S(1)} %bitcast.26, s32[1,256]{1,0:T(1,128)S(1)} %copy-done.23, f32[1,512]{1,0:T(1,128)S(1)} %bitcast.30, f32[1,512]{1,0:T(1,128)S(1)} %bitcast.32, f32[512,128]{1,0:T(8,128)S(1)} %copy-done.6, ...), custom_call_target="tpu_custom_call" | custom-call | tf_op jit(solution)/shard_map/project/pallas_call | solution.py:137
  27.5 0.0 copy-start.4
  27.5 0.0 copy-start.10
  27.5 17.1 %attend.1 = (f32[128,256]{1,0:T(8,128)S(1)}, f32[16,256,128]{2,1,0:T(8,128)S(1)}, f32[256,1024]{1,0:T(8,128)}, f32[16,1024]{1,0:T(8,128)S(1)}) custom-call(f32[1,16,256,1024]{3,2,1,0:T(8,128)} %pair.3, f32[128,256]{1,0:T(8,128)S(1)} %get-tuple-element.46.queries, f32[4,264,256]{2,1,0:T(8,128)S(1)} %get-tuple-element.47.keys.values.ids, ...), custom_call_target="tpu_custom_call" | custom-call | flops 1677721600 | bytes 16777216 | tf_op jit(solution)/shard_map/attend/pallas_call | solution.py:246
  44.6 1.4 copy-done.3
  46.0 0.6 copy-done.14
  46.6 0.0 reduce-scatter.2.cloned.1.call-update
  46.7 0.0 all-reduce.4.cloned.1.call-start
  46.7 0.0 all-gather.2.cloned.1.call-done.w_out
  46.8 1.2 copy-done.9
  48.0 53.0 %feed.1 = (f32[128,256]{1,0:T(8,128)S(1)}, f32[256,512]{1,0:T(8,128)S(1)}, f32[256,512]{1,0:T(8,128)S(1)}, f32[64,512]{1,0:T(8,128)S(1)}, f32[512,512]{1,0:T(8,1...) custom-call(f32[128,256]{1,0:T(8,128)S(1)} %get-tuple-element.49.mixed, f32[256,512]{1,0:T(8,128)S(1)} %bitcast.27, ...), custom_call_target="tpu_custom_call" | custom-call | tf_op jit(solution)/shard_map/feed/pallas_call | solution.py:468
  101.0 0.0 copy-start.13
  101.0 0.8 copy-done.13
  101.8 0.7 copy-done.15
  102.5 0.6 copy-done.16
  103.1 0.0 all-reduce.4.cloned.1.call-update
  103.1 0.0 all-reduce.6.cloned.1.call-start
  103.2 0.5 all-reduce.6.cloned.1.call-update
  103.7 19.7 %all_gather.7.d_hidden_all = f32[256,512]{1,0:T(8,128)} all-gather(f32[64,512]{1,0:T(8,128)S(1)} %get-tuple-element.59.d_hidden), channel_id=1, replica_groups=mesh['blk'=4,'head'=4,'dp'=2] {'head'}, dimensions={0}, use_global_device_ids=true | all-gather | bytes 655360 | tf_op jit(solution)/shard_map/all_gather | solution.py:717
  123.4 0.0 copy-start.26
  123.5 32.6 %attend_back.1 = (f32[1,16,256,1024]{3,2,1,0:T(8,128)}, f32[1,16,256,1024]{3,2,1,0:T(8,128)}, f32[128,256]{1,0:T(8,128)}, f32[2,2,128,256]{3,2,1,0:T(8,128)}, f32[2,2,128,256]{3,2,1,0:T(8,128)}) custom-call(f32[1,16,256,1024]{3,2,1,0:T(8,128)} %pair.3, f32[1,16,256,1024]{3,2,1,0:T(8,128)} %cot.1, f32[128,256]{1,0:T(8,128)} %copy-done.10, ...), custom_call_target="tpu_custom_call" | custom-call | flops 3355443200 | bytes 67108864 | tf_op jit(solution)/shard_map/attend_back/pallas_call | solution.py:354
  156.1 0.0 reduce-scatter.2.cloned.1.call-done.squares
  156.1 41.5 %finish.1 = (f32[256,512]{1,0:T(8,128)}, f32[512,128]{1,0:T(8,128)}, f32[512,128]{1,0:T(8,128)}, f32[512,128]{1,0:T(8,128)}, f32[128,512]{1,0:T(8,128)}, /*index=5*/f32[16,512]{1,0:T(8,128)}, f32[1,1]{1,0:T(1,128)}) custom-call(f32[128,256]{1,0:T(8,128)} %get-tuple-element.56.d_queries, f32[2,2,128,256]{3,2,1,0:T(8,128)} %get-tuple-element.57.d_keys, ...), custom_call_target="tpu_custom_call" | custom-call | tf_op jit(solution)/shard_map/finish/pallas_call | solution.py:660
  197.6 1.3 slice_bitcast_fusion
  198.9 1.5 fusion
  200.4 0.0 all-reduce.4.cloned.1.call-done
  200.4 1.9 add_bitcast_fusion
  202.4 14.4 %all-reduce.6.cloned.1.call-done = (f32[512,512]{1,0:T(8,128)}, f32[512,512]{1,0:T(8,128)}) async-done(((f32[512,512]{1,0:T(8,128)}, f32[512,512]{1,0:T(8,128)}), (f32[512,512]{1,0:T(8,128)}, f32[512,512]{1,0:T(8,128)})) %all-reduce.6.cloned.1.call-update) | async-done | bytes 2097168 | tf_op jit(solution)/shard_map/psum | solution.py:718
  217.4 1.9 copy.52
  219.2 1.7 copy.53
  220.9 1.7 copy.54
  222.6 1.7 copy.55
  224.2 1.7 copy.56
  225.9 2.3 copy.57
  228.2 2.3 copy.58
  (34 shorter events, 0.1 us)
Async XLA Ops:
  7.2 39.5 %copy-start.22 = (f32[512]{0:T(512)S(1)}, f32[512]{0:T(512)}, u32[]{:S(2)}) copy-start(f32[512]{0:T(512)} %param.35) | copy-start | bytes 6148
  7.2 39.5 %copy-start.21 = (f32[512]{0:T(512)S(1)}, f32[512]{0:T(512)}, u32[]{:S(2)}) copy-start(f32[512]{0:T(512)} %param.33) | copy-start | bytes 6148
  7.2 39.5 %copy-start.20 = (f32[512]{0:T(512)S(1)}, f32[512]{0:T(512)}, u32[]{:S(2)}) copy-start(f32[512]{0:T(512)} %param.32) | copy-start | bytes 6148
  7.2 39.5 %copy-start.19 = (f32[512]{0:T(512)S(1)}, f32[512]{0:T(512)}, u32[]{:S(2)}) copy-start(f32[512]{0:T(512)} %param.31) | copy-start | bytes 6148
  7.2 39.5 %all-gather.2.cloned.1.call-start = ((), (), s32[]{:S(2)}) async-start(), calls=%async_computation.1 | async-start | bytes 1310720 | tf_op jit(solution)/shard_map/all_gather | solution.py:709
  8.0 148.1 %reduce-scatter.2.cloned.1.call-start = ((), (), s32[]{:S(2)}) async-start(), calls=%async_computation.3 | async-start | bytes 1310720 | tf_op jit(solution)/shard_map/reduce_scatter | solution.py:711
  8.0 1.0 copy-start.1
  9.1 0.9 copy-start.6
  10.0 0.9 copy-start.7
  11.0 0.9 copy-start.8
  11.9 0.7 copy-start.17
  12.6 0.7 copy-start.18
  13.3 0.7 copy-start.23
  14.0 0.7 copy-start.24
  14.6 0.7 copy-start.25
  15.3 31.5 %copy-start.2 = (f32[1,256,512]{2,1,0:T(8,128)S(1)}, f32[1,256,512]{2,1,0:T(8,128)}, u32[]{:S(2)}) copy-start(f32[1,256,512]{2,1,0:T(8,128)} %param.20) | copy-start | bytes 1572868
  15.3 31.5 %copy-start.11 = (f32[1,256,512]{2,1,0:T(8,128)S(1)}, f32[1,256,512]{2,1,0:T(8,128)}, u32[]{:S(2)}) copy-start(f32[1,256,512]{2,1,0:T(8,128)} %param.38) | copy-start | bytes 1572868
  27.5 95.9 %copy-start = (f32[4,264,256]{2,1,0:T(8,128)}, f32[4,264,256]{2,1,0:T(8,128)S(1)}, u32[]{:S(2)}) copy-start(f32[4,264,256]{2,1,0:T(8,128)S(1)} %get-tuple-element.47.keys.values.ids) | copy-start | bytes 3244036
  27.5 95.9 %copy-start.4 = (f32[256,128]{1,0:T(8,128)}, f32[256,128]{1,0:T(8,128)S(1)}, u32[]{:S(2)}) copy-start(f32[256,128]{1,0:T(8,128)S(1)} %get-tuple-element.48.id_column) | copy-start | bytes 393220
  27.5 95.9 %copy-start.10 = (f32[128,256]{1,0:T(8,128)}, f32[128,256]{1,0:T(8,128)S(1)}, u32[]{:S(2)}) copy-start(f32[128,256]{1,0:T(8,128)S(1)} %get-tuple-element.46.queries) | copy-start | bytes 393220
  44.6 1.4 copy-start.3
  46.0 0.6 copy-start.14
  46.6 76.8 %copy-start.5 = (f32[128,256]{1,0:T(8,128)}, f32[128,256]{1,0:T(8,128)S(1)}, u32[]{:S(2)}) copy-start(f32[128,256]{1,0:T(8,128)S(1)} %get-tuple-element.49.mixed) | copy-start | bytes 393220
  46.7 153.8 %all-reduce.4.cloned.1.call-start = ((), (), s32[]{:S(2)}) async-start(), calls=%async_computation.2 | async-start | bytes 1048576 | tf_op jit(solution)/shard_map/psum | solution.py:715
  46.8 1.2 copy-start.9
  101.0 0.8 copy-start.13
  101.8 0.7 copy-start.15
  102.5 0.6 copy-start.16
  103.1 53.0 %copy-start.12 = (f32[64,512]{1,0:T(8,128)}, f32[64,512]{1,0:T(8,128)S(1)}, u32[]{:S(2)}) copy-start(f32[64,512]{1,0:T(8,128)S(1)} %get-tuple-element.59.d_hidden) | copy-start | bytes 393220
  103.1 113.6 %all-reduce.6.cloned.1.call-start = ((), (), s32[]{:S(2)}) async-start(), calls=%async_computation.4 | async-start | bytes 4194304 | tf_op jit(solution)/shard_map/psum | solution.py:718
  123.4 77.0 %copy-start.26 = (f32[512]{0:T(512)S(1)}, f32[512]{0:T(512)}, u32[]{:S(2)}) copy-start(f32[512]{0:T(512)} %param.37) | copy-start | bytes 6148
Sparse Core Ops, SparseCore 0:
  9.6 30.6 all-gather.1
  46.8 40.1 reduce-scatter.1
  103.2 40.9 all-reduce.3
  147.7 68.9 all-reduce.5

commit v2 on v1

--- a/solution.py
+++ b/solution.py
@@ -92,10 +92,78 @@
     return [lax.rem(index + step, count) for step in range(1, count)]
 
 
-def project_kernel(
-    atoms, ids, gain, bias, w_query, b_query, w_key, w_value, b_value,
-    queries, kept, id_column, send_sem, recv_sem,
-):
+class Operand:
+    def __init__(self, source, slot, sem):
+        self.source, self.slot, self.shape = source, slot, slot.shape
+        self.copy = pltpu.make_async_copy(source, slot, sem)
+        self.copy.start()
+
+    @property
+    def ref(self):
+        if self.copy is not None:
+            self.copy.wait()
+            self.copy = None
+        return self.slot
+
+    def __getitem__(self, index):
+        return self.ref[index]
+
+
+class Result:
+    def __init__(self, target, slot, sem):
+        self.slot, self.shape, self.at = slot, slot.shape, slot.at
+        self.copy = pltpu.make_async_copy(slot, target, sem)
+        self.begun = False
+
+    def __setitem__(self, index, value):
+        self.slot[index] = value
+
+    def __getitem__(self, index):
+        return self.slot[index]
+
+    def flush(self):
+        if not self.begun:
+            self.copy.start()
+            self.begun = True
+
+
+def staged_call(kernel, name, operands, results, scratch, megabytes, remote=None):
+    n_in, n_out = len(operands), len(results)
+
+    def body(*refs):
+        sources, targets, refs = refs[:n_in], refs[n_in : n_in + n_out], refs[n_in + n_out :]
+        slots, made, refs = refs[:n_in], refs[n_in : n_in + n_out], refs[n_in + n_out :]
+        in_sem, out_sem, refs = refs[0], refs[1], refs[2:]
+        ins = [Operand(sources[n], slots[n], in_sem.at[n]) for n in range(n_in)]
+        outs = [Result(targets[n], made[n], out_sem.at[n]) for n in range(n_out)]
+        kernel(ins, outs, refs)
+        for operand in ins:
+            operand.ref
+        for result in outs:
+            result.flush()
+        for result in outs:
+            result.copy.wait()
+
+    anywhere = pl.BlockSpec(memory_space=pl.ANY)
+    extra = {} if remote is None else {"collective_id": remote, "has_side_effects": True}
+    return pl.pallas_call(
+        body,
+        out_shape=[jax.ShapeDtypeStruct(shape, F32) for shape in results],
+        in_specs=[anywhere] * n_in,
+        out_specs=[anywhere] * n_out,
+        scratch_shapes=[pltpu.VMEM(value.shape, value.dtype) for value in operands]
+        + [pltpu.VMEM(shape, F32) for shape in results]
+        + [pltpu.SemaphoreType.DMA((n_in,)), pltpu.SemaphoreType.DMA((n_out,))]
+        + list(scratch),
+        compiler_params=pltpu.CompilerParams(vmem_limit_bytes=megabytes << 20, **extra),
+        name=name,
+    )(*operands)
+
+
+def project_kernel(operands, results, scratch):
+    atoms, ids, gain, bias, w_key, w_value, b_value, w_query, b_query = operands
+    queries, kept, id_column = results
+    send_sem, recv_sem = scratch
     blocks, feats = kept.shape[0], w_query.shape[1]
     rows = atoms.shape[0]
     chips = blocks // 2
@@ -132,26 +200,17 @@
         copy.wait_send()
 
 
-def project(blocks, atoms, ids, gain, bias, w_query, b_query, w_key, w_value, b_value):
-    rows, feats = atoms.shape[0], w_query.shape[1]
-    return pl.pallas_call(
+def project(blocks, *operands):
+    rows, feats = operands[0].shape[0], operands[4].shape[1]
+    return staged_call(
         project_kernel,
-        out_shape=[
-            jax.ShapeDtypeStruct((feats, rows), F32),
-            jax.ShapeDtypeStruct((blocks, 2 * feats + 8, rows), F32),
-            jax.ShapeDtypeStruct((rows, LANES), F32),
-        ],
-        in_specs=[VMEM] * 9,
-        out_specs=[VMEM] * 3,
-        scratch_shapes=[
-            pltpu.SemaphoreType.DMA((blocks,)),
-            pltpu.SemaphoreType.DMA((blocks,)),
-        ],
-        compiler_params=pltpu.CompilerParams(
-            collective_id=0, has_side_effects=True, vmem_limit_bytes=32 << 20
-        ),
-        name="project",
-    )(atoms, ids, gain, bias, w_query, b_query, w_key, w_value, b_value)
+        "project",
+        operands,
+        [(feats, rows), (blocks, 2 * feats + 8, rows), (rows, LANES)],
+        [pltpu.SemaphoreType.DMA((blocks,)), pltpu.SemaphoreType.DMA((blocks,))],
+        32,
+        remote=0,
+    )
 
 
 def whole_row(ref, low, count):
@@ -386,36 +445,46 @@
 SMALL_ROWS = 16
 
 
-def feed_kernel(
-    mixed, atoms, w_out, b_out, gain, bias, w_up, b_up, w_down, cot,
-    d_mixed, hidden, down, d_hidden, grad_up, grad_down, small,
-    mixed_all, normal_two, rate_two, part, landed, back, back_landed,
-    mix_send, mix_recv, part_send, part_recv, back_send, back_recv,
-):
+def team_device(team, core, chips):
+    return {"dp": lax.div(team, chips), "blk": lax.rem(team, chips) * 2 + core}
+
+
+def feed_kernel(operands, results, scratch):
+    mixed, cot, w_down, atoms, w_up, w_out, b_out, gain, bias, b_up = operands
+    d_mixed, hidden, down, d_hidden, grad_share, small = results
+    (
+        mixed_all, normal_two, rate_two, part, landed, back, back_landed, grads, sib_grads, go_grads, got_grads,
+        mix_send, mix_recv, part_send, part_recv, back_send, back_recv, sib_send, sib_recv, g_send, g_recv,
+    ) = scratch
     zs, feats, rows = mixed_all.shape
+    teams, _, share, width = grads.shape
+    chips = teams // lax.axis_size("dp")
     piece = rows // zs
-    width = atoms.shape[1]
-    z = lax.axis_index("head")
-    peers = others(z, zs)
-    meet([{"head": peer} for peer in peers])
-    mixed_all[z] = mixed[...]
+    z, blk = lax.axis_index("head"), lax.axis_index("blk")
+    core, chip = lax.rem(blk, 2), lax.div(blk, 2)
+    team = lax.axis_index("dp") * chips + chip
+    sibling = {"blk": blk + 1 - 2 * core}
+    peers, far_teams = others(z, zs), others(team, teams)
+    meet([{"head": peer} for peer in peers] + [sibling] + [team_device(peer, core, chips) for peer in far_teams])
     copies = [
-        send(mixed_all.at[z], mixed_all.at[z], mix_send.at[n], mix_recv.at[z], {"head": peer})
+        send(mixed.source, mixed_all.at[z], mix_send.at[n], mix_recv.at[z], {"head": peer})
         for n, peer in enumerate(peers)
     ]
     mine = pl.ds(pl.multiple_of(z * piece, 8), piece)
-    small[...] = jnp.zeros_like(small)
+    small[...] = jnp.zeros(small.shape, F32)
     small[SMALL_B_DOWN : SMALL_B_DOWN + 1, :] = column_sum(cot[mine, :])
     cots = halves(cot[...])
     downs = halves(w_down[...])
     d_act = dot_halves(cots, downs, NT)
     ups = halves(w_up[...])
     outs = halves(w_out[...])
+    mixed_all[z] = mixed[...]
     for peer in peers:
         arrived(mixed_all.at[peer], mix_recv.at[peer])
     mixed_rows = mixed_all[...].reshape(zs * feats, rows).T
     hidden_rows = atoms[...] + dot_halves(halves(mixed_rows), outs) + b_out[...]
     hidden[...] = hidden_rows
+    hidden.flush()
     normal, rate = normalize(hidden_rows)
     normal_two[...] = normal
     rate_two[...] = jnp.broadcast_to(rate, rate_two.shape)
@@ -431,19 +500,27 @@
         for n, peer in enumerate(peers)
     ]
     landed[z] = part[z]
+    grad_up = dot_halves(halves(d_pre.T), halves(normed))
+    grad_down = dot_halves(halves(act.T), cots)
+    grads[...] = jnp.concatenate([grad_up, grad_down], axis=0).reshape(grads.shape)
+    copies.append(send(grads.at[:, 1 - core], sib_grads, sib_send.at[0], sib_recv.at[0], sibling))
     down[...] = dot_halves(halves(act), downs)
-    grad_up[...] = dot_halves(halves(normed.T), d_pres)
-    grad_down[...] = dot_halves(halves(act.T), cots)
+    down.flush()
     small[SMALL_B_UP : SMALL_B_UP + 1, 0 : d_pre.shape[1]] = column_sum(d_pre)
+    arrived(sib_grads, sib_recv.at[0])
+    go_grads[...] = sib_grads[...] + grads[:, core]
+    copies += [
+        send(
+            go_grads.at[peer], got_grads.at[team], g_send.at[n], g_recv.at[team], team_device(peer, core, chips)
+        )
+        for n, peer in enumerate(far_teams)
+    ]
+    got_grads[team] = go_grads[team]
     for peer in peers:
         arrived(landed.at[peer], part_recv.at[peer])
     d_normed = functools.reduce(jnp.add, [landed[n] for n in range(zs)])
     normal = normal_two[mine, :]
-    small[SMALL_LN2_GAIN : SMALL_LN2_GAIN + 1, :] = column_sum(d_normed * normal)
-    small[SMALL_LN2_BIAS : SMALL_LN2_BIAS + 1, :] = column_sum(d_normed)
     d_rows = cot[mine, :] + normalize_back(d_normed, gain[...], normal, rate_two[mine, 0:1])
-    d_hidden[...] = d_rows
-    small[SMALL_B_OUT : SMALL_B_OUT + 1, :] = column_sum(d_rows)
     d_halves = halves(d_rows)
     for n in range(zs):
         some = slice(n * feats, (n + 1) * feats)
@@ -453,57 +530,65 @@
         for n, peer in enumerate(peers)
     ]
     back_landed[z] = back[z]
+    d_hidden[...] = d_rows
+    d_hidden.flush()
+    small[SMALL_LN2_GAIN : SMALL_LN2_GAIN + 1, :] = column_sum(d_normed * normal)
+    small[SMALL_LN2_BIAS : SMALL_LN2_BIAS + 1, :] = column_sum(d_normed)
+    small[SMALL_B_OUT : SMALL_B_OUT + 1, :] = column_sum(d_rows)
+    small.flush()
     for peer in peers:
         arrived(back_landed.at[peer], back_recv.at[peer])
     d_mixed[...] = back_landed[...].reshape(rows, feats).T
+    d_mixed.flush()
+    for peer in far_teams:
+        arrived(got_grads.at[peer], g_recv.at[peer])
+    grad_share[...] = functools.reduce(jnp.add, [got_grads[n] for n in range(teams)])
     for copy in copies:
         copy.wait_send()
 
 
-def feed(zs, mixed, atoms, w_out, b_out, gain, bias, w_up, b_up, w_down, cot):
-    feats, rows = mixed.shape
-    width = atoms.shape[1]
-    units = w_up.shape[1]
+def feed(zs, teams, *operands):
+    feats, rows = operands[0].shape
+    width, units = operands[4].shape
     piece = rows // zs
-    return pl.pallas_call(
+    share = units // teams
+    slab = pltpu.VMEM((zs, piece, width), F32)
+    narrow = pltpu.VMEM((zs, piece, feats), F32)
+    one = pltpu.VMEM((teams, share, width), F32)
+    dma = pltpu.SemaphoreType.DMA
+    return staged_call(
         feed_kernel,
-        out_shape=[
-            jax.ShapeDtypeStruct((feats, rows), F32),
-            jax.ShapeDtypeStruct((rows, width), F32),
-            jax.ShapeDtypeStruct((rows, width), F32),
-            jax.ShapeDtypeStruct((piece, width), F32),
-            jax.ShapeDtypeStruct((width, units), F32),
-            jax.ShapeDtypeStruct((units, width), F32),
-            jax.ShapeDtypeStruct((SMALL_ROWS, width), F32),
-        ],
-        in_specs=[VMEM] * 10,
-        out_specs=[VMEM] * 7,
-        scratch_shapes=[
+        "feed",
+        operands,
+        [(feats, rows), (rows, width), (rows, width), (piece, width), (share, width), (SMALL_ROWS, width)],
+        [
             pltpu.VMEM((zs, feats, rows), F32),
             pltpu.VMEM((rows, width), F32),
             pltpu.VMEM((rows, LANES), F32),
-            pltpu.VMEM((zs, piece, width), F32),
-            pltpu.VMEM((zs, piece, width), F32),
-            pltpu.VMEM((zs, piece, feats), F32),
-            pltpu.VMEM((zs, piece, feats), F32),
+            slab, slab, narrow, narrow,
+            pltpu.VMEM((teams, 2, share, width), F32),
+            one, one, one,
         ]
-        + [pltpu.SemaphoreType.DMA((zs,))] * 6,
-        compiler_params=pltpu.CompilerParams(
-            collective_id=1, has_side_effects=True, vmem_limit_bytes=48 << 20
-        ),
-        name="feed",
-    )(mixed, atoms, w_out, b_out, gain, bias, w_up, b_up, w_down, cot)
-
-
-def finish_kernel(
-    d_queries, d_keys, d_values, mixed, atoms, d_hidden, d_hidden_all, w_query, w_key, w_value,
-    gain, bias, squares, id_column, id_row, small_in,
-    grad_atoms, grad_query, grad_key, grad_value, grad_out, small, penalty,
-    sib_keys, sib_values, go_keys, go_values, got_keys, got_values,
-    part, landed, grads, sib_grads, go_grads, got_grads, total_grads, small_z, small_all,
-    sib_send, sib_recv, kv_send, kv_recv, part_send, part_recv, back_send, back_recv,
-    g_send, g_recv, t_send, t_recv, f_send, small_z_send, small_z_recv, small_send, small_recv,
-):
+        + [dma((zs,))] * 6
+        + [dma((1,)), dma((1,)), dma((teams,)), dma((teams,))],
+        56,
+        remote=1,
+    )
+
+
+def finish_kernel(operands, results, scratch):
+    (
+        d_keys, d_values, d_hidden, share_in, d_queries, atoms, gain, bias, w_query, mixed, squares, id_column,
+        id_row, small_in, w_key, w_value,
+    ) = operands
+    grad_atoms, total_grads, total_big, small, penalty = results
+    (
+        sib_keys, sib_values, go_keys, go_values, got_keys, got_values,
+        part, landed, grads, sib_grads, go_grads, got_grads, hidden_all, small_z, small_all,
+        sib_send, sib_recv, kv_send, kv_recv, part_send, part_recv, back_send, back_recv,
+        g_send, g_recv, t_send, t_recv, f_send, b_send, b_recv, bf_send, h_send, h_recv,
+        small_z_send, small_z_recv, small_send, small_recv,
+    ) = scratch
     chips, _, feats, rows = d_keys.shape
     zs, piece, width = part.shape
     teams, _, share, _ = grads.shape
@@ -517,41 +602,21 @@
     far_chips = others(chip, chips)
     place = team * 2 + core
     far_places = others(place, teams * 2)
-
-    def of_team(value, kind):
-        return {"dp": lax.div(value, chips), "blk": lax.rem(value, chips) * 2 + kind}
-
-    plane = [of_team(lax.div(value, 2), lax.rem(value, 2)) for value in far_places]
+    plane = [team_device(lax.div(value, 2), lax.rem(value, 2), chips) for value in far_places]
     meet([{"head": peer} for peer in peers] + plane)
     copies = [
-        send(d_keys.at[:, other_core], sib_keys, sib_send.at[0], sib_recv.at[0], sibling),
-        send(d_values.at[:, other_core], sib_values, sib_send.at[1], sib_recv.at[1], sibling),
-    ]
-    normal, rate = normalize(atoms[...])
-    normed = halves(normal * gain[...] + bias[...])
-    dq_rows = d_queries[...].T
-    d_normed = dot_full(dq_rows, w_query[...], NT)
-    grad_q = dot_halves(halves(d_queries[...]), normed)
-    grad_o = dot_full(mixed[...], d_hidden_all[...])
-    mine = pl.ds(pl.multiple_of(z * piece, 8), piece)
-    own = id_column[mine, 0:1]
-    same = own == id_row[0:1, :]
-    norms = jnp.sqrt(squares[...] + 1.0)
-    terms = jnp.where(same, jnp.log1p(jnp.exp(norms - math.sqrt(zs * feats // DH))), 0.0)
-    number = jnp.where(same, 1.0, 0.0)
-
-    def total(value):
-        return jnp.sum(jnp.sum(value, axis=1, keepdims=True), axis=0, keepdims=True)
-
-    lane = lax.broadcasted_iota(jnp.int32, (1, width), 1)
-    small_z[z] = small_in[0:8, :]
-    small_z[z, SMALL_PENALTY : SMALL_PENALTY + 1, :] = jnp.where(
-        lane == 0, total(terms), jnp.where(lane == 1, total(number), 0.0)
-    )
+        send(d_keys.source.at[:, other_core], sib_keys, sib_send.at[0], sib_recv.at[0], sibling),
+        send(d_values.source.at[:, other_core], sib_values, sib_send.at[1], sib_recv.at[1], sibling),
+    ]
+    copies += [
+        send(d_hidden.source, hidden_all.at[z], h_send.at[n], h_recv.at[z], {"head": peer})
+        for n, peer in enumerate(peers)
+    ]
+    own_keys, own_values = d_keys.ref, d_values.ref
     arrived(sib_keys, sib_recv.at[0])
     arrived(sib_values, sib_recv.at[1])
-    go_keys[...] = sib_keys[...] + d_keys[:, core]
-    go_values[...] = sib_values[...] + d_values[:, core]
+    go_keys[...] = sib_keys[...] + own_keys[:, core]
+    go_values[...] = sib_values[...] + own_values[:, core]
     for n, peer in enumerate(far_chips):
         target = {"blk": peer * 2 + core}
         copies.append(send(go_keys.at[peer], got_keys.at[chip], kv_send.at[0, n], kv_recv.at[0, chip], target))
@@ -560,6 +625,34 @@
         )
     got_keys[chip] = go_keys[chip]
     got_values[chip] = go_values[chip]
+    total_big[team, core] = share_in[...]
+    ready = total_big.at[team, core]
+    copies.append(send(ready, ready, b_send.at[0], b_recv.at[team, core], sibling))
+    copies += [
+        send(ready, ready, b_send.at[n + 1], b_recv.at[team, core], team_device(peer, core, chips))
+        for n, peer in enumerate(far_teams)
+    ]
+    normal, rate = normalize(atoms[...])
+    normed = halves(normal * gain[...] + bias[...])
+    dq_rows = d_queries[...].T
+    d_normed = dot_full(dq_rows, w_query[...], NT)
+    grad_q = dot_halves(halves(d_queries[...]), normed)
+    mine = pl.ds(pl.multiple_of(z * piece, 8), piece)
+    own = id_column[mine, 0:1]
+    same = own == id_row[0:1, :]
+    norms = jnp.sqrt(squares[...] + 1.0)
+    terms = jnp.where(same, jnp.log1p(jnp.exp(norms - math.sqrt(zs * feats // DH))), 0.0)
+    number = jnp.where(same, 1.0, 0.0)
+
+    def total(value):
+        return jnp.sum(jnp.sum(value, axis=1, keepdims=True), axis=0, keepdims=True)
+
+    lane = lax.broadcasted_iota(jnp.int32, (1, width), 1)
+    small_z[z] = small_in[0:8, :]
+    small_z[z, SMALL_PENALTY : SMALL_PENALTY + 1, :] = jnp.where(
+        lane == 0, total(terms), jnp.where(lane == 1, total(number), 0.0)
+    )
+    hidden_all[z] = d_hidden[...]
     for peer in far_chips:
         arrived(got_keys.at[peer], kv_recv.at[0, peer])
         arrived(got_values.at[peer], kv_recv.at[1, peer])
@@ -577,12 +670,17 @@
     landed[z] = part[z]
     grad_k = dot_halves(halves(dk), normed)
     grad_v = dot_halves(halves(dv), normed)
+    for peer in peers:
+        arrived(hidden_all.at[peer], h_recv.at[peer])
+    grad_o = dot_full(mixed[...], hidden_all[...].reshape(rows, width))
     grads[...] = jnp.concatenate([grad_q, grad_k, grad_v, grad_o], axis=0).reshape(grads.shape)
     copies.append(send(grads.at[:, other_core], sib_grads, sib_send.at[2], sib_recv.at[2], sibling))
     arrived(sib_grads, sib_recv.at[2])
     go_grads[...] = sib_grads[...] + grads[:, core]
     copies += [
-        send(go_grads.at[peer], got_grads.at[team], g_send.at[n], g_recv.at[team], of_team(peer, core))
+        send(
+            go_grads.at[peer], got_grads.at[team], g_send.at[n], g_recv.at[team], team_device(peer, core, chips)
+        )
         for n, peer in enumerate(far_teams)
     ]
     got_grads[team] = go_grads[team]
@@ -590,9 +688,9 @@
         arrived(landed.at[peer], part_recv.at[peer])
     d_normed = functools.reduce(jnp.add, [landed[n] for n in range(zs)])
     normal, rate = normalize(atoms[mine, :])
+    grad_atoms[mine, :] = d_hidden[...] + normalize_back(d_normed, gain[...], normal, rate)
     small_z[z, SMALL_LN1_GAIN : SMALL_LN1_GAIN + 1, :] = column_sum(d_normed * normal)
     small_z[z, SMALL_LN1_BIAS : SMALL_LN1_BIAS + 1, :] = column_sum(d_normed)
-    grad_atoms[mine, :] = d_hidden[...] + normalize_back(d_normed, gain[...], normal, rate)
     copies += [
         send(small_z.at[z], small_z.at[z], small_z_send.at[n], small_z_recv.at[z], {"head": peer})
         for n, peer in enumerate(peers)
@@ -607,7 +705,7 @@
     ready = total_grads.at[team, core]
     copies.append(send(ready, ready, t_send.at[0], t_recv.at[team, core], sibling))
     copies += [
-        send(ready, ready, t_send.at[n + 1], t_recv.at[team, core], of_team(peer, core))
+        send(ready, ready, t_send.at[n + 1], t_recv.at[team, core], team_device(peer, core, chips))
         for n, peer in enumerate(far_teams)
     ]
     for peer in peers:
@@ -620,6 +718,10 @@
         send(small_all.at[place], small_all.at[place], small_send.at[n], small_recv.at[place], target)
         for n, target in enumerate(plane)
     ]
+    for n, peer in enumerate(far_teams):
+        ready = total_big.at[peer, core]
+        arrived(ready, b_recv.at[peer, core])
+        copies.append(send(ready, ready, bf_send.at[n], b_recv.at[peer, core], sibling))
     for n, peer in enumerate(far_teams):
         ready = total_grads.at[peer, core]
         arrived(ready, t_recv.at[peer, core])
@@ -631,13 +733,11 @@
     ends = summed[SMALL_PENALTY : SMALL_PENALTY + 1, :]
     penalty[...] = ends[:, 0:1] / ends[:, 1:2]
     for peer in [team] + far_teams:
-        ready = total_grads.at[peer, other_core]
-        arrived(ready, t_recv.at[peer, other_core])
-    done = total_grads[...].reshape(4 * feats, width)
-    grad_query[...] = done[0:feats].T
-    grad_key[...] = done[feats : 2 * feats].T
-    grad_value[...] = done[2 * feats : 3 * feats].T
-    grad_out[...] = done[3 * feats :]
+        arrived(total_big.at[peer, other_core], b_recv.at[peer, other_core])
+    total_big.flush()
+    for peer in [team] + far_teams:
+        arrived(total_grads.at[peer, other_core], t_recv.at[peer, other_core])
+    total_grads.flush()
     for peer in peers:
         there = pl.ds(pl.multiple_of(peer * piece, 8), piece)
         arrived(grad_atoms.at[there], back_recv.at[peer])
@@ -646,7 +746,7 @@
 
 
 def finish(zs, dps, *operands):
-    d_queries, d_keys, atoms = operands[0], operands[1], operands[4]
+    d_keys, share_in, atoms = operands[0], operands[3], operands[5]
     chips, _, feats, rows = d_keys.shape
     width = atoms.shape[1]
     piece = rows // zs
@@ -654,24 +754,21 @@
     share = 4 * feats // (2 * teams)
     some = pltpu.VMEM((chips, feats, rows), F32)
     slab = pltpu.VMEM((zs, piece, width), F32)
-    both = pltpu.VMEM((teams, 2, share, width), F32)
     one = pltpu.VMEM((teams, share, width), F32)
     dma = pltpu.SemaphoreType.DMA
-    return pl.pallas_call(
+    return staged_call(
         finish_kernel,
-        out_shape=[
-            jax.ShapeDtypeStruct((rows, width), F32),
-            jax.ShapeDtypeStruct((width, feats), F32),
-            jax.ShapeDtypeStruct((width, feats), F32),
-            jax.ShapeDtypeStruct((width, feats), F32),
-            jax.ShapeDtypeStruct((feats, width), F32),
-            jax.ShapeDtypeStruct((SMALL_ROWS, width), F32),
-            jax.ShapeDtypeStruct((1, 1), F32),
+        "finish",
+        operands,
+        [
+            (rows, width),
+            (teams, 2, share, width),
+            (teams, 2) + share_in.shape,
+            (SMALL_ROWS, width),
+            (1, 1),
         ],
-        in_specs=[VMEM] * len(operands),
-        out_specs=[VMEM] * 7,
-        scratch_shapes=[some] * 6
-        + [slab, slab, both, one, one, one, both]
+        [some] * 6
+        + [slab, slab, pltpu.VMEM((teams, 2, share, width), F32), one, one, one, slab]
         + [
             pltpu.VMEM((zs, 8, width), F32),
             pltpu.VMEM((2 * teams, SMALL_ROWS, width), F32),
@@ -681,14 +778,62 @@
             dma((zs,)), dma((zs,)),
             dma((teams,)), dma((teams,)),
             dma((teams,)), dma((teams, 2)), dma((teams,)),
+            dma((teams,)), dma((teams, 2)), dma((teams,)),
+            dma((zs,)), dma((zs,)),
             dma((zs,)), dma((zs,)),
             dma((2 * teams,)), dma((2 * teams,)),
         ],
-        compiler_params=pltpu.CompilerParams(
-            collective_id=2, has_side_effects=True, vmem_limit_bytes=56 << 20
-        ),
-        name="finish",
-    )(*operands)
+        58,
+        remote=2,
+    )
+
+
+def place_kernel(operands, results, scratch):
+    total_grads, total_big, small, hidden, down, b_down, rows_in = operands
+    grad_query, grad_key, grad_value, grad_out, grad_up, grad_down, out_atoms, grad_atoms = results[:8]
+    feats, units = grad_out.shape[0], grad_down.shape[0]
+    width = grad_out.shape[1]
+    grad_atoms[...] = rows_in[...]
+    grad_atoms.flush()
+    done = total_grads[...].reshape(4 * feats, width)
+    grad_query[...] = done[0:feats].T
+    grad_query.flush()
+    grad_key[...] = done[feats : 2 * feats].T
+    grad_key.flush()
+    grad_value[...] = done[2 * feats : 3 * feats].T
+    grad_value.flush()
+    grad_out[...] = done[3 * feats :]
+    grad_out.flush()
+    done = total_big[...].reshape(2 * units, width)
+    grad_up[...] = done[0:units].T
+    grad_up.flush()
+    grad_down[...] = done[units:]
+    grad_down.flush()
+    out_atoms[...] = hidden[...] + down[...] + b_down[...]
+    out_atoms.flush()
+    for result, row in zip(results[8:], SMALL_OUTPUTS, strict=True):
+        result[...] = small[row : row + 1, 0 : result.shape[1]]
+
+
+SMALL_OUTPUTS = (
+    SMALL_LN1_GAIN, SMALL_LN1_BIAS, SMALL_B_QUERY, SMALL_B_VALUE, SMALL_B_OUT, SMALL_LN2_GAIN, SMALL_LN2_BIAS,
+    SMALL_B_UP, SMALL_B_DOWN,
+)
+
+
+def place(feats, units, *operands):
+    rows, width = operands[3].shape
+    lengths = {SMALL_B_QUERY: feats, SMALL_B_VALUE: feats, SMALL_B_UP: units}
+    return staged_call(
+        place_kernel,
+        "place",
+        operands,
+        [(width, feats)] * 3
+        + [(feats, width), (width, units), (units, width), (rows, width), (rows, width)]
+        + [(1, lengths.get(row, width)) for row in SMALL_OUTPUTS],
+        [],
+        32,
+    )
 
 
 def local(
@@ -703,49 +848,56 @@
         return value.reshape(1, -1)
 
     queries, kept, id_column = project(
-        blocks, inputs, mol_ids, line(ln1_gain), line(ln1_bias), w_query, line(b_query), w_key, w_value,
-        line(b_value),
+        blocks, inputs, mol_ids, line(ln1_gain), line(ln1_bias), w_key, w_value, line(b_value), w_query,
+        line(b_query),
     )
     w_out_all = lax.all_gather(w_out, "head", axis=0, tiled=True)
     mixed, log_sums, squares, id_row = attend(pair, queries, kept, id_column)
+    d_mixed, hidden, down, d_hidden, grad_share, small = feed(
+        zs, dps * blocks // 2,
+        mixed, cot, w_down, inputs, w_up, w_out_all, line(b_out), line(ln2_gain), line(ln2_bias), line(b_up),
+    )
+    squares, d_mixed = lax.optimization_barrier((squares, d_mixed))
     squares = lax.psum_scatter(squares, "head", scatter_dimension=0, tiled=True)
-    d_mixed, hidden, down, d_hidden, grad_up, grad_down, small = feed(
-        zs, mixed, inputs, w_out_all, line(b_out), line(ln2_gain), line(ln2_bias), w_up, line(b_up), w_down, cot
-    )
     down = lax.psum(down, "head")
-    out_atoms = hidden + down + b_down
-    d_hidden_all = lax.all_gather(d_hidden, "head", axis=0, tiled=True)
-    grad_up, grad_down = lax.psum((grad_up, grad_down), ("blk", "dp"))
     out_pair, grad_pair, d_queries, d_keys, d_values = attend_back(
         pair, cot_pair, queries, kept, mixed, d_mixed, log_sums, id_column, id_row
     )
-    grad_atoms, grad_query, grad_key, grad_value, grad_out, small, penalty = finish(
+    grad_atoms, total_grads, total_big, small, penalty = finish(
         zs, dps,
-        d_queries, d_keys, d_values, mixed, inputs, d_hidden, d_hidden_all, w_query, w_key, w_value,
-        line(ln1_gain), line(ln1_bias), squares, id_column, id_row, small,
-    )
-    feats, units = w_query.shape[1], w_up.shape[1]
+        d_keys, d_values, d_hidden, grad_share, d_queries, inputs, line(ln1_gain), line(ln1_bias), w_query, mixed,
+        squares, id_column, id_row, small, w_key, w_value,
+    )
+    placed = place(
+        w_query.shape[1], w_up.shape[1],
+        total_grads, total_big, small, hidden, down, line(b_down), grad_atoms,
+    )
+    grad_query, grad_key, grad_value, grad_out, grad_up, grad_down, out_atoms, grad_atoms = placed[:8]
+    (
+        grad_ln1_gain, grad_ln1_bias, grad_b_query, grad_b_value, grad_b_out, grad_ln2_gain, grad_ln2_bias,
+        grad_b_up, grad_b_down,
+    ) = [value.reshape(-1) for value in placed[8:]]
     return (
         out_atoms[None],
         out_pair,
         penalty[0, 0],
         grad_atoms[None],
         grad_pair,
-        small[SMALL_LN1_GAIN],
-        small[SMALL_LN1_BIAS],
+        grad_ln1_gain,
+        grad_ln1_bias,
         grad_query,
-        small[SMALL_B_QUERY, :feats],
+        grad_b_query,
         grad_key,
         grad_value,
-        small[SMALL_B_VALUE, :feats],
+        grad_b_value,
         grad_out,
-        small[SMALL_B_OUT],
-        small[SMALL_LN2_GAIN],
-        small[SMALL_LN2_BIAS],
+        grad_b_out,
+        grad_ln2_gain,
+        grad_ln2_bias,
         grad_up,
-        small[SMALL_B_UP, :units],
+        grad_b_up,
         grad_down,
-        small[SMALL_B_DOWN],
+        grad_b_down,
     )
 
 

time: 239 us -> 192 us (0.80)
  blocking collectives: 19.7 us -> 0 us
  waiting for transfers between devices: 15.7 us -> 1.24 us
  local copies, waits for them, and re-layouts: 28.4 us -> 15.5 us
    all_gather x1 -> x0, blocking collectives: 19.7 us -> none  [local(): d_hidden_all = lax.all_gather(d_hidden, 'head', axis=0, tiled=True)]
    psum x1 -> x0, waiting for transfers between devices: 14.4 us -> none  [local(): grad_up, grad_down = lax.psum((grad_up, grad_down), ('blk', 'dp'))]
    unnamed x61 -> x44, local copies, waits for them, and re-layouts: 25.6 us -> 15.5 us
    pallas_call x3 -> x4, Pallas kernels: 107 us -> 109 us  [staged_call(): pl.pallas_call(body, out_shape=[jax.ShapeDtypeStruct(shape, F32) for shap...]
  transfers between devices with their start and end apart: 4 -> 3, of which waited for: 1 -> 0; matrix products, arithmetic and copies ran while one was open for 2% -> 0% of each run, Pallas kernels for 66% -> 61%
where the time goes in v2:
time: 192 us; the launch traced here: 191 us
  Pallas kernels  158 us (82%)
  between operations  15.7 us (8%)
  local copies, waits for them, and re-layouts  15.5 us (8%)
    pallas_call x4, Pallas kernels, staged_call(): pl.pallas_call(body, out_shape=[jax.ShapeDtypeStruct(shape, F32) for shap...  109 us
    pallas_call x1, Pallas kernels, attend_back(): pl.pallas_call(attend_back_kernel, grid=(heads // group,), in_specs=[big,...  32.5 us
    pallas_call x1, Pallas kernels, attend(): pl.pallas_call(attend_kernel, grid=(heads // group,), in_specs=[pl.BlockS...  17.1 us
    unnamed x44, local copies, waits for them, and re-layouts  15.5 us
  transfers between devices with their start and end apart: 3, of which 0 were waited for; matrix products, arithmetic and copies ran while one was open for 0% of the time, Pallas kernels for 61%

profile of v2, /device:TPU:0, one launch (start us, length us, event | category | flops | bytes accessed | tf_op | source)
XLA Modules:
  0.0 190.9 jit_solution(5822502737399817411)
XLA Ops:
  7.2 0.0 all-gather.2.cloned.1.call-start
  7.2 0.7 all-gather.2.cloned.1.call-update
  7.9 0.0 reduce-scatter.2.cloned.1.call-start
  8.0 0.0 copy-start.1
  8.0 1.0 copy-done.1
  9.0 0.0 copy-start.7
  9.0 0.9 copy-done.7
  10.0 0.0 copy-start.8
  10.0 0.9 copy-done.8
  10.9 0.0 copy-start.9
  10.9 0.9 copy-done.9
  11.9 0.0 copy-start.16
  11.9 0.7 copy-done.16
  12.6 0.0 copy-start.17
  12.6 0.7 copy-done.17
  13.2 0.7 copy-done.19
  13.9 0.7 copy-done.20
  14.6 0.7 copy-done.21
  15.2 13.3 %project.1 = (f32[128,256]{1,0:T(8,128)S(1)}, f32[4,264,256]{2,1,0:T(8,128)S(1)}, f32[256,128]{1,0:T(8,128)S(1)}) custom-call(f32[256,512]{1,0:T(8,128)S(1)} %bitcast.25, s32[1,256]{1,0:T(1,128)S(1)} %copy-done.19, f32[1,512]{1,0:T(1,128)S(1)} %bitcast.27, f32[1,512]{1,0:T(1,128)S(1)} %bitcast.29, f32[512,128]{1,0:T(8,128)S(1)} %copy-done.7, ...), custom_call_target="tpu_custom_call" | custom-call | tf_op jit(solution)/shard_map/project/pallas_call | solution.py:149
  28.5 0.0 copy-start
  28.5 0.0 copy-start.4
  28.5 0.0 copy-start.10
  28.5 17.1 %attend.1 = (f32[128,256]{1,0:T(8,128)S(1)}, f32[16,256,128]{2,1,0:T(8,128)S(1)}, f32[256,1024]{1,0:T(8,128)}, f32[16,1024]{1,0:T(8,128)S(1)}) custom-call(f32[1,16,256,1024]{3,2,1,0:T(8,128)} %pair.3, f32[128,256]{1,0:T(8,128)S(1)} %get-tuple-element.62.queries, f32[4,264,256]{2,1,0:T(8,128)S(1)} %get-tuple-element.63.keys.values.ids, ...), custom_call_target="tpu_custom_call" | custom-call | flops 1677721600 | bytes 16777216 | tf_op jit(solution)/shard_map/attend/pallas_call | solution.py:305
  45.6 1.3 copy-done.2
  47.0 0.7 copy-done.5
  47.6 0.6 copy-done.14
  48.2 39.8 %feed.1 = (f32[128,256]{1,0:T(8,128)}, f32[256,512]{1,0:T(8,128)}, f32[256,512]{1,0:T(8,128)}, f32[64,512]{1,0:T(8,128)}, f32[128,512]{1,0:T(8,128)}, /*index=5*/f32[16,512]{1,0:T(8,128)}) custom-call(f32[128,256]{1,0:T(8,128)} %copy-done.5, f32[256,512]{1,0:T(8,128)} %bitcast.33, f32[512,512]{1,0:T(8,128)} %refs_2_.1, f32[256,512]{1,0:T(8,128)} %bitcast.23, ...), custom_call_target="tpu_custom_call" | custom-call | tf_op jit(solution)/shard_map/feed/pallas_call | solution.py:149
  88.1 0.0 reduce-scatter.2.cloned.1.call-update
  88.1 0.2 all-reduce.2.cloned.1.call-start
  88.3 0.5 all-reduce.2.cloned.1.call-update
  88.8 0.0 copy-done
  88.9 0.0 copy-done.4
  88.9 0.0 copy-done.10
  88.9 0.0 copy-start.11
  88.9 0.0 copy-start.18
  88.9 32.5 %attend_back.1 = (f32[1,16,256,1024]{3,2,1,0:T(8,128)}, f32[1,16,256,1024]{3,2,1,0:T(8,128)}, f32[128,256]{1,0:T(8,128)}, f32[2,2,128,256]{3,2,1,0:T(8,128)}, f32[2,2,128,256]{3,2,1,0:T(8,128)}) custom-call(f32[1,16,256,1024]{3,2,1,0:T(8,128)} %pair.3, f32[1,16,256,1024]{3,2,1,0:T(8,128)} %cot.1, f32[128,256]{1,0:T(8,128)} %copy-done.10, ...), custom_call_target="tpu_custom_call" | custom-call | flops 3355443200 | bytes 67108864 | tf_op jit(solution)/shard_map/attend_back/pallas_call | solution.py:413
  121.4 0.0 reduce-scatter.2.cloned.1.call-done.refs_10_
  121.4 52.7 %finish.1 = (f32[256,512]{1,0:T(8,128)}, f32[4,2,64,512]{3,2,1,0:T(8,128)}, f32[4,2,128,512]{3,2,1,0:T(8,128)}, f32[16,512]{1,0:T(8,128)}, f32[1,1]{1,0:T(1,128)}) custom-call(f32[2,2,128,256]{3,2,1,0:T(8,128)} %get-tuple-element.71.refs_0_, f32[2,2,128,256]{3,2,1,0:T(8,128)} %get-tuple-element.72.refs_1_, f32[64,512]{1,0:T(8,128)} %get-tuple-element.73.refs_2_, ...), custom_call_target="tpu_custom_call" | custom-call | tf_op jit(solution)/shard_map/finish/pallas_call | solution.py:149
  174.2 0.0 all-reduce.2.cloned.1.call-done.refs_4_
  174.2 0.0 copy-done.11
  174.2 0.0 copy-done.18
  174.2 0.0 copy-start.3
  174.2 1.6 copy-done.3
  175.8 1.2 copy-done.6
  177.1 1.0 copy-done.12
  178.1 1.0 copy-done.13
  179.1 0.8 copy-done.15
  179.9 2.7 %place.1 = (f32[512,128]{1,0:T(8,128)}, f32[512,128]{1,0:T(8,128)}, f32[512,128]{1,0:T(8,128)}, f32[128,512]{1,0:T(8,128)}, f32[512,512]{1,0:T(8,128)}, /*index=...) custom-call(f32[4,2,64,512]{3,2,1,0:T(8,128)S(1)} %copy-done.6, ...), custom_call_target="tpu_custom_call" | custom-call | tf_op jit(solution)/shard_map/place/pallas_call | solution.py:149
  (11 shorter events, 0.0 us)
Async XLA Ops:
  7.2 41.1 %all-gather.2.cloned.1.call-start = ((), (), s32[]{:S(2)}) async-start(), calls=%async_computation.1 | async-start | bytes 1310720 | tf_op jit(solution)/shard_map/all_gather | solution.py:854
  7.9 113.5 %reduce-scatter.2.cloned.1.call-start = ((), (), s32[]{:S(2)}) async-start(), calls=%async_computation.2 | async-start | bytes 1310720 | tf_op jit(solution)/shard_map/reduce_scatter | solution.py:861
  8.0 1.0 copy-start.1
  9.0 0.9 copy-start.7
  10.0 0.9 copy-start.8
  10.9 0.9 copy-start.9
  11.9 0.7 copy-start.16
  12.6 0.7 copy-start.17
  13.2 0.7 copy-start.19
  13.9 0.7 copy-start.20
  14.6 0.7 copy-start.21
  28.5 60.4 %copy-start = (f32[4,264,256]{2,1,0:T(8,128)}, f32[4,264,256]{2,1,0:T(8,128)S(1)}, u32[]{:S(2)}) copy-start(f32[4,264,256]{2,1,0:T(8,128)S(1)} %get-tuple-element.63.keys.values.ids) | copy-start | bytes 3244036
  28.5 60.4 %copy-start.4 = (f32[256,128]{1,0:T(8,128)}, f32[256,128]{1,0:T(8,128)S(1)}, u32[]{:S(2)}) copy-start(f32[256,128]{1,0:T(8,128)S(1)} %get-tuple-element.64.id_column.refs_11_) | copy-start | bytes 393220
  28.5 60.4 %copy-start.10 = (f32[128,256]{1,0:T(8,128)}, f32[128,256]{1,0:T(8,128)S(1)}, u32[]{:S(2)}) copy-start(f32[128,256]{1,0:T(8,128)S(1)} %get-tuple-element.62.queries) | copy-start | bytes 393220
  45.6 1.3 copy-start.2
  47.0 0.7 copy-start.5
  47.6 0.6 copy-start.14
  88.1 86.1 %all-reduce.2.cloned.1.call-start = ((), (), s32[]{:S(2)}) async-start(), calls=%async_computation.3 | async-start | bytes 1048576 | tf_op jit(solution)/shard_map/psum | solution.py:862
  88.9 85.3 %copy-start.11 = (f32[256,512]{1,0:T(8,128)S(1)}, f32[256,512]{1,0:T(8,128)}, u32[]{:S(2)}) copy-start(f32[256,512]{1,0:T(8,128)} %get-tuple-element.81.refs_3_) | copy-start | bytes 1572868
  88.9 85.3 %copy-start.18 = (f32[512]{0:T(512)S(1)}, f32[512]{0:T(512)}, u32[]{:S(2)}) copy-start(f32[512]{0:T(512)} %param.37) | copy-start | bytes 6148
  174.2 1.6 copy-start.3
  175.8 1.2 copy-start.6
  177.1 1.0 copy-start.12
  178.1 1.0 copy-start.13
  179.1 0.8 copy-start.15
Sparse Core Ops, SparseCore 0:
  9.6 30.6 all-gather.1
  88.2 25.4 reduce-scatter.1
  116.2 53.4 all-reduce.1

commit v3 on v2

--- a/solution.py
+++ b/solution.py
@@ -81,11 +81,13 @@
     ).wait_recv()
 
 
+def greet(targets):
+    for target in targets:
+        pl.semaphore_signal(pltpu.get_barrier_semaphore(), inc=1, device_id=target, device_id_type=MESH)
+
+
 def meet(targets):
-    barrier = pltpu.get_barrier_semaphore()
-    for target in targets:
-        pl.semaphore_signal(barrier, inc=1, device_id=target, device_id_type=MESH)
-    pl.semaphore_wait(barrier, len(targets))
+    pl.semaphore_wait(pltpu.get_barrier_semaphore(), len(targets))
 
 
 def others(index, count):
@@ -127,16 +129,17 @@
             self.begun = True
 
 
-def staged_call(kernel, name, operands, results, scratch, megabytes, remote=None):
-    n_in, n_out = len(operands), len(results)
+def staged_call(kernel, name, operands, results, scratch, megabytes, remote=None, raw=()):
+    n_in, n_out, n_raw = len(operands), len(results), len(raw)
 
     def body(*refs):
-        sources, targets, refs = refs[:n_in], refs[n_in : n_in + n_out], refs[n_in + n_out :]
+        sources, left, refs = refs[:n_in], refs[n_in : n_in + n_raw], refs[n_in + n_raw :]
+        targets, refs = refs[:n_out], refs[n_out:]
         slots, made, refs = refs[:n_in], refs[n_in : n_in + n_out], refs[n_in + n_out :]
         in_sem, out_sem, refs = refs[0], refs[1], refs[2:]
         ins = [Operand(sources[n], slots[n], in_sem.at[n]) for n in range(n_in)]
         outs = [Result(targets[n], made[n], out_sem.at[n]) for n in range(n_out)]
-        kernel(ins, outs, refs)
+        kernel(ins, outs, refs, left)
         for operand in ins:
             operand.ref
         for result in outs:
@@ -144,12 +147,12 @@
         for result in outs:
             result.copy.wait()
 
-    anywhere = pl.BlockSpec(memory_space=pl.ANY)
+    anywhere = pl.BlockSpec(memory_space=pltpu.HBM)
     extra = {} if remote is None else {"collective_id": remote, "has_side_effects": True}
     return pl.pallas_call(
         body,
         out_shape=[jax.ShapeDtypeStruct(shape, F32) for shape in results],
-        in_specs=[anywhere] * n_in,
+        in_specs=[anywhere] * (n_in + n_raw),
         out_specs=[anywhere] * n_out,
         scratch_shapes=[pltpu.VMEM(value.shape, value.dtype) for value in operands]
         + [pltpu.VMEM(shape, F32) for shape in results]
@@ -157,64 +160,15 @@
         + list(scratch),
         compiler_params=pltpu.CompilerParams(vmem_limit_bytes=megabytes << 20, **extra),
         name=name,
-    )(*operands)
-
-
-def project_kernel(operands, results, scratch):
-    atoms, ids, gain, bias, w_key, w_value, b_value, w_query, b_query = operands
-    queries, kept, id_column = results
-    send_sem, recv_sem = scratch
-    blocks, feats = kept.shape[0], w_query.shape[1]
-    rows = atoms.shape[0]
-    chips = blocks // 2
-    blk = lax.axis_index("blk")
-    core, chip = lax.rem(blk, 2), lax.div(blk, 2)
-    sibling = blk + 1 - 2 * core
-    far = [step * 2 + core for step in others(chip, chips)]
-    meet([{"blk": peer} for peer in [sibling] + far])
-    normal, _ = normalize(atoms[...])
-    normed = halves(normal * gain[...] + bias[...])
-    kept[blk, 0:feats, :] = dot_halves(normed, halves(w_key[...])).T
-    kept[blk, feats : 2 * feats, :] = (dot_halves(normed, halves(w_value[...])) + b_value[...]).T
-    id_row = ids[...].astype(F32)
-    kept[blk, 2 * feats : 2 * feats + 8, :] = jnp.broadcast_to(id_row, (8, rows))
-    copies = [
-        send(kept.at[blk], kept.at[blk], send_sem.at[place], recv_sem.at[blk], {"blk": peer})
-        for place, peer in enumerate([sibling] + far)
-    ]
-    id_column[...] = jnp.broadcast_to(id_row, (LANES, rows)).T
-    queries[...] = (
-        (dot_halves(normed, halves(w_query[...])) + b_query[...]) * (DH ** (-0.5))
-    ).T
-    for place, source in enumerate(far):
-        arrived(kept.at[source], recv_sem.at[source])
-        copies.append(
-            send(
-                kept.at[source], kept.at[source], send_sem.at[chips + place], recv_sem.at[source],
-                {"blk": sibling},
-            )
-        )
-    for source in [sibling] + [peer + 1 - 2 * core for peer in far]:
-        arrived(kept.at[source], recv_sem.at[source])
-    for copy in copies:
-        copy.wait_send()
-
-
-def project(blocks, *operands):
-    rows, feats = operands[0].shape[0], operands[4].shape[1]
-    return staged_call(
-        project_kernel,
-        "project",
-        operands,
-        [(feats, rows), (blocks, 2 * feats + 8, rows), (rows, LANES)],
-        [pltpu.SemaphoreType.DMA((blocks,)), pltpu.SemaphoreType.DMA((blocks,))],
-        32,
-        remote=0,
-    )
+    )(*operands, *raw)
 
 
 def whole_row(ref, low, count):
     return jnp.concatenate([ref[n, low : low + count, :] for n in range(ref.shape[0])], axis=1)
+
+
+def joined(pieces):
+    return jnp.concatenate(list(pieces), axis=1)
 
 
 def stacked(parts):
@@ -226,25 +180,16 @@
     return high, value - high
 
 
-def attend_kernel(
-    pair, queries, keys, values, ids, id_column,
-    mixed, log_sums, squares, id_row, score, high, low,
-):
+def attend_group(pair, queries, keys, values, id_column, id_row, log_sums, first, score, high, low):
     group, rows, cols = score.shape
     strips = rows // STRIP
     chunk = min(CHUNK, cols)
-
-    @pl.when(pl.program_id(0) == 0)
-    def _():
-        squares[...] = jnp.zeros_like(squares)
-        one = whole_row(ids, 0, 8)
-        id_row[...] = jnp.concatenate([one, one], axis=0)
-
+    mixed = []
     for g in range(group):
         head = slice(8 * g, 8 * g + 8)
         q_high, q_low = wide_halves(queries[head, :])
-        k_high, k_low = wide_halves(whole_row(keys, 8 * g, 8))
-        v_high, v_low = wide_halves(whole_row(values, 8 * g, 8))
+        k_high, k_low = wide_halves(keys[head, :])
+        v_high, v_low = wide_halves(values[head, :])
         ones = jnp.ones_like(v_high)
         q_pack = stacked([q_high, q_high, q_low, q_low])
         k_pack = stacked([k_high, k_low, k_high, k_low])
@@ -258,9 +203,8 @@
                 own = id_column[line, :]
                 for j in range(start, start + chunk, LANES):
                     tile = pl.ds(j, LANES)
-                    value = score[g, line, tile]
-                    squares[line, tile] += value * value
-                    value = jnp.where(own == id_row[:, tile], pair[0, g, line, tile] + value, MASK_FILL)
+                    value = pair[g, line, tile] + score[g, line, tile]
+                    value = jnp.where(own == id_row[:, tile], value, MASK_FILL)
                     score[g, line, tile] = value
                     tops[s] = value if tops[s] is None else jnp.maximum(tops[s], value)
         tops = [
@@ -283,8 +227,9 @@
             gathered = term if gathered is None else gathered + term
         for s in range(strips):
             total = jnp.sum(totals[s], axis=1, keepdims=True)
-            log_sums[g, pl.ds(s * STRIP, STRIP), :] = tops[s] + jnp.log(total)
-        mixed[head, :] = (gathered[0:8] + gathered[8:16]) / gathered[16:17]
+            log_sums[first + g, pl.ds(s * STRIP, STRIP), :] = tops[s] + jnp.log(total)
+        mixed.append((gathered[0:8] + gathered[8:16]) / gathered[16:17])
+    return jnp.concatenate(mixed, axis=0)
 
 
 def head_specs(kept_shape, feats, group):
@@ -295,49 +240,6 @@
         pl.BlockSpec((blocks, 8 * group, rows), lambda h: (0, first + h, 0)),
         pl.BlockSpec((blocks, 8, rows), lambda h: (0, 2 * feats // 8, 0)),
     )
-
-
-def attend(pair, queries, kept, id_column):
-    _, heads, rows, cols = pair.shape
-    group = GROUP
-    feats = heads * DH
-    keys, values, ids = head_specs(kept.shape, feats, group)
-    return pl.pallas_call(
-        attend_kernel,
-        grid=(heads // group,),
-        in_specs=[
-            pl.BlockSpec((1, group, rows, cols), lambda h: (0, h, 0, 0)),
-            pl.BlockSpec((8 * group, rows), lambda h: (h, 0)),
-            keys,
-            values,
-            ids,
-            pl.BlockSpec((rows, LANES), lambda h: (0, 0)),
-        ],
-        out_specs=[
-            pl.BlockSpec((8 * group, rows), lambda h: (h, 0)),
-            pl.BlockSpec((group, rows, LANES), lambda h: (h, 0, 0)),
-            pl.BlockSpec((rows, cols), lambda h: (0, 0)),
-            pl.BlockSpec((STRIP, cols), lambda h: (0, 0)),
-        ],
-        out_shape=[
-            jax.ShapeDtypeStruct((feats, rows), F32),
-            jax.ShapeDtypeStruct((heads, rows, LANES), F32),
-            jax.ShapeDtypeStruct((rows, cols), F32),
-            jax.ShapeDtypeStruct((STRIP, cols), F32),
-        ],
-        scratch_shapes=[
-            pltpu.VMEM((group, rows, cols), F32),
-            pltpu.VMEM((group, rows, cols), BF16),
-            pltpu.VMEM((group, rows, cols), BF16),
-        ],
-        compiler_params=pltpu.CompilerParams(vmem_limit_bytes=48 << 20),
-        cost_estimate=pl.CostEstimate(
-            flops=2 * 200 * heads * rows * cols,
-            bytes_accessed=4 * heads * rows * cols,
-            transcendentals=heads * rows * cols,
-        ),
-        name="attend",
-    )(pair, queries, kept, kept, kept, id_column)
 
 
 def attend_back_kernel(
@@ -449,38 +351,161 @@
     return {"dp": lax.div(team, chips), "blk": lax.rem(team, chips) * 2 + core}
 
 
-def feed_kernel(operands, results, scratch):
-    mixed, cot, w_down, atoms, w_up, w_out, b_out, gain, bias, b_up = operands
-    d_mixed, hidden, down, d_hidden, grad_share, small = results
+def front_kernel(operands, results, scratch, raw):
     (
-        mixed_all, normal_two, rate_two, part, landed, back, back_landed, grads, sib_grads, go_grads, got_grads,
+        atoms, ids, gain_one, bias_one, w_key, w_value, b_value, w_query, b_query, w_out, cot, w_down, w_up, b_out,
+        gain, bias, b_up,
+    ) = operands
+    (pair,) = raw
+    (
+        queries, kept, id_column, log_sums, mixed, id_row, d_mixed, hidden, down, d_hidden, grad_share, small,
+    ) = results
+    (
+        pair_buf, score, high, low, q_part, q_land, q_all, k_all, w_all, squares, mixed_all, normal_two, rate_two,
+        part, landed, back, back_landed, grads, sib_grads, go_grads, got_grads,
+        pair_sem, kept_send, kept_recv, kz_send, kf_send, ks_send, k_recv, q_send, q_recv, w_send, wf_send, w_recv,
         mix_send, mix_recv, part_send, part_recv, back_send, back_recv, sib_send, sib_recv, g_send, g_recv,
     ) = scratch
     zs, feats, rows = mixed_all.shape
+    blocks = kept.shape[0]
+    chips = blocks // 2
     teams, _, share, width = grads.shape
-    chips = teams // lax.axis_size("dp")
+    _, group, _, cols = pair_buf.shape
+    heads = feats // DH
+    groups = heads // group
     piece = rows // zs
     z, blk = lax.axis_index("head"), lax.axis_index("blk")
     core, chip = lax.rem(blk, 2), lax.div(blk, 2)
     team = lax.axis_index("dp") * chips + chip
-    sibling = {"blk": blk + 1 - 2 * core}
+    other_core = 1 - core
+    sib_blk = blk + 1 - 2 * core
+    sibling = {"blk": sib_blk}
     peers, far_teams = others(z, zs), others(team, teams)
-    meet([{"head": peer} for peer in peers] + [sibling] + [team_device(peer, core, chips) for peer in far_teams])
+    far = [step * 2 + core for step in others(chip, chips)]
+    far_siblings = [step * 2 + other_core for step in others(chip, chips)]
+    mine = pl.ds(pl.multiple_of(z * piece, 8), piece)
+
+    def pair_copy(index, slot):
+        return pltpu.make_async_copy(
+            pair.at[0, pl.ds(index * group, group)], pair_buf.at[slot], pair_sem.at[slot]
+        )
+
+    meeting = [{"head": peer} for peer in peers] + [sibling]
+    meeting += [team_device(peer, core, chips) for peer in far_teams]
+    greet(meeting)
+    for n in range(2):
+        pair_copy(n, n).start()
+
+    normal, _ = normalize(atoms[...])
+    normed = halves(normal * gain_one[...] + bias_one[...])
+    kept[blk, 0:feats, :] = dot_halves(normed, halves(w_key[...])).T
+    kept[blk, feats : 2 * feats, :] = (dot_halves(normed, halves(w_value[...])) + b_value[...]).T
+    id_line = ids[...].astype(F32)
+    kept[blk, 2 * feats : 2 * feats + 8, :] = jnp.broadcast_to(id_line, (8, rows))
+    meet(meeting)
     copies = [
-        send(mixed.source, mixed_all.at[z], mix_send.at[n], mix_recv.at[z], {"head": peer})
+        send(kept.at[blk], kept.at[blk], kept_send.at[n], kept_recv.at[blk], {"blk": peer})
+        for n, peer in enumerate([sib_blk] + far)
+    ]
+    copies += [
+        send(kept.at[blk, 0:feats], k_all.at[blk, z], kz_send.at[n], k_recv.at[blk, z], {"head": peer})
         for n, peer in enumerate(peers)
     ]
-    mine = pl.ds(pl.multiple_of(z * piece, 8), piece)
+    q_rows = (dot_halves(normed, halves(w_query[...])) + b_query[...]) * (DH ** (-0.5))
+    q_part[...] = q_rows.reshape(zs, piece, feats)
+    copies += [
+        send(q_part.at[peer], q_land.at[z], q_send.at[n], q_recv.at[z], {"head": peer})
+        for n, peer in enumerate(peers)
+    ]
+    half = feats // 2
+    w_mine = w_out.source.at[pl.ds(pl.multiple_of(core * half, 8), half)]
+    copies += [
+        send(w_mine, w_all.at[z, core], w_send.at[n], w_recv.at[z, core], {"head": peer})
+        for n, peer in enumerate(peers)
+    ]
+    queries[...] = q_rows.T
+    queries.flush()
+    q_land[z] = q_part[z]
+    w_all[z] = w_out[...].reshape(2, half, width)
+    id_column[...] = jnp.broadcast_to(id_line, (LANES, rows)).T
+    id_column.flush()
     small[...] = jnp.zeros(small.shape, F32)
+    for n, source in enumerate(far):
+        arrived(kept.at[source], kept_recv.at[source])
+        copies.append(
+            send(kept.at[source], kept.at[source], kept_send.at[chips + n], kept_recv.at[source], sibling)
+        )
+    for source in [sib_blk] + far_siblings:
+        arrived(kept.at[source], kept_recv.at[source])
+    kept.flush()
+    one = joined(kept[n, 2 * feats : 2 * feats + 8, :] for n in range(blocks))
+    id_row[...] = jnp.concatenate([one, one], axis=0)
+    id_row.flush()
+
+    def mix_copies(index):
+        some = pl.ds(pl.multiple_of(index * (8 * group), 8 * group), 8 * group)
+        return [
+            pltpu.make_async_remote_copy(
+                src_ref=mixed.at[some],
+                dst_ref=mixed_all.at[z, some],
+                send_sem=mix_send.at[n, index],
+                recv_sem=mix_recv.at[z, index],
+                device_id={"head": peer},
+                device_id_type=MESH,
+            )
+            for n, peer in enumerate(peers)
+        ]
+
+    def step(index, carry):
+        slot = lax.rem(index, 2)
+        pair_copy(index, slot).wait()
+        low_row = pl.multiple_of(index * (8 * group), 8 * group)
+        some = pl.ds(low_row, 8 * group)
+        values = pl.ds(pl.multiple_of(feats + low_row, 8), 8 * group)
+        mixed[some, :] = attend_group(
+            pair_buf.at[slot],
+            queries[some, :],
+            joined(kept[n, some, :] for n in range(blocks)),
+            joined(kept[n, values, :] for n in range(blocks)),
+            id_column, id_row, log_sums, index * group, score, high, low,
+        )
+        for copy in mix_copies(index):
+            copy.start()
+
+        @pl.when(index + 2 < groups)
+        def _():
+            pair_copy(index + 2, slot).start()
+
+        return carry
+
+    lax.fori_loop(0, groups, step, 0)
+    mixed.flush()
+    log_sums.flush()
+    for n, peer in enumerate(peers):
+        ready = w_all.at[peer, core]
+        arrived(ready, w_recv.at[peer, core])
+        copies.append(send(ready, ready, wf_send.at[n], w_recv.at[peer, core], sibling))
+    for n, peer in enumerate(peers):
+        ready = k_all.at[blk, peer]
+        arrived(ready, k_recv.at[blk, peer])
+        copies += [
+            send(ready, ready, kf_send.at[n, m], k_recv.at[blk, peer], {"blk": target})
+            for m, target in enumerate([sib_blk] + far)
+        ]
+
     small[SMALL_B_DOWN : SMALL_B_DOWN + 1, :] = column_sum(cot[mine, :])
     cots = halves(cot[...])
     downs = halves(w_down[...])
     d_act = dot_halves(cots, downs, NT)
     ups = halves(w_up[...])
-    outs = halves(w_out[...])
+    for peer in peers:
+        arrived(w_all.at[peer, other_core], w_recv.at[peer, other_core])
+    outs = halves(w_all[...].reshape(zs * feats, width))
     mixed_all[z] = mixed[...]
     for peer in peers:
-        arrived(mixed_all.at[peer], mix_recv.at[peer])
+        for index in range(groups):
+            some = pl.ds(index * (8 * group), 8 * group)
+            arrived(mixed_all.at[peer, some], mix_recv.at[peer, index])
     mixed_rows = mixed_all[...].reshape(zs * feats, rows).T
     hidden_rows = atoms[...] + dot_halves(halves(mixed_rows), outs) + b_out[...]
     hidden[...] = hidden_rows
@@ -503,7 +528,12 @@
     grad_up = dot_halves(halves(d_pre.T), halves(normed))
     grad_down = dot_halves(halves(act.T), cots)
     grads[...] = jnp.concatenate([grad_up, grad_down], axis=0).reshape(grads.shape)
-    copies.append(send(grads.at[:, 1 - core], sib_grads, sib_send.at[0], sib_recv.at[0], sibling))
+    copies.append(send(grads.at[:, other_core], sib_grads, sib_send.at[0], sib_recv.at[0], sibling))
+    for n, source in enumerate(far):
+        for m, peer in enumerate(peers):
+            ready = k_all.at[source, peer]
+            arrived(ready, k_recv.at[source, peer])
+            copies.append(send(ready, ready, ks_send.at[n, m], k_recv.at[source, peer], sibling))
     down[...] = dot_halves(halves(act), downs)
     down.flush()
     small[SMALL_B_UP : SMALL_B_UP + 1, 0 : d_pre.shape[1]] = column_sum(d_pre)
@@ -516,6 +546,49 @@
         for n, peer in enumerate(far_teams)
     ]
     got_grads[team] = go_grads[team]
+    for peer in peers:
+        arrived(q_land.at[peer], q_recv.at[peer])
+    for n in range(zs):
+        q_all[n] = q_land[n].T
+    for n in range(blocks):
+        k_all[n, z] = kept[n, 0:feats, :]
+    for source in [sib_blk] + far_siblings:
+        for peer in peers:
+            arrived(k_all.at[source, peer], k_recv.at[source, peer])
+    squares[...] = jnp.zeros(squares.shape, F32)
+    at_once = 4
+    rounds = heads // at_once
+
+    def square_step(index, carry):
+        there = lax.div(index, rounds)
+        some = pl.ds(pl.multiple_of(lax.rem(index, rounds) * (8 * at_once), 8 * at_once), 8 * at_once)
+        q_some = q_all[there, some, :]
+        k_some = joined(k_all[n, there, some, :] for n in range(blocks))
+        added = None
+        for h in range(at_once):
+            head = slice(8 * h, 8 * h + 8)
+            q_high, q_low = wide_halves(q_some[head])
+            k_high, k_low = wide_halves(k_some[head])
+            value = dot(
+                stacked([q_high, q_high, q_low, q_low]), stacked([k_high, k_low, k_high, k_low]), TN
+            )
+            added = value * value if added is None else added + value * value
+        squares[...] += added
+        return carry
+
+    lax.fori_loop(0, zs * rounds, square_step, 0)
+    same = id_column[mine, 0:1] == id_row[0:1, :]
+    norms = jnp.sqrt(squares[...] + 1.0)
+    terms = jnp.where(same, jnp.log1p(jnp.exp(norms - math.sqrt(zs * heads))), 0.0)
+    number = jnp.where(same, 1.0, 0.0)
+
+    def total(value):
+        return jnp.sum(jnp.sum(value, axis=1, keepdims=True), axis=0, keepdims=True)
+
+    lane = lax.broadcasted_iota(jnp.int32, (1, width), 1)
+    small[SMALL_PENALTY : SMALL_PENALTY + 1, :] = jnp.where(
+        lane == 0, total(terms), jnp.where(lane == 1, total(number), 0.0)
+    )
     for peer in peers:
         arrived(landed.at[peer], part_recv.at[peer])
     d_normed = functools.reduce(jnp.add, [landed[n] for n in range(zs)])
@@ -546,40 +619,69 @@
     for copy in copies:
         copy.wait_send()
 
-
-def feed(zs, teams, *operands):
-    feats, rows = operands[0].shape
-    width, units = operands[4].shape
-    piece = rows // zs
-    share = units // teams
+    def drain(index, carry):
+        for copy in mix_copies(index):
+            copy.wait_send()
+        return carry
+
+    lax.fori_loop(0, groups, drain, 0)
+
+
+def front(zs, teams, pair, *operands):
+    _, heads, rows, cols = pair.shape
+    feats, blocks = heads * DH, cols // rows
+    width, units = operands[0].shape[1], operands[12].shape[1]
+    piece, share, group = rows // zs, units // teams, GROUP
+    groups = heads // group
     slab = pltpu.VMEM((zs, piece, width), F32)
     narrow = pltpu.VMEM((zs, piece, feats), F32)
     one = pltpu.VMEM((teams, share, width), F32)
     dma = pltpu.SemaphoreType.DMA
     return staged_call(
-        feed_kernel,
-        "feed",
+        front_kernel,
+        "front",
         operands,
-        [(feats, rows), (rows, width), (rows, width), (piece, width), (share, width), (SMALL_ROWS, width)],
         [
+            (feats, rows), (blocks, 2 * feats + 8, rows), (rows, LANES), (heads, rows, LANES), (feats, rows),
+            (STRIP, cols), (feats, rows), (rows, width), (rows, width), (piece, width), (share, width),
+            (SMALL_ROWS, width),
+        ],
+        [
+            pltpu.VMEM((2, group, rows, cols), F32),
+            pltpu.VMEM((group, rows, cols), F32),
+            pltpu.VMEM((group, rows, cols), BF16),
+            pltpu.VMEM((group, rows, cols), BF16),
+            narrow, narrow,
+            pltpu.VMEM((zs, feats, piece), F32),
+            pltpu.VMEM((blocks, zs, feats, rows), F32),
+            pltpu.VMEM((zs, 2, feats // 2, width), F32),
+            pltpu.VMEM((piece, cols), F32),
             pltpu.VMEM((zs, feats, rows), F32),
             pltpu.VMEM((rows, width), F32),
             pltpu.VMEM((rows, LANES), F32),
             slab, slab, narrow, narrow,
             pltpu.VMEM((teams, 2, share, width), F32),
             one, one, one,
-        ]
-        + [dma((zs,))] * 6
-        + [dma((1,)), dma((1,)), dma((teams,)), dma((teams,))],
-        56,
-        remote=1,
-    )
-
-
-def finish_kernel(operands, results, scratch):
+            dma((2,)),
+            dma((blocks,)), dma((blocks,)),
+            dma((zs,)), dma((zs, blocks // 2)), dma((blocks // 2, zs)), dma((blocks, zs)),
+            dma((zs,)), dma((zs,)),
+            dma((zs,)), dma((zs,)), dma((zs, 2)),
+            dma((zs, groups)), dma((zs, groups)),
+            dma((zs,)), dma((zs,)),
+            dma((zs,)), dma((zs,)),
+            dma((1,)), dma((1,)),
+            dma((teams,)), dma((teams,)),
+        ],
+        58,
+        remote=0,
+        raw=(pair,),
+    )
+
+
+def finish_kernel(operands, results, scratch, raw):
     (
-        d_keys, d_values, d_hidden, share_in, d_queries, atoms, gain, bias, w_query, mixed, squares, id_column,
-        id_row, small_in, w_key, w_value,
+        d_keys, d_values, d_hidden, share_in, d_queries, atoms, gain, bias, w_query, mixed, small_in, w_key, w_value,
     ) = operands
     grad_atoms, total_grads, total_big, small, penalty = results
     (
@@ -603,7 +705,9 @@
     place = team * 2 + core
     far_places = others(place, teams * 2)
     plane = [team_device(lax.div(value, 2), lax.rem(value, 2), chips) for value in far_places]
-    meet([{"head": peer} for peer in peers] + plane)
+    meeting = [{"head": peer} for peer in peers] + plane
+    greet(meeting)
+    meet(meeting)
     copies = [
         send(d_keys.source.at[:, other_core], sib_keys, sib_send.at[0], sib_recv.at[0], sibling),
         send(d_values.source.at[:, other_core], sib_values, sib_send.at[1], sib_recv.at[1], sibling),
@@ -638,20 +742,7 @@
     d_normed = dot_full(dq_rows, w_query[...], NT)
     grad_q = dot_halves(halves(d_queries[...]), normed)
     mine = pl.ds(pl.multiple_of(z * piece, 8), piece)
-    own = id_column[mine, 0:1]
-    same = own == id_row[0:1, :]
-    norms = jnp.sqrt(squares[...] + 1.0)
-    terms = jnp.where(same, jnp.log1p(jnp.exp(norms - math.sqrt(zs * feats // DH))), 0.0)
-    number = jnp.where(same, 1.0, 0.0)
-
-    def total(value):
-        return jnp.sum(jnp.sum(value, axis=1, keepdims=True), axis=0, keepdims=True)
-
-    lane = lax.broadcasted_iota(jnp.int32, (1, width), 1)
     small_z[z] = small_in[0:8, :]
-    small_z[z, SMALL_PENALTY : SMALL_PENALTY + 1, :] = jnp.where(
-        lane == 0, total(terms), jnp.where(lane == 1, total(number), 0.0)
-    )
     hidden_all[z] = d_hidden[...]
     for peer in far_chips:
         arrived(got_keys.at[peer], kv_recv.at[0, peer])
@@ -788,7 +879,7 @@
     )
 
 
-def place_kernel(operands, results, scratch):
+def place_kernel(operands, results, scratch, raw):
     total_grads, total_big, small, hidden, down, b_down, rows_in = operands
     grad_query, grad_key, grad_value, grad_out, grad_up, grad_down, out_atoms, grad_atoms = results[:8]
     feats, units = grad_out.shape[0], grad_down.shape[0]
@@ -847,18 +938,13 @@
     def line(value):
         return value.reshape(1, -1)
 
-    queries, kept, id_column = project(
-        blocks, inputs, mol_ids, line(ln1_gain), line(ln1_bias), w_key, w_value, line(b_value), w_query,
-        line(b_query),
-    )
-    w_out_all = lax.all_gather(w_out, "head", axis=0, tiled=True)
-    mixed, log_sums, squares, id_row = attend(pair, queries, kept, id_column)
-    d_mixed, hidden, down, d_hidden, grad_share, small = feed(
-        zs, dps * blocks // 2,
-        mixed, cot, w_down, inputs, w_up, w_out_all, line(b_out), line(ln2_gain), line(ln2_bias), line(b_up),
-    )
-    squares, d_mixed = lax.optimization_barrier((squares, d_mixed))
-    squares = lax.psum_scatter(squares, "head", scatter_dimension=0, tiled=True)
+    (
+        queries, kept, id_column, log_sums, mixed, id_row, d_mixed, hidden, down, d_hidden, grad_share, small,
+    ) = front(
+        zs, dps * blocks // 2, pair,
+        inputs, mol_ids, line(ln1_gain), line(ln1_bias), w_key, w_value, line(b_value), w_query, line(b_query),
+        w_out, cot, w_down, w_up, line(b_out), line(ln2_gain), line(ln2_bias), line(b_up),
+    )
     down = lax.psum(down, "head")
     out_pair, grad_pair, d_queries, d_keys, d_values = attend_back(
         pair, cot_pair, queries, kept, mixed, d_mixed, log_sums, id_column, id_row
@@ -866,7 +952,7 @@
     grad_atoms, total_grads, total_big, small, penalty = finish(
         zs, dps,
         d_keys, d_values, d_hidden, grad_share, d_queries, inputs, line(ln1_gain), line(ln1_bias), w_query, mixed,
-        squares, id_column, id_row, small, w_key, w_value,
+        small, w_key, w_value,
     )
     placed = place(
         w_query.shape[1], w_up.shape[1],

time: 192 us -> 168 us (0.88)
  Pallas kernels: 158 us -> 146 us
  local copies, waits for them, and re-layouts: 15.5 us -> 5.66 us
    pallas_call x1 -> x0, Pallas kernels: 17.1 us -> none  [attend(): pl.pallas_call(attend_kernel, grid=(heads // group,), in_specs=[pl.BlockS...]
    unnamed x44 -> x14, local copies, waits for them, and re-layouts: 15.5 us -> 5.66 us
    pallas_call x4 -> x3, Pallas kernels: 109 us -> 113 us  [staged_call(): pl.pallas_call(body, out_shape=[jax.ShapeDtypeStruct(shape, F32) for shap...]
  transfers between devices with their start and end apart: 3 -> 1, of which waited for: 0 -> 0; matrix products, arithmetic and copies ran while one was open for 0% -> 0% of each run, Pallas kernels for 61% -> 46%
where the time goes in v3:
time: 168 us; the launch traced here: 167 us
  Pallas kernels  146 us (87%)
  between operations  15.9 us (9%)
  local copies, waits for them, and re-layouts  5.66 us (3%)
    pallas_call x3, Pallas kernels, staged_call(): pl.pallas_call(body, out_shape=[jax.ShapeDtypeStruct(shape, F32) for shap...  113 us
    pallas_call x1, Pallas kernels, attend_back(): pl.pallas_call(attend_back_kernel, grid=(heads // group,), in_specs=[big,...  32.6 us
    unnamed x14, local copies, waits for them, and re-layouts  5.66 us
  transfers between devices with their start and end apart: 1, of which 0 were waited for; matrix products, arithmetic and copies ran while one was open for 0% of the time, Pallas kernels for 46%

profile of v3, /device:TPU:0, one launch (start us, length us, event | category | flops | bytes accessed | tf_op | source)
XLA Modules:
  0.0 167.4 jit_solution(445172791040305677)
XLA Ops:
  7.2 0.0 all-reduce.2.cloned.1.call-start
  7.2 65.6 %front.1 = (f32[128,256]{1,0:T(8,128)}, f32[4,264,256]{2,1,0:T(8,128)}, f32[256,128]{1,0:T(8,128)}, f32[16,256,128]{2,1,0:T(8,128)}, f32[128,256]{1,0:T(8,128)},...) custom-call(f32[256,512]{1,0:T(8,128)} %bitcast.24, ...), custom_call_target="tpu_custom_call" | custom-call | tf_op jit(solution)/shard_map/front/pallas_call | solution.py:152
  72.8 0.0 all-reduce.2.cloned.1.call-update
  72.9 0.0 copy-start.2
  72.9 0.0 copy-start.6
  72.9 32.6 %attend_back.1 = (f32[1,16,256,1024]{3,2,1,0:T(8,128)}, f32[1,16,256,1024]{3,2,1,0:T(8,128)}, f32[128,256]{1,0:T(8,128)}, f32[2,2,128,256]{3,2,1,0:T(8,128)}, f32[2,2,128,256]{3,2,1,0:T(8,128)}) custom-call(f32[1,16,256,1024]{3,2,1,0:T(8,128)} %pair.1, f32[1,16,256,1024]{3,2,1,0:T(8,128)} %cot.1, f32[128,256]{1,0:T(8,128)} %get-tuple-element.59.queries, ...), custom_call_target="tpu_custom_call" | custom-call | flops 3355443200 | bytes 67108864 | tf_op jit(solution)/shard_map/attend_back/pallas_call | solution.py:315
  105.4 44.9 %finish.1 = (f32[256,512]{1,0:T(8,128)}, f32[4,2,64,512]{3,2,1,0:T(8,128)}, f32[4,2,128,512]{3,2,1,0:T(8,128)}, f32[16,512]{1,0:T(8,128)}, f32[1,1]{1,0:T(1,128)}) custom-call(f32[2,2,128,256]{3,2,1,0:T(8,128)} %get-tuple-element.66.refs_0_, f32[2,2,128,256]{3,2,1,0:T(8,128)} %get-tuple-element.67.refs_1_, f32[64,512]{1,0:T(8,128)} %get-tuple-element.68.refs_2_, ...), custom_call_target="tpu_custom_call" | custom-call | tf_op jit(solution)/shard_map/finish/pallas_call | solution.py:152
  150.3 0.0 all-reduce.2.cloned.1.call-done.refs_4_
  150.3 0.0 copy-done.2
  150.4 0.0 copy-done.6
  150.4 0.0 copy-start
  150.4 1.6 copy-done
  152.0 0.0 copy-start.1
  152.0 1.2 copy-done.1
  153.2 0.0 copy-start.3
  153.2 1.0 copy-done.3
  154.2 0.0 copy-start.4
  154.2 1.0 copy-done.4
  155.3 0.0 copy-start.5
  155.3 0.8 copy-done.5
  156.0 2.7 %place.1 = (f32[512,128]{1,0:T(8,128)}, f32[512,128]{1,0:T(8,128)}, f32[512,128]{1,0:T(8,128)}, f32[128,512]{1,0:T(8,128)}, f32[512,512]{1,0:T(8,128)}, /*index=...) custom-call(f32[4,2,64,512]{3,2,1,0:T(8,128)S(1)} %copy-done.1, ...), custom_call_target="tpu_custom_call" | custom-call | tf_op jit(solution)/shard_map/place/pallas_call | solution.py:152
Async XLA Ops:
  7.2 143.1 %all-reduce.2.cloned.1.call-start = ((), (), s32[]{:S(2)}) async-start(), calls=%async_computation | async-start | bytes 1048576 | tf_op jit(solution)/shard_map/psum | solution.py:948
  72.9 77.5 %copy-start.2 = (f32[256,512]{1,0:T(8,128)S(1)}, f32[256,512]{1,0:T(8,128)}, u32[]{:S(2)}) copy-start(f32[256,512]{1,0:T(8,128)} %get-tuple-element.75.refs_3_) | copy-start | bytes 1572868
  72.9 77.5 %copy-start.6 = (f32[512]{0:T(512)S(1)}, f32[512]{0:T(512)}, u32[]{:S(2)}) copy-start(f32[512]{0:T(512)} %param.37) | copy-start | bytes 6148
  150.4 1.6 copy-start
  152.0 1.2 copy-start.1
  153.2 1.0 copy-start.3
  154.2 1.0 copy-start.4
  155.3 0.8 copy-start.5
Sparse Core Ops, SparseCore 0:
  73.0 37.3 all-reduce.1

commit v4 on v3

--- a/solution.py
+++ b/solution.py
@@ -129,42 +129,50 @@
             self.begun = True
 
 
-def staged_call(kernel, name, operands, results, scratch, megabytes, remote=None, raw=()):
-    n_in, n_out, n_raw = len(operands), len(results), len(raw)
+def staged_call(kernel, name, operands, results, scratch, megabytes, remote=None, raw=(), straight=()):
+    n_in, n_out, n_raw, n_straight = len(operands), len(results), len(raw), len(straight)
 
     def body(*refs):
         sources, left, refs = refs[:n_in], refs[n_in : n_in + n_raw], refs[n_in + n_raw :]
+        moved, refs = refs[:n_straight], refs[n_straight:]
+        arrays, refs = refs[:n_straight], refs[n_straight:]
         targets, refs = refs[:n_out], refs[n_out:]
         slots, made, refs = refs[:n_in], refs[n_in : n_in + n_out], refs[n_in + n_out :]
-        in_sem, out_sem, refs = refs[0], refs[1], refs[2:]
+        in_sem, out_sem, move_sem, refs = refs[0], refs[1], refs[2], refs[3:]
+        through, refs = refs[:n_straight], refs[n_straight:]
+        loads = [pltpu.make_async_copy(moved[n], through[n], move_sem.at[n]) for n in range(n_straight)]
+        moves = [pltpu.make_async_copy(through[n], arrays[n], move_sem.at[n]) for n in range(n_straight)]
+        for load in loads:
+            load.start()
         ins = [Operand(sources[n], slots[n], in_sem.at[n]) for n in range(n_in)]
         outs = [Result(targets[n], made[n], out_sem.at[n]) for n in range(n_out)]
+        for load, move in zip(loads, moves, strict=True):
+            load.wait()
+            move.start()
         kernel(ins, outs, refs, left)
         for operand in ins:
             operand.ref
         for result in outs:
             result.flush()
-        for result in outs:
-            result.copy.wait()
+        for copy in moves + [result.copy for result in outs]:
+            copy.wait()
 
     anywhere = pl.BlockSpec(memory_space=pltpu.HBM)
     extra = {} if remote is None else {"collective_id": remote, "has_side_effects": True}
     return pl.pallas_call(
         body,
-        out_shape=[jax.ShapeDtypeStruct(shape, F32) for shape in results],
-        in_specs=[anywhere] * (n_in + n_raw),
-        out_specs=[anywhere] * n_out,
+        out_shape=[jax.ShapeDtypeStruct(value.shape, value.dtype) for value in straight]
+        + [jax.ShapeDtypeStruct(shape, F32) for shape in results],
+        in_specs=[anywhere] * (n_in + n_raw + n_straight),
+        out_specs=[anywhere] * (n_straight + n_out),
         scratch_shapes=[pltpu.VMEM(value.shape, value.dtype) for value in operands]
         + [pltpu.VMEM(shape, F32) for shape in results]
-        + [pltpu.SemaphoreType.DMA((n_in,)), pltpu.SemaphoreType.DMA((n_out,))]
+        + [pltpu.SemaphoreType.DMA((n,)) for n in (n_in, n_out, max(1, n_straight))]
+        + [pltpu.VMEM(value.shape, value.dtype) for value in straight]
         + list(scratch),
         compiler_params=pltpu.CompilerParams(vmem_limit_bytes=megabytes << 20, **extra),
         name=name,
-    )(*operands, *raw)
-
-
-def whole_row(ref, low, count):
-    return jnp.concatenate([ref[n, low : low + count, :] for n in range(ref.shape[0])], axis=1)
+    )(*operands, *raw, *straight)
 
 
 def joined(pieces):
@@ -232,38 +240,49 @@
     return jnp.concatenate(mixed, axis=0)
 
 
-def head_specs(kept_shape, feats, group):
-    blocks, _, rows = kept_shape
-    first = feats // (8 * group)
-    return (
-        pl.BlockSpec((blocks, 8 * group, rows), lambda h: (0, h, 0)),
-        pl.BlockSpec((blocks, 8 * group, rows), lambda h: (0, first + h, 0)),
-        pl.BlockSpec((blocks, 8, rows), lambda h: (0, 2 * feats // 8, 0)),
-    )
-
-
 def attend_back_kernel(
     pair, cot, queries, keys, values, mixed, d_mixed, log_sums, id_column, id_row,
-    out_pair, grad_pair, d_queries, d_keys, d_values, score, d_prob, p_high, p_low, g_high, g_low,
+    out_pair, grad_pair, d_queries, d_keys, d_values,
+    pair_buf, cot_buf, out_buf, grad_buf, score, d_prob, p_high, p_low, g_high, g_low, in_sem, out_sem,
 ):
-    group, rows, cols = score.shape
-    blocks = d_keys.shape[0] * 2
+    heads = pair.shape[1]
+    rows, cols = score.shape
+    depth = pair_buf.shape[0]
     chunk = min(CHUNK, cols)
     place = lax.broadcasted_iota(jnp.int32, (8, rows), 0)
+
+    def moves(index, sources, targets, sem, outward):
+        slot = lax.rem(index, depth)
+        return [
+            pltpu.make_async_copy(buf.at[slot], array.at[0, index], sem.at[n, slot])
+            if outward
+            else pltpu.make_async_copy(array.at[0, index], buf.at[slot], sem.at[n, slot])
+            for n, (array, buf) in enumerate(zip(sources, targets, strict=True))
+        ]
+
+    def inward(index):
+        return moves(index, (pair, cot), (pair_buf, cot_buf), in_sem, False)
+
+    def outward(index):
+        return moves(index, (out_pair, grad_pair), (out_buf, grad_buf), out_sem, True)
 
     def both(left, high, low, dims):
         value = dot(left, high, dims) + dot(left, low, dims)
         return value[0:8] + value[8:16]
 
-    for g in range(group):
-        head = slice(8 * g, 8 * g + 8)
+    for n in range(min(depth, heads)):
+        for copy in inward(n):
+            copy.start()
+
+    def step(index, carry):
+        slot = lax.rem(index, depth)
+        head = pl.ds(pl.multiple_of(index * 8, 8), 8)
         q_high, q_low = wide_halves(queries[head, :])
-        k_high, k_low = wide_halves(whole_row(keys, 8 * g, 8))
-        v_high, v_low = wide_halves(whole_row(values, 8 * g, 8))
+        k_high, k_low = wide_halves(joined(keys[n, head, :] for n in range(keys.shape[0])))
+        v_high, v_low = wide_halves(joined(values[n, head, :] for n in range(keys.shape[0])))
         m_high, m_low = wide_halves(d_mixed[head, :])
-        first = -column_sum(mixed[head, :] * d_mixed[head, :])
-        delta_high, second = wide_halves(first)
-        delta_mid, delta_low = wide_halves(second)
+        delta_high, rest = wide_halves(-column_sum(mixed[head, :] * d_mixed[head, :]))
+        delta_mid, delta_low = wide_halves(rest)
         deltas = jnp.where(
             place == 0, delta_high, jnp.where(place == 1, delta_mid, jnp.where(place == 2, delta_low, 0.0))
         )
@@ -274,52 +293,90 @@
         q_pair = stacked([q_high, q_low])
         k_pair = stacked([k_high, k_low])
         m_pair = stacked([m_high, m_low])
-        d_query = None
-        for start in range(0, cols, chunk):
-            part = slice(start, start + chunk)
-            score[g, :, part] = dot(q_pack, k_pack[:, part], TN)
-            d_prob[g, :, part] = dot(m_pack, v_pack[:, part], TN)
+        for copy in inward(index):
+            copy.wait()
+
+        @pl.when(index >= depth)
+        def _():
+            for copy in outward(index - depth):
+                copy.wait()
+
+        d_query = [None]
+
+        def before(part):
+            score[:, part] = dot(q_pack, k_pack[:, part], TN)
+            d_prob[:, part] = dot(m_pack, v_pack[:, part], TN)
+
+        def middle(part):
             for s in range(rows // STRIP):
                 line = pl.ds(s * STRIP, STRIP)
                 own = id_column[line, :]
-                log_sum = log_sums[g, line, :]
-                for j in range(start, start + chunk, LANES):
+                log_sum = log_sums[index, line, :]
+                for j in range(part.start, part.stop, LANES):
                     tile = pl.ds(j, LANES)
-                    value = pair[0, g, line, tile] + score[g, line, tile]
-                    out_pair[0, g, line, tile] = value
+                    value = pair_buf[slot, line, tile] + score[line, tile]
+                    out_buf[slot, line, tile] = value
                     prob = jnp.exp(jnp.where(own == id_row[:, tile], value - log_sum, MASK_FILL))
-                    p_high[g, line, tile], p_low[g, line, tile] = halves(prob)
-                    grad = prob * d_prob[g, line, tile] + cot[0, g, line, tile]
-                    grad_pair[0, g, line, tile] = grad
-                    g_high[g, line, tile], g_low[g, line, tile] = halves(grad)
-            d_value = both(m_pair, p_high[g, :, part], p_low[g, :, part], NN)
-            d_key = both(q_pair, g_high[g, :, part], g_low[g, :, part], NN)
-            for n in range(start // rows, (start + chunk) // rows):
-                span = slice(n * rows - start, (n + 1) * rows - start)
+                    p_high[line, tile], p_low[line, tile] = halves(prob)
+                    grad = prob * d_prob[line, tile] + cot_buf[slot, line, tile]
+                    grad_buf[slot, line, tile] = grad
+                    g_high[line, tile], g_low[line, tile] = halves(grad)
+
+        def after(part):
+            d_value = both(m_pair, p_high[:, part], p_low[:, part], NN)
+            d_key = both(q_pair, g_high[:, part], g_low[:, part], NN)
+            for n in range(part.start // rows, part.stop // rows):
+                span = slice(n * rows - part.start, (n + 1) * rows - part.start)
                 d_keys[n // 2, n % 2, head, :] = d_key[:, span]
                 d_values[n // 2, n % 2, head, :] = d_value[:, span]
-            term = both(k_pair[:, part], g_high[g, :, part], g_low[g, :, part], NT)
-            d_query = term if d_query is None else d_query + term
-        d_queries[head, :] = d_query * (DH ** (-0.5))
+            term = both(k_pair[:, part], g_high[:, part], g_low[:, part], NT)
+            d_query[0] = term if d_query[0] is None else d_query[0] + term
+
+        parts = [slice(start, start + chunk) for start in range(0, cols, chunk)]
+        before(parts[0])
+        for n, part in enumerate(parts):
+            if n + 1 < len(parts):
+                before(parts[n + 1])
+            middle(part)
+            if n >= 1:
+                after(parts[n - 1])
+        after(parts[-1])
+        d_queries[head, :] = d_query[0] * (DH ** (-0.5))
+        for copy in outward(index):
+            copy.start()
+
+        @pl.when(index + depth < heads)
+        def _():
+            for copy in inward(index + depth):
+                copy.start()
+
+        return carry
+
+    lax.fori_loop(0, heads, step, 0)
+    for n in range(max(0, heads - depth), heads):
+        for copy in outward(n):
+            copy.wait()
 
 
 def attend_back(pair, cot, queries, kept, mixed, d_mixed, log_sums, id_column, id_row):
     _, heads, rows, cols = pair.shape
-    group = GROUP
     feats = heads * DH
     blocks = kept.shape[0]
-    keys, values, _ = head_specs(kept.shape, feats, group)
-    big = pl.BlockSpec((1, group, rows, cols), lambda h: (0, h, 0, 0))
-    flat = pl.BlockSpec((8 * group, rows), lambda h: (h, 0))
-    split = pl.BlockSpec((blocks // 2, 2, 8 * group, rows), lambda h: (0, 0, h, 0))
+    depth = 4
+    big = pl.BlockSpec(memory_space=pltpu.HBM)
+    flat = pl.BlockSpec((feats, rows), lambda n: (0, 0))
+    split = pl.BlockSpec((blocks // 2, 2, feats, rows), lambda n: (0, 0, 0, 0))
     return pl.pallas_call(
         attend_back_kernel,
-        grid=(heads // group,),
+        grid=(1,),
         in_specs=[
-            big, big, flat, keys, values, flat, flat,
-            pl.BlockSpec((group, rows, LANES), lambda h: (h, 0, 0)),
-            pl.BlockSpec((rows, LANES), lambda h: (0, 0)),
-            pl.BlockSpec((STRIP, cols), lambda h: (0, 0)),
+            big, big, flat,
+            pl.BlockSpec((blocks, feats, rows), lambda n: (0, 0, 0)),
+            pl.BlockSpec((blocks, feats, rows), lambda n: (0, 1, 0)),
+            flat, flat,
+            pl.BlockSpec((heads, rows, LANES), lambda n: (0, 0, 0)),
+            pl.BlockSpec((rows, LANES), lambda n: (0, 0)),
+            pl.BlockSpec((STRIP, cols), lambda n: (0, 0)),
         ],
         out_specs=[big, big, flat, split, split],
         out_shape=[
@@ -329,9 +386,11 @@
             jax.ShapeDtypeStruct((blocks // 2, 2, feats, rows), F32),
             jax.ShapeDtypeStruct((blocks // 2, 2, feats, rows), F32),
         ],
-        scratch_shapes=[pltpu.VMEM((group, rows, cols), F32)] * 2
-        + [pltpu.VMEM((group, rows, cols), BF16)] * 4,
-        compiler_params=pltpu.CompilerParams(vmem_limit_bytes=56 << 20),
+        scratch_shapes=[pltpu.VMEM((depth, rows, cols), F32)] * 4
+        + [pltpu.VMEM((rows, cols), F32)] * 2
+        + [pltpu.VMEM((rows, cols), BF16)] * 4
+        + [pltpu.SemaphoreType.DMA((2, depth))] * 2,
+        compiler_params=pltpu.CompilerParams(vmem_limit_bytes=60 << 20),
         cost_estimate=pl.CostEstimate(
             flops=2 * 400 * heads * rows * cols,
             bytes_accessed=16 * heads * rows * cols,
@@ -358,25 +417,27 @@
     ) = operands
     (pair,) = raw
     (
-        queries, kept, id_column, log_sums, mixed, id_row, d_mixed, hidden, down, d_hidden, grad_share, small,
+        queries, kept, id_column, log_sums, mixed, id_row, d_mixed, hidden, down, d_hidden, up_share, down_share, small,
     ) = results
     (
         pair_buf, score, high, low, q_part, q_land, q_all, k_all, w_all, squares, mixed_all, normal_two, rate_two,
-        part, landed, back, back_landed, grads, sib_grads, go_grads, got_grads,
-        pair_sem, kept_send, kept_recv, kz_send, kf_send, ks_send, k_recv, q_send, q_recv, w_send, wf_send, w_recv,
+        part, landed, back, back_landed, ups_part, ups_sib, ups_go, ups_got, downs_part, downs_sib, downs_go, downs_got,
+        pair_sem, kept_send, kept_recv, kz_send, kf_send, ks_send, k_recv, q_send, q_recv, w_send, wx_send, wf_send, w_recv,
         mix_send, mix_recv, part_send, part_recv, back_send, back_recv, sib_send, sib_recv, g_send, g_recv,
     ) = scratch
     zs, feats, rows = mixed_all.shape
     blocks = kept.shape[0]
     chips = blocks // 2
-    teams, _, share, width = grads.shape
+    teams, width = ups_part.shape[0], atoms.shape[1]
     _, group, _, cols = pair_buf.shape
     heads = feats // DH
     groups = heads // group
     piece = rows // zs
     z, blk = lax.axis_index("head"), lax.axis_index("blk")
     core, chip = lax.rem(blk, 2), lax.div(blk, 2)
-    team = lax.axis_index("dp") * chips + chip
+    dp, dps = lax.axis_index("dp"), lax.axis_size("dp")
+    partners = others(dp, dps)
+    team = dp * chips + chip
     other_core = 1 - core
     sib_blk = blk + 1 - 2 * core
     sibling = {"blk": sib_blk}
@@ -398,38 +459,42 @@
 
     normal, _ = normalize(atoms[...])
     normed = halves(normal * gain_one[...] + bias_one[...])
+    meet(meeting)
+    copies = []
+    fewer = feats // (2 * dps)
+    w_mine = w_out.source.at[pl.ds(pl.multiple_of((dp * 2 + core) * fewer, 8), fewer)]
+    copies += [
+        send(w_mine, w_all.at[z, dp, core], w_send.at[n], w_recv.at[z, dp, core], {"head": peer})
+        for n, peer in enumerate(peers)
+    ]
     kept[blk, 0:feats, :] = dot_halves(normed, halves(w_key[...])).T
+    copies += [
+        send(kept.at[blk, 0:feats], k_all.at[blk, z], kz_send.at[n], k_recv.at[blk, z], {"head": peer})
+        for n, peer in enumerate(peers)
+    ]
     kept[blk, feats : 2 * feats, :] = (dot_halves(normed, halves(w_value[...])) + b_value[...]).T
     id_line = ids[...].astype(F32)
     kept[blk, 2 * feats : 2 * feats + 8, :] = jnp.broadcast_to(id_line, (8, rows))
-    meet(meeting)
-    copies = [
+    copies += [
         send(kept.at[blk], kept.at[blk], kept_send.at[n], kept_recv.at[blk], {"blk": peer})
         for n, peer in enumerate([sib_blk] + far)
     ]
-    copies += [
-        send(kept.at[blk, 0:feats], k_all.at[blk, z], kz_send.at[n], k_recv.at[blk, z], {"head": peer})
-        for n, peer in enumerate(peers)
-    ]
     q_rows = (dot_halves(normed, halves(w_query[...])) + b_query[...]) * (DH ** (-0.5))
     q_part[...] = q_rows.reshape(zs, piece, feats)
-    copies += [
-        send(q_part.at[peer], q_land.at[z], q_send.at[n], q_recv.at[z], {"head": peer})
-        for n, peer in enumerate(peers)
-    ]
-    half = feats // 2
-    w_mine = w_out.source.at[pl.ds(pl.multiple_of(core * half, 8), half)]
-    copies += [
-        send(w_mine, w_all.at[z, core], w_send.at[n], w_recv.at[z, core], {"head": peer})
-        for n, peer in enumerate(peers)
-    ]
     queries[...] = q_rows.T
     queries.flush()
     q_land[z] = q_part[z]
-    w_all[z] = w_out[...].reshape(2, half, width)
+    w_all[z] = w_out[...].reshape(dps, 2, fewer, width)
     id_column[...] = jnp.broadcast_to(id_line, (LANES, rows)).T
     id_column.flush()
     small[...] = jnp.zeros(small.shape, F32)
+    for n, peer in enumerate(peers):
+        ready = w_all.at[peer, dp, core]
+        arrived(ready, w_recv.at[peer, dp, core])
+        copies += [
+            send(ready, ready, wx_send.at[n, m], w_recv.at[peer, dp, core], {"dp": partner})
+            for m, partner in enumerate(partners)
+        ]
     for n, source in enumerate(far):
         arrived(kept.at[source], kept_recv.at[source])
         copies.append(
@@ -482,9 +547,14 @@
     mixed.flush()
     log_sums.flush()
     for n, peer in enumerate(peers):
-        ready = w_all.at[peer, core]
-        arrived(ready, w_recv.at[peer, core])
-        copies.append(send(ready, ready, wf_send.at[n], w_recv.at[peer, core], sibling))
+        for kind in range(dps):
+            ready = w_all.at[peer, kind, core]
+
+            @pl.when(dp != kind)
+            def _(ready=ready, sem=w_recv.at[peer, kind, core]):
+                arrived(ready, sem)
+
+            copies.append(send(ready, ready, wf_send.at[n, kind], w_recv.at[peer, kind, core], sibling))
     for n, peer in enumerate(peers):
         ready = k_all.at[blk, peer]
         arrived(ready, k_recv.at[blk, peer])
@@ -499,13 +569,18 @@
     d_act = dot_halves(cots, downs, NT)
     ups = halves(w_up[...])
     for peer in peers:
-        arrived(w_all.at[peer, other_core], w_recv.at[peer, other_core])
+        for kind in range(dps):
+            arrived(w_all.at[peer, kind, other_core], w_recv.at[peer, kind, other_core])
     outs = halves(w_all[...].reshape(zs * feats, width))
     mixed_all[z] = mixed[...]
     for peer in peers:
         for index in range(groups):
             some = pl.ds(index * (8 * group), 8 * group)
             arrived(mixed_all.at[peer, some], mix_recv.at[peer, index])
+    copies += [
+        send(q_part.at[peer], q_land.at[z], q_send.at[n], q_recv.at[z], {"head": peer})
+        for n, peer in enumerate(peers)
+    ]
     mixed_rows = mixed_all[...].reshape(zs * feats, rows).T
     hidden_rows = atoms[...] + dot_halves(halves(mixed_rows), outs) + b_out[...]
     hidden[...] = hidden_rows
@@ -525,10 +600,10 @@
         for n, peer in enumerate(peers)
     ]
     landed[z] = part[z]
-    grad_up = dot_halves(halves(d_pre.T), halves(normed))
-    grad_down = dot_halves(halves(act.T), cots)
-    grads[...] = jnp.concatenate([grad_up, grad_down], axis=0).reshape(grads.shape)
-    copies.append(send(grads.at[:, other_core], sib_grads, sib_send.at[0], sib_recv.at[0], sibling))
+    ups_part[...] = dot_halves(halves(normed.T), d_pres).reshape(ups_part.shape)
+    copies.append(send(ups_part.at[:, other_core], ups_sib, sib_send.at[0], sib_recv.at[0], sibling))
+    downs_part[...] = dot_halves(halves(act.T), cots).reshape(downs_part.shape)
+    copies.append(send(downs_part.at[:, other_core], downs_sib, sib_send.at[1], sib_recv.at[1], sibling))
     for n, source in enumerate(far):
         for m, peer in enumerate(peers):
             ready = k_all.at[source, peer]
@@ -537,15 +612,19 @@
     down[...] = dot_halves(halves(act), downs)
     down.flush()
     small[SMALL_B_UP : SMALL_B_UP + 1, 0 : d_pre.shape[1]] = column_sum(d_pre)
-    arrived(sib_grads, sib_recv.at[0])
-    go_grads[...] = sib_grads[...] + grads[:, core]
-    copies += [
-        send(
-            go_grads.at[peer], got_grads.at[team], g_send.at[n], g_recv.at[team], team_device(peer, core, chips)
-        )
-        for n, peer in enumerate(far_teams)
-    ]
-    got_grads[team] = go_grads[team]
+    for kind, (parts, sib, go, got) in enumerate(
+        [(ups_part, ups_sib, ups_go, ups_got), (downs_part, downs_sib, downs_go, downs_got)]
+    ):
+        arrived(sib, sib_recv.at[kind])
+        go[...] = sib[...] + parts[:, core]
+        copies += [
+            send(
+                go.at[peer], got.at[team], g_send.at[kind, n], g_recv.at[kind, team],
+                team_device(peer, core, chips),
+            )
+            for n, peer in enumerate(far_teams)
+        ]
+        got[team] = go[team]
     for peer in peers:
         arrived(q_land.at[peer], q_recv.at[peer])
     for n in range(zs):
@@ -613,9 +692,11 @@
         arrived(back_landed.at[peer], back_recv.at[peer])
     d_mixed[...] = back_landed[...].reshape(rows, feats).T
     d_mixed.flush()
-    for peer in far_teams:
-        arrived(got_grads.at[peer], g_recv.at[peer])
-    grad_share[...] = functools.reduce(jnp.add, [got_grads[n] for n in range(teams)])
+    for kind, (got, result) in enumerate([(ups_got, up_share), (downs_got, down_share)]):
+        for peer in far_teams:
+            arrived(got.at[peer], g_recv.at[kind, peer])
+        result[...] = functools.reduce(jnp.add, [got[n] for n in range(teams)])
+        result.flush()
     for copy in copies:
         copy.wait_send()
 
@@ -627,15 +708,16 @@
     lax.fori_loop(0, groups, drain, 0)
 
 
-def front(zs, teams, pair, *operands):
+def front(zs, dps, teams, pair, *operands):
     _, heads, rows, cols = pair.shape
     feats, blocks = heads * DH, cols // rows
     width, units = operands[0].shape[1], operands[12].shape[1]
-    piece, share, group = rows // zs, units // teams, GROUP
+    piece, group = rows // zs, GROUP
+    up_rows, down_rows = width // (2 * teams), units // (2 * teams)
     groups = heads // group
     slab = pltpu.VMEM((zs, piece, width), F32)
     narrow = pltpu.VMEM((zs, piece, feats), F32)
-    one = pltpu.VMEM((teams, share, width), F32)
+    one_up, one_down = pltpu.VMEM((teams, up_rows, units), F32), pltpu.VMEM((teams, down_rows, width), F32)
     dma = pltpu.SemaphoreType.DMA
     return staged_call(
         front_kernel,
@@ -643,8 +725,8 @@
         operands,
         [
             (feats, rows), (blocks, 2 * feats + 8, rows), (rows, LANES), (heads, rows, LANES), (feats, rows),
-            (STRIP, cols), (feats, rows), (rows, width), (rows, width), (piece, width), (share, width),
-            (SMALL_ROWS, width),
+            (STRIP, cols), (feats, rows), (rows, width), (rows, width), (piece, width),
+            (up_rows, units), (down_rows, width), (SMALL_ROWS, width),
         ],
         [
             pltpu.VMEM((2, group, rows, cols), F32),
@@ -654,24 +736,26 @@
             narrow, narrow,
             pltpu.VMEM((zs, feats, piece), F32),
             pltpu.VMEM((blocks, zs, feats, rows), F32),
-            pltpu.VMEM((zs, 2, feats // 2, width), F32),
+            pltpu.VMEM((zs, dps, 2, feats // (2 * dps), width), F32),
             pltpu.VMEM((piece, cols), F32),
             pltpu.VMEM((zs, feats, rows), F32),
             pltpu.VMEM((rows, width), F32),
             pltpu.VMEM((rows, LANES), F32),
             slab, slab, narrow, narrow,
-            pltpu.VMEM((teams, 2, share, width), F32),
-            one, one, one,
+            pltpu.VMEM((teams, 2, up_rows, units), F32),
+            one_up, one_up, one_up,
+            pltpu.VMEM((teams, 2, down_rows, width), F32),
+            one_down, one_down, one_down,
             dma((2,)),
             dma((blocks,)), dma((blocks,)),
             dma((zs,)), dma((zs, blocks // 2)), dma((blocks // 2, zs)), dma((blocks, zs)),
             dma((zs,)), dma((zs,)),
-            dma((zs,)), dma((zs,)), dma((zs, 2)),
+            dma((zs,)), dma((zs, dps)), dma((zs, dps)), dma((zs, dps, 2)),
             dma((zs, groups)), dma((zs, groups)),
             dma((zs,)), dma((zs,)),
             dma((zs,)), dma((zs,)),
-            dma((1,)), dma((1,)),
-            dma((teams,)), dma((teams,)),
+            dma((2,)), dma((2,)),
+            dma((2, teams)), dma((2, teams)),
         ],
         58,
         remote=0,
@@ -681,14 +765,14 @@
 
 def finish_kernel(operands, results, scratch, raw):
     (
-        d_keys, d_values, d_hidden, share_in, d_queries, atoms, gain, bias, w_query, mixed, small_in, w_key, w_value,
+        d_keys, d_values, d_hidden, d_queries, atoms, gain, bias, w_query, mixed, small_in, w_key, w_value,
     ) = operands
-    grad_atoms, total_grads, total_big, small, penalty = results
+    grad_atoms, total_grads, small, penalty = results
     (
         sib_keys, sib_values, go_keys, go_values, got_keys, got_values,
         part, landed, grads, sib_grads, go_grads, got_grads, hidden_all, small_z, small_all,
         sib_send, sib_recv, kv_send, kv_recv, part_send, part_recv, back_send, back_recv,
-        g_send, g_recv, t_send, t_recv, f_send, b_send, b_recv, bf_send, h_send, h_recv,
+        g_send, g_recv, t_send, t_recv, f_send, h_send, h_recv,
         small_z_send, small_z_recv, small_send, small_recv,
     ) = scratch
     chips, _, feats, rows = d_keys.shape
@@ -717,25 +801,20 @@
         for n, peer in enumerate(peers)
     ]
     own_keys, own_values = d_keys.ref, d_values.ref
-    arrived(sib_keys, sib_recv.at[0])
-    arrived(sib_values, sib_recv.at[1])
-    go_keys[...] = sib_keys[...] + own_keys[:, core]
-    go_values[...] = sib_values[...] + own_values[:, core]
-    for n, peer in enumerate(far_chips):
-        target = {"blk": peer * 2 + core}
-        copies.append(send(go_keys.at[peer], got_keys.at[chip], kv_send.at[0, n], kv_recv.at[0, chip], target))
-        copies.append(
-            send(go_values.at[peer], got_values.at[chip], kv_send.at[1, n], kv_recv.at[1, chip], target)
-        )
+    for kind, (sib, mine_too, go, got) in enumerate(
+        [(sib_keys, own_keys, go_keys, got_keys), (sib_values, own_values, go_values, got_values)]
+    ):
+        arrived(sib, sib_recv.at[kind])
+        go[...] = sib[...] + mine_too[:, core]
+        copies += [
+            send(
+                go.at[peer], got.at[chip], kv_send.at[kind, n], kv_recv.at[kind, chip],
+                {"blk": peer * 2 + core},
+            )
+            for n, peer in enumerate(far_chips)
+        ]
     got_keys[chip] = go_keys[chip]
     got_values[chip] = go_values[chip]
-    total_big[team, core] = share_in[...]
-    ready = total_big.at[team, core]
-    copies.append(send(ready, ready, b_send.at[0], b_recv.at[team, core], sibling))
-    copies += [
-        send(ready, ready, b_send.at[n + 1], b_recv.at[team, core], team_device(peer, core, chips))
-        for n, peer in enumerate(far_teams)
-    ]
     normal, rate = normalize(atoms[...])
     normed = halves(normal * gain[...] + bias[...])
     dq_rows = d_queries[...].T
@@ -810,10 +889,6 @@
         for n, target in enumerate(plane)
     ]
     for n, peer in enumerate(far_teams):
-        ready = total_big.at[peer, core]
-        arrived(ready, b_recv.at[peer, core])
-        copies.append(send(ready, ready, bf_send.at[n], b_recv.at[peer, core], sibling))
-    for n, peer in enumerate(far_teams):
         ready = total_grads.at[peer, core]
         arrived(ready, t_recv.at[peer, core])
         copies.append(send(ready, ready, f_send.at[n], t_recv.at[peer, core], sibling))
@@ -824,9 +899,6 @@
     ends = summed[SMALL_PENALTY : SMALL_PENALTY + 1, :]
     penalty[...] = ends[:, 0:1] / ends[:, 1:2]
     for peer in [team] + far_teams:
-        arrived(total_big.at[peer, other_core], b_recv.at[peer, other_core])
-    total_big.flush()
-    for peer in [team] + far_teams:
         arrived(total_grads.at[peer, other_core], t_recv.at[peer, other_core])
     total_grads.flush()
     for peer in peers:
@@ -837,7 +909,7 @@
 
 
 def finish(zs, dps, *operands):
-    d_keys, share_in, atoms = operands[0], operands[3], operands[5]
+    d_keys, atoms = operands[0], operands[4]
     chips, _, feats, rows = d_keys.shape
     width = atoms.shape[1]
     piece = rows // zs
@@ -854,7 +926,6 @@
         [
             (rows, width),
             (teams, 2, share, width),
-            (teams, 2) + share_in.shape,
             (SMALL_ROWS, width),
             (1, 1),
         ],
@@ -869,7 +940,6 @@
             dma((zs,)), dma((zs,)),
             dma((teams,)), dma((teams,)),
             dma((teams,)), dma((teams, 2)), dma((teams,)),
-            dma((teams,)), dma((teams, 2)), dma((teams,)),
             dma((zs,)), dma((zs,)),
             dma((zs,)), dma((zs,)),
             dma((2 * teams,)), dma((2 * teams,)),
@@ -880,12 +950,9 @@
 
 
 def place_kernel(operands, results, scratch, raw):
-    total_grads, total_big, small, hidden, down, b_down, rows_in = operands
-    grad_query, grad_key, grad_value, grad_out, grad_up, grad_down, out_atoms, grad_atoms = results[:8]
-    feats, units = grad_out.shape[0], grad_down.shape[0]
-    width = grad_out.shape[1]
-    grad_atoms[...] = rows_in[...]
-    grad_atoms.flush()
+    total_grads, hidden, down, b_down, small = operands
+    grad_query, grad_key, grad_value, grad_out, out_atoms = results[:5]
+    feats, width = grad_out.shape
     done = total_grads[...].reshape(4 * feats, width)
     grad_query[...] = done[0:feats].T
     grad_query.flush()
@@ -895,14 +962,9 @@
     grad_value.flush()
     grad_out[...] = done[3 * feats :]
     grad_out.flush()
-    done = total_big[...].reshape(2 * units, width)
-    grad_up[...] = done[0:units].T
-    grad_up.flush()
-    grad_down[...] = done[units:]
-    grad_down.flush()
     out_atoms[...] = hidden[...] + down[...] + b_down[...]
     out_atoms.flush()
-    for result, row in zip(results[8:], SMALL_OUTPUTS, strict=True):
+    for result, row in zip(results[5:], SMALL_OUTPUTS, strict=True):
         result[...] = small[row : row + 1, 0 : result.shape[1]]
 
 
@@ -912,18 +974,19 @@
 )
 
 
-def place(feats, units, *operands):
-    rows, width = operands[3].shape
+def place(feats, units, straight, *operands):
+    rows, width = operands[1].shape
     lengths = {SMALL_B_QUERY: feats, SMALL_B_VALUE: feats, SMALL_B_UP: units}
     return staged_call(
         place_kernel,
         "place",
         operands,
         [(width, feats)] * 3
-        + [(feats, width), (width, units), (units, width), (rows, width), (rows, width)]
+        + [(feats, width), (rows, width)]
         + [(1, lengths.get(row, width)) for row in SMALL_OUTPUTS],
         [],
-        32,
+        58,
+        straight=straight,
     )
 
 
@@ -939,26 +1002,29 @@
         return value.reshape(1, -1)
 
     (
-        queries, kept, id_column, log_sums, mixed, id_row, d_mixed, hidden, down, d_hidden, grad_share, small,
+        queries, kept, id_column, log_sums, mixed, id_row, d_mixed, hidden, down, d_hidden, up_share, down_share, small,
     ) = front(
-        zs, dps * blocks // 2, pair,
+        zs, dps, dps * blocks // 2, pair,
         inputs, mol_ids, line(ln1_gain), line(ln1_bias), w_key, w_value, line(b_value), w_query, line(b_query),
         w_out, cot, w_down, w_up, line(b_out), line(ln2_gain), line(ln2_bias), line(b_up),
     )
     down = lax.psum(down, "head")
+    grad_up = lax.all_gather(up_share, ("dp", "blk"), axis=0, tiled=True)
+    grad_down = lax.all_gather(down_share, ("dp", "blk"), axis=0, tiled=True)
     out_pair, grad_pair, d_queries, d_keys, d_values = attend_back(
         pair, cot_pair, queries, kept, mixed, d_mixed, log_sums, id_column, id_row
     )
-    grad_atoms, total_grads, total_big, small, penalty = finish(
+    grad_atoms, total_grads, small, penalty = finish(
         zs, dps,
-        d_keys, d_values, d_hidden, grad_share, d_queries, inputs, line(ln1_gain), line(ln1_bias), w_query, mixed,
+        d_keys, d_values, d_hidden, d_queries, inputs, line(ln1_gain), line(ln1_bias), w_query, mixed,
         small, w_key, w_value,
     )
     placed = place(
         w_query.shape[1], w_up.shape[1],
-        total_grads, total_big, small, hidden, down, line(b_down), grad_atoms,
-    )
-    grad_query, grad_key, grad_value, grad_out, grad_up, grad_down, out_atoms, grad_atoms = placed[:8]
+        [grad_atoms, grad_up, grad_down],
+        total_grads, hidden, down, line(b_down), small,
+    )
+    grad_atoms, grad_up, grad_down, grad_query, grad_key, grad_value, grad_out, out_atoms = placed[:8]
     (
         grad_ln1_gain, grad_ln1_bias, grad_b_query, grad_b_value, grad_b_out, grad_ln2_gain, grad_ln2_bias,
         grad_b_up, grad_b_down,

time: 168 us -> 156 us (0.929)
  the two profiles are of different devices: /device:TPU:0 before, /device:TPU:13 now
where the time goes in v4:
time: 156 us
  Pallas kernels  137 us (88%)
  between operations  17.2 us (11%)
    pallas_call x3, Pallas kernels, staged_call(): pl.pallas_call(body, out_shape=[jax.ShapeDtypeStruct(value.shape, value.d...  109 us
    pallas_call x1, Pallas kernels, attend_back(): pl.pallas_call(attend_back_kernel, grid=(1,), in_specs=[big, big, flat, p...  28.3 us
  transfers between devices with their start and end apart: 3, of which 0 were waited for; matrix products, arithmetic and copies ran while one was open for 0% of the time, Pallas kernels for 48%

profile of v4, /device:TPU:13, one launch (start us, length us, event | category | flops | bytes accessed | tf_op | source)
XLA Modules:
  0.0 155.7 jit_solution(10836747665340929991)
XLA Ops:
  8.0 0.0 all-reduce.2.cloned.1.call-start
  8.1 58.7 %front.1 = (f32[128,256]{1,0:T(8,128)}, f32[4,264,256]{2,1,0:T(8,128)}, f32[256,128]{1,0:T(8,128)}, f32[16,256,128]{2,1,0:T(8,128)}, f32[128,256]{1,0:T(8,128)},...) custom-call(f32[256,512]{1,0:T(8,128)} %bitcast.23, ...), custom_call_target="tpu_custom_call" | custom-call | tf_op jit(solution)/shard_map/front/pallas_call | solution.py:162
  66.8 0.0 all-reduce.2.cloned.1.call-update
  66.8 0.0 all-gather.3.cloned.1.call-start
  66.9 0.5 all-gather.3.cloned.1.call-update
  67.4 0.2 all-gather.5.cloned.1.call-start
  67.7 0.4 all-gather.5.cloned.1.call-update
  68.0 28.3 %attend_back.1 = (f32[1,16,256,1024]{3,2,1,0:T(8,128)}, f32[1,16,256,1024]{3,2,1,0:T(8,128)}, f32[128,256]{1,0:T(8,128)}, f32[2,2,128,256]{3,2,1,0:T(8,128)}, f32[2,2,128,256]{3,2,1,0:T(8,128)}) custom-call(f32[1,16,256,1024]{3,2,1,0:T(8,128)} %pair.1, f32[1,16,256,1024]{3,2,1,0:T(8,128)} %cot.1, f32[128,256]{1,0:T(8,128)} %get-tuple-element.59.queries, ...), custom_call_target="tpu_custom_call" | custom-call | flops 3355443200 | bytes 67108864 | tf_op jit(solution)/shard_map/attend_back/pallas_call | solution.py:369
  96.3 46.1 %finish.1 = (f32[256,512]{1,0:T(8,128)}, f32[4,2,64,512]{3,2,1,0:T(8,128)}, f32[16,512]{1,0:T(8,128)}, f32[1,1]{1,0:T(1,128)}) custom-call(f32[2,2,128,256]{3,2,1,0:T(8,128)} %get-tuple-element.66.refs_0_, f32[2,2,128,256]{3,2,1,0:T(8,128)} %get-tuple-element.67.refs_1_, f32[64,512]{1,0:T(8,128)} %get-tuple-element.68.refs_2_, ...), custom_call_target="tpu_custom_call" | custom-call | tf_op jit(solution)/shard_map/finish/pallas_call | solution.py:162
  142.4 0.0 all-reduce.2.cloned.1.call-done.refs_2_
  142.4 0.0 all-gather.3.cloned.1.call-done.refs_6_
  142.5 0.0 all-gather.5.cloned.1.call-done.refs_7_
  142.5 4.1 %place.1 = (f32[256,512]{1,0:T(8,128)}, f32[512,512]{1,0:T(8,128)}, f32[512,512]{1,0:T(8,128)}, f32[512,128]{1,0:T(8,128)}, f32[512,128]{1,0:T(8,128)}, /*index=...) custom-call(f32[4,2,64,512]{3,2,1,0:T(8,128)} %get-tuple-element.71., ...), custom_call_target="tpu_custom_call" | custom-call | tf_op jit(solution)/shard_map/place/pallas_call | solution.py:162
Async XLA Ops:
  8.0 134.4 %all-reduce.2.cloned.1.call-start = ((), (), s32[]{:S(2)}) async-start(), calls=%async_computation | async-start | bytes 1048576 | tf_op jit(solution)/shard_map/psum | solution.py:1011
  66.8 75.6 %all-gather.3.cloned.1.call-start = ((), (), s32[]{:S(2)}) async-start(), calls=%async_computation.1 | async-start | bytes 1179648 | tf_op jit(solution)/shard_map/all_gather | solution.py:1012
  67.4 75.1 %all-gather.5.cloned.1.call-start = ((), (), s32[]{:S(2)}) async-start(), calls=%async_computation.2 | async-start | bytes 1179648 | tf_op jit(solution)/shard_map/all_gather | solution.py:1013
Sparse Core Ops, SparseCore 0:
  67.0 38.2 all-reduce.1
Sparse Core Ops, SparseCore 1:
  69.2 22.2 all-gather.2
  93.2 24.8 all-gather.4

commit v5 on v4

--- a/solution.py
+++ b/solution.py
@@ -413,14 +413,15 @@
 def front_kernel(operands, results, scratch, raw):
     (
         atoms, ids, gain_one, bias_one, w_key, w_value, b_value, w_query, b_query, w_out, cot, w_down, w_up, b_out,
-        gain, bias, b_up,
+        gain, bias, b_up, b_down,
     ) = operands
     (pair,) = raw
     (
-        queries, kept, id_column, log_sums, mixed, id_row, d_mixed, hidden, down, d_hidden, up_share, down_share, small,
-    ) = results
+        queries, kept, id_column, log_sums, mixed, id_row, d_mixed, out_mine, d_hidden, up_share, down_share, small,
+    ) = results[:12]
+    parcels = results[12:]
     (
-        pair_buf, score, high, low, q_part, q_land, q_all, k_all, w_all, squares, mixed_all, normal_two, rate_two,
+        pair_buf, score, high, low, q_part, q_land, q_all, k_all, w_all, squares, mixed_all, hidden_two, down, normal_two, rate_two,
         part, landed, back, back_landed, ups_part, ups_sib, ups_go, ups_got, downs_part, downs_sib, downs_go, downs_got,
         pair_sem, kept_send, kept_recv, kz_send, kf_send, ks_send, k_recv, q_send, q_recv, w_send, wx_send, wf_send, w_recv,
         mix_send, mix_recv, part_send, part_recv, back_send, back_recv, sib_send, sib_recv, g_send, g_recv,
@@ -583,8 +584,7 @@
     ]
     mixed_rows = mixed_all[...].reshape(zs * feats, rows).T
     hidden_rows = atoms[...] + dot_halves(halves(mixed_rows), outs) + b_out[...]
-    hidden[...] = hidden_rows
-    hidden.flush()
+    hidden_two[...] = hidden_rows
     normal, rate = normalize(hidden_rows)
     normal_two[...] = normal
     rate_two[...] = jnp.broadcast_to(rate, rate_two.shape)
@@ -610,7 +610,8 @@
             arrived(ready, k_recv.at[source, peer])
             copies.append(send(ready, ready, ks_send.at[n, m], k_recv.at[source, peer], sibling))
     down[...] = dot_halves(halves(act), downs)
-    down.flush()
+    out_mine[...] = hidden_two[mine, :] + down[mine, :] + b_down[...]
+    out_mine.flush()
     small[SMALL_B_UP : SMALL_B_UP + 1, 0 : d_pre.shape[1]] = column_sum(d_pre)
     for kind, (parts, sib, go, got) in enumerate(
         [(ups_part, ups_sib, ups_go, ups_got), (downs_part, downs_sib, downs_go, downs_got)]
@@ -684,6 +685,10 @@
     back_landed[z] = back[z]
     d_hidden[...] = d_rows
     d_hidden.flush()
+    for peer, parcel in zip(peers, parcels, strict=True):
+        parcel[0:piece, :] = down[pl.ds(pl.multiple_of(peer * piece, 8), piece), :]
+        parcel[piece : 2 * piece, :] = d_rows
+        parcel.flush()
     small[SMALL_LN2_GAIN : SMALL_LN2_GAIN + 1, :] = column_sum(d_normed * normal)
     small[SMALL_LN2_BIAS : SMALL_LN2_BIAS + 1, :] = column_sum(d_normed)
     small[SMALL_B_OUT : SMALL_B_OUT + 1, :] = column_sum(d_rows)
@@ -725,9 +730,10 @@
         operands,
         [
             (feats, rows), (blocks, 2 * feats + 8, rows), (rows, LANES), (heads, rows, LANES), (feats, rows),
-            (STRIP, cols), (feats, rows), (rows, width), (rows, width), (piece, width),
+            (STRIP, cols), (feats, rows), (piece, width), (piece, width),
             (up_rows, units), (down_rows, width), (SMALL_ROWS, width),
-        ],
+        ]
+        + [(2 * piece, width)] * (zs - 1),
         [
             pltpu.VMEM((2, group, rows, cols), F32),
             pltpu.VMEM((group, rows, cols), F32),
@@ -739,6 +745,8 @@
             pltpu.VMEM((zs, dps, 2, feats // (2 * dps), width), F32),
             pltpu.VMEM((piece, cols), F32),
             pltpu.VMEM((zs, feats, rows), F32),
+            pltpu.VMEM((rows, width), F32),
+            pltpu.VMEM((rows, width), F32),
             pltpu.VMEM((rows, width), F32),
             pltpu.VMEM((rows, LANES), F32),
             slab, slab, narrow, narrow,
@@ -765,14 +773,16 @@
 
 def finish_kernel(operands, results, scratch, raw):
     (
-        d_keys, d_values, d_hidden, d_queries, atoms, gain, bias, w_query, mixed, small_in, w_key, w_value,
-    ) = operands
-    grad_atoms, total_grads, small, penalty = results
+        d_keys, d_values, out_mine, d_hidden, d_queries, atoms, gain, bias, w_query, mixed, small_in, w_key, w_value,
+        up_share, down_share,
+    ) = operands[:15]
+    parcels = operands[15:]
+    grad_atoms, out_atoms, total_grads, grad_up, grad_down, small, penalty = results
     (
         sib_keys, sib_values, go_keys, go_values, got_keys, got_values,
         part, landed, grads, sib_grads, go_grads, got_grads, hidden_all, small_z, small_all,
         sib_send, sib_recv, kv_send, kv_recv, part_send, part_recv, back_send, back_recv,
-        g_send, g_recv, t_send, t_recv, f_send, h_send, h_recv,
+        g_send, g_recv, t_send, t_recv, f_send, b_send, b_recv, bf_send, out_send, out_recv,
         small_z_send, small_z_recv, small_send, small_recv,
     ) = scratch
     chips, _, feats, rows = d_keys.shape
@@ -796,8 +806,10 @@
         send(d_keys.source.at[:, other_core], sib_keys, sib_send.at[0], sib_recv.at[0], sibling),
         send(d_values.source.at[:, other_core], sib_values, sib_send.at[1], sib_recv.at[1], sibling),
     ]
-    copies += [
-        send(d_hidden.source, hidden_all.at[z], h_send.at[n], h_recv.at[z], {"head": peer})
+    mine = pl.ds(pl.multiple_of(z * piece, 8), piece)
+    out_atoms[mine, :] = functools.reduce(jnp.add, [parcel[0:piece, :] for parcel in parcels], out_mine[...])
+    copies += [
+        send(out_atoms.at[mine], out_atoms.at[mine], out_send.at[n], out_recv.at[z], {"head": peer})
         for n, peer in enumerate(peers)
     ]
     own_keys, own_values = d_keys.ref, d_values.ref
@@ -820,9 +832,11 @@
     dq_rows = d_queries[...].T
     d_normed = dot_full(dq_rows, w_query[...], NT)
     grad_q = dot_halves(halves(d_queries[...]), normed)
-    mine = pl.ds(pl.multiple_of(z * piece, 8), piece)
     small_z[z] = small_in[0:8, :]
     hidden_all[z] = d_hidden[...]
+    for n, parcel in enumerate(parcels):
+        hidden_all[lax.rem(z + zs - 1 - n, zs)] = parcel[piece : 2 * piece, :]
+    grad_o = dot_full(mixed[...], hidden_all[...].reshape(rows, width))
     for peer in far_chips:
         arrived(got_keys.at[peer], kv_recv.at[0, peer])
         arrived(got_values.at[peer], kv_recv.at[1, peer])
@@ -840,9 +854,6 @@
     landed[z] = part[z]
     grad_k = dot_halves(halves(dk), normed)
     grad_v = dot_halves(halves(dv), normed)
-    for peer in peers:
-        arrived(hidden_all.at[peer], h_recv.at[peer])
-    grad_o = dot_full(mixed[...], hidden_all[...].reshape(rows, width))
     grads[...] = jnp.concatenate([grad_q, grad_k, grad_v, grad_o], axis=0).reshape(grads.shape)
     copies.append(send(grads.at[:, other_core], sib_grads, sib_send.at[2], sib_recv.at[2], sibling))
     arrived(sib_grads, sib_recv.at[2])
@@ -854,6 +865,23 @@
         for n, peer in enumerate(far_teams)
     ]
     got_grads[team] = go_grads[team]
+    bigs = [(up_share, grad_up), (down_share, grad_down)]
+
+    def big_rows(result, source, kind):
+        count = result.shape[0] // (2 * teams)
+        return result.at[pl.ds(pl.multiple_of((source * 2 + kind) * count, 8), count)]
+
+    for kind, (share_in, result) in enumerate(bigs):
+        ready = big_rows(result, team, core)
+        ready[...] = share_in[...]
+        copies.append(send(ready, ready, b_send.at[kind, 0], b_recv.at[kind, team, core], sibling))
+        copies += [
+            send(
+                ready, ready, b_send.at[kind, n + 1], b_recv.at[kind, team, core],
+                team_device(peer, core, chips),
+            )
+            for n, peer in enumerate(far_teams)
+        ]
     for peer in peers:
         arrived(landed.at[peer], part_recv.at[peer])
     d_normed = functools.reduce(jnp.add, [landed[n] for n in range(zs)])
@@ -892,6 +920,11 @@
         ready = total_grads.at[peer, core]
         arrived(ready, t_recv.at[peer, core])
         copies.append(send(ready, ready, f_send.at[n], t_recv.at[peer, core], sibling))
+    for kind, (_, result) in enumerate(bigs):
+        for n, peer in enumerate(far_teams):
+            ready = big_rows(result, peer, core)
+            arrived(ready, b_recv.at[kind, peer, core])
+            copies.append(send(ready, ready, bf_send.at[kind, n], b_recv.at[kind, peer, core], sibling))
     for source in far_places:
         arrived(small_all.at[source], small_recv.at[source])
     summed = functools.reduce(jnp.add, [small_all[n] for n in range(2 * teams)])
@@ -901,6 +934,14 @@
     for peer in [team] + far_teams:
         arrived(total_grads.at[peer, other_core], t_recv.at[peer, other_core])
     total_grads.flush()
+    for kind, (_, result) in enumerate(bigs):
+        for peer in [team] + far_teams:
+            arrived(big_rows(result, peer, other_core), b_recv.at[kind, peer, other_core])
+        result.flush()
+    for peer in peers:
+        there = pl.ds(pl.multiple_of(peer * piece, 8), piece)
+        arrived(out_atoms.at[there], out_recv.at[peer])
+    out_atoms.flush()
     for peer in peers:
         there = pl.ds(pl.multiple_of(peer * piece, 8), piece)
         arrived(grad_atoms.at[there], back_recv.at[peer])
@@ -909,7 +950,8 @@
 
 
 def finish(zs, dps, *operands):
-    d_keys, atoms = operands[0], operands[4]
+    d_keys, atoms = operands[0], operands[5]
+    units = operands[14].shape[0] * 2 * dps * d_keys.shape[0]
     chips, _, feats, rows = d_keys.shape
     width = atoms.shape[1]
     piece = rows // zs
@@ -925,7 +967,10 @@
         operands,
         [
             (rows, width),
+            (rows, width),
             (teams, 2, share, width),
+            (width, units),
+            (units, width),
             (SMALL_ROWS, width),
             (1, 1),
         ],
@@ -940,6 +985,7 @@
             dma((zs,)), dma((zs,)),
             dma((teams,)), dma((teams,)),
             dma((teams,)), dma((teams, 2)), dma((teams,)),
+            dma((2, teams)), dma((2, teams, 2)), dma((2, teams)),
             dma((zs,)), dma((zs,)),
             dma((zs,)), dma((zs,)),
             dma((2 * teams,)), dma((2 * teams,)),
@@ -950,8 +996,8 @@
 
 
 def place_kernel(operands, results, scratch, raw):
-    total_grads, hidden, down, b_down, small = operands
-    grad_query, grad_key, grad_value, grad_out, out_atoms = results[:5]
+    total_grads, small = operands
+    grad_query, grad_key, grad_value, grad_out = results[:4]
     feats, width = grad_out.shape
     done = total_grads[...].reshape(4 * feats, width)
     grad_query[...] = done[0:feats].T
@@ -962,9 +1008,7 @@
     grad_value.flush()
     grad_out[...] = done[3 * feats :]
     grad_out.flush()
-    out_atoms[...] = hidden[...] + down[...] + b_down[...]
-    out_atoms.flush()
-    for result, row in zip(results[5:], SMALL_OUTPUTS, strict=True):
+    for result, row in zip(results[4:], SMALL_OUTPUTS, strict=True):
         result[...] = small[row : row + 1, 0 : result.shape[1]]
 
 
@@ -975,14 +1019,14 @@
 
 
 def place(feats, units, straight, *operands):
-    rows, width = operands[1].shape
+    width = operands[1].shape[1]
     lengths = {SMALL_B_QUERY: feats, SMALL_B_VALUE: feats, SMALL_B_UP: units}
     return staged_call(
         place_kernel,
         "place",
         operands,
         [(width, feats)] * 3
-        + [(feats, width), (rows, width)]
+        + [(feats, width)]
         + [(1, lengths.get(row, width)) for row in SMALL_OUTPUTS],
         [],
         58,
@@ -1002,29 +1046,32 @@
         return value.reshape(1, -1)
 
     (
-        queries, kept, id_column, log_sums, mixed, id_row, d_mixed, hidden, down, d_hidden, up_share, down_share, small,
+        queries, kept, id_column, log_sums, mixed, id_row, d_mixed, out_mine, d_hidden, up_share, down_share, small,
+        *parcels,
     ) = front(
         zs, dps, dps * blocks // 2, pair,
         inputs, mol_ids, line(ln1_gain), line(ln1_bias), w_key, w_value, line(b_value), w_query, line(b_query),
         w_out, cot, w_down, w_up, line(b_out), line(ln2_gain), line(ln2_bias), line(b_up),
-    )
-    down = lax.psum(down, "head")
-    grad_up = lax.all_gather(up_share, ("dp", "blk"), axis=0, tiled=True)
-    grad_down = lax.all_gather(down_share, ("dp", "blk"), axis=0, tiled=True)
+        line(b_down),
+    )
+    parcels = [
+        lax.ppermute(parcel, "head", [(source, (source + n + 1) % zs) for source in range(zs)])
+        for n, parcel in enumerate(parcels)
+    ]
     out_pair, grad_pair, d_queries, d_keys, d_values = attend_back(
         pair, cot_pair, queries, kept, mixed, d_mixed, log_sums, id_column, id_row
     )
-    grad_atoms, total_grads, small, penalty = finish(
+    grad_atoms, out_atoms, total_grads, grad_up, grad_down, small, penalty = finish(
         zs, dps,
-        d_keys, d_values, d_hidden, d_queries, inputs, line(ln1_gain), line(ln1_bias), w_query, mixed,
-        small, w_key, w_value,
+        d_keys, d_values, out_mine, d_hidden, d_queries, inputs, line(ln1_gain), line(ln1_bias), w_query, mixed,
+        small, w_key, w_value, up_share, down_share, *parcels,
     )
     placed = place(
         w_query.shape[1], w_up.shape[1],
-        [grad_atoms, grad_up, grad_down],
-        total_grads, hidden, down, line(b_down), small,
-    )
-    grad_atoms, grad_up, grad_down, grad_query, grad_key, grad_value, grad_out, out_atoms = placed[:8]
+        [grad_atoms, out_atoms, grad_up, grad_down],
+        total_grads, small,
+    )
+    grad_atoms, out_atoms, grad_up, grad_down, grad_query, grad_key, grad_value, grad_out = placed[:8]
     (
         grad_ln1_gain, grad_ln1_bias, grad_b_query, grad_b_value, grad_b_out, grad_ln2_gain, grad_ln2_bias,
         grad_b_up, grad_b_down,

time: 156 us -> 144 us (0.923)
  the two profiles are of different devices: /device:TPU:13 before, /device:TPU:0 now
where the time goes in v5:
time: 144 us
  Pallas kernels  137 us (95%)
  starting transfers between devices  4.32 us (3%)
  between operations  2.49 us (2%)
    pallas_call x3, Pallas kernels, staged_call(): pl.pallas_call(body, out_shape=[jax.ShapeDtypeStruct(value.shape, value.d...  108 us
    pallas_call x1, Pallas kernels, attend_back(): pl.pallas_call(attend_back_kernel, grid=(1,), in_specs=[big, big, flat, p...  28.3 us
    ppermute x3, starting transfers between devices, local(): lax.ppermute(parcel, 'head', [(source, (source + n + 1) % zs) for source...  4.32 us
  transfers between devices with their start and end apart: 3, of which 0 were waited for; matrix products, arithmetic and copies ran while one was open for 0% of the time, Pallas kernels for 20%

profile of v5, /device:TPU:0, one launch (start us, length us, event | category | flops | bytes accessed | tf_op | source)
XLA Modules:
  0.0 144.2 jit_solution(10388111993923840207)
XLA Ops:
  0.7 60.3 %front.1 = (f32[128,256]{1,0:T(8,128)}, f32[4,264,256]{2,1,0:T(8,128)}, f32[256,128]{1,0:T(8,128)}, f32[16,256,128]{2,1,0:T(8,128)}, f32[128,256]{1,0:T(8,128)},...) custom-call(f32[256,512]{1,0:T(8,128)} %bitcast.23, ...), custom_call_target="tpu_custom_call" | custom-call | tf_op jit(solution)/shard_map/front/pallas_call | solution.py:162
  61.0 1.1 collective-permute-start
  62.1 1.3 collective-permute-start.1
  63.4 1.9 %collective-permute-start.2 = (f32[128,512]{1,0:T(8,128)}, f32[128,512]{1,0:T(8,128)S(1)}, u32[]{:S(2)}, u32[]{:S(2)}) collective-permute-start(f32[128,512]{1,0:T(8,128)} %get-tuple-element.81), channel_id=1, source_target_pairs={{0,6},{2,0},{4,2},{6,4},{1,7},{3,1},{5,3},{7,5},{8,14},{10,8},{12,... | collective-permute-start | bytes 786440 | tf_op jit(solution)/shard_map/ppermute | solution.py:1058
  65.3 28.3 %attend_back.1 = (f32[1,16,256,1024]{3,2,1,0:T(8,128)}, f32[1,16,256,1024]{3,2,1,0:T(8,128)}, f32[128,256]{1,0:T(8,128)}, f32[2,2,128,256]{3,2,1,0:T(8,128)}, f32[2,2,128,256]{3,2,1,0:T(8,128)}) custom-call(f32[1,16,256,1024]{3,2,1,0:T(8,128)} %pair.1, f32[1,16,256,1024]{3,2,1,0:T(8,128)} %cot.1, f32[128,256]{1,0:T(8,128)} %get-tuple-element.64.queries, ...), custom_call_target="tpu_custom_call" | custom-call | flops 3355443200 | bytes 67108864 | tf_op jit(solution)/shard_map/attend_back/pallas_call | solution.py:369
  93.6 0.0 collective-permute-done.refs_15_
  93.6 0.0 copy-start
  93.6 0.0 collective-permute-done.1.refs_16_
  93.6 0.0 copy-start.1
  93.6 0.0 collective-permute-done.2.refs_17_
  93.6 0.0 copy-start.2
  93.6 0.6 copy-done
  94.3 0.1 copy-done.1
  94.4 0.1 copy-done.2
  94.5 43.8 %finish.1 = (f32[256,512]{1,0:T(8,128)}, f32[256,512]{1,0:T(8,128)}, f32[4,2,64,512]{3,2,1,0:T(8,128)}, f32[512,512]{1,0:T(8,128)}, f32[512,512]{1,0:T(8,128)}, /*index=5*/f32[16,512]{1,0:T(8,128)}, f32[1,1]{1,0:T(1,128)}) custom-call(f32[2,2,128,256]{3,2,1,0:T(8,128)} %get-tuple-element.71.refs_0_, f32[2,2,128,256]{3,2,1,0:T(8,128)} %get-tuple-element.72.refs_1_, ...), custom_call_target="tpu_custom_call" | custom-call | tf_op jit(solution)/shard_map/finish/pallas_call | solution.py:162
  138.3 4.2 %place.1 = (f32[256,512]{1,0:T(8,128)}, f32[256,512]{1,0:T(8,128)}, f32[512,512]{1,0:T(8,128)}, f32[512,512]{1,0:T(8,128)}, f32[512,128]{1,0:T(8,128)}, /*index=...) custom-call(f32[4,2,64,512]{3,2,1,0:T(8,128)} %get-tuple-element.82., ...), custom_call_target="tpu_custom_call" | custom-call | tf_op jit(solution)/shard_map/place/pallas_call | solution.py:162
Async XLA Ops:
  61.0 32.6 %collective-permute-start = (f32[128,512]{1,0:T(8,128)}, f32[128,512]{1,0:T(8,128)S(1)}, u32[]{:S(2)}, u32[]{:S(2)}) collective-permute-start(f32[128,512]{1,0:T(8,128)} %get-tuple-element.79), channel_id=1, source_target_pairs={{0,2},{2,4},{4,6},{6,0},{1,3},{3,5},{5,7},{7,1},{8,10},{10,12},{12... | collective-permute-start | bytes 786440 | tf_op jit(solution)/shard_map/ppermute | solution.py:1058
  62.1 31.5 %collective-permute-start.1 = (f32[128,512]{1,0:T(8,128)}, f32[128,512]{1,0:T(8,128)S(1)}, u32[]{:S(2)}, u32[]{:S(2)}) collective-permute-start(f32[128,512]{1,0:T(8,128)} %get-tuple-element.80), channel_id=1, source_target_pairs={{0,4},{2,6},{4,0},{6,2},{1,5},{3,7},{5,1},{7,3},{8,12},{10,14},{12... | collective-permute-start | bytes 786440 | tf_op jit(solution)/shard_map/ppermute | solution.py:1058
  63.4 30.2 %collective-permute-start.2 = (f32[128,512]{1,0:T(8,128)}, f32[128,512]{1,0:T(8,128)S(1)}, u32[]{:S(2)}, u32[]{:S(2)}) collective-permute-start(f32[128,512]{1,0:T(8,128)} %get-tuple-element.81), channel_id=1, source_target_pairs={{0,6},{2,0},{4,2},{6,4},{1,7},{3,1},{5,3},{7,5},{8,14},{10,8},{12,... | collective-permute-start | bytes 786440 | tf_op jit(solution)/shard_map/ppermute | solution.py:1058
  93.6 0.7 copy-start
  93.6 0.8 copy-start.1
  93.6 0.8 copy-start.2

commit v6 on v5

--- a/solution.py
+++ b/solution.py
@@ -129,13 +129,15 @@
             self.begun = True
 
 
-def staged_call(kernel, name, operands, results, scratch, megabytes, remote=None, raw=(), straight=()):
+def staged_call(kernel, name, operands, results, scratch, megabytes, remote=None, raw=(), straight=(), raw_results=(), cost=None):
     n_in, n_out, n_raw, n_straight = len(operands), len(results), len(raw), len(straight)
+    n_left = len(raw_results)
 
     def body(*refs):
         sources, left, refs = refs[:n_in], refs[n_in : n_in + n_raw], refs[n_in + n_raw :]
         moved, refs = refs[:n_straight], refs[n_straight:]
         arrays, refs = refs[:n_straight], refs[n_straight:]
+        left, refs = left + refs[:n_left], refs[n_left:]
         targets, refs = refs[:n_out], refs[n_out:]
         slots, made, refs = refs[:n_in], refs[n_in : n_in + n_out], refs[n_in + n_out :]
         in_sem, out_sem, move_sem, refs = refs[0], refs[1], refs[2], refs[3:]
@@ -162,15 +164,17 @@
     return pl.pallas_call(
         body,
         out_shape=[jax.ShapeDtypeStruct(value.shape, value.dtype) for value in straight]
+        + [jax.ShapeDtypeStruct(shape, F32) for shape in raw_results]
         + [jax.ShapeDtypeStruct(shape, F32) for shape in results],
         in_specs=[anywhere] * (n_in + n_raw + n_straight),
-        out_specs=[anywhere] * (n_straight + n_out),
+        out_specs=[anywhere] * (n_straight + n_left + n_out),
         scratch_shapes=[pltpu.VMEM(value.shape, value.dtype) for value in operands]
         + [pltpu.VMEM(shape, F32) for shape in results]
         + [pltpu.SemaphoreType.DMA((n,)) for n in (n_in, n_out, max(1, n_straight))]
         + [pltpu.VMEM(value.shape, value.dtype) for value in straight]
         + list(scratch),
         compiler_params=pltpu.CompilerParams(vmem_limit_bytes=megabytes << 20, **extra),
+        cost_estimate=cost,
         name=name,
     )(*operands, *raw, *straight)
 
@@ -240,59 +244,119 @@
     return jnp.concatenate(mixed, axis=0)
 
 
-def attend_back_kernel(
-    pair, cot, queries, keys, values, mixed, d_mixed, log_sums, id_column, id_row,
-    out_pair, grad_pair, d_queries, d_keys, d_values,
-    pair_buf, cot_buf, out_buf, grad_buf, score, d_prob, p_high, p_low, g_high, g_low, in_sem, out_sem,
-):
+def chunks_of(cols):
+    chunk = min(CHUNK, cols)
+    return [slice(start, start + chunk) for start in range(0, cols, chunk)]
+
+
+def score_packs(queries, keys):
+    q_high, q_low = wide_halves(queries)
+    k_high, k_low = wide_halves(keys)
+    return stacked([q_high, q_high, q_low, q_low]), stacked([k_high, k_low, k_high, k_low])
+
+
+def attend_back_kernel(operands, results, scratch, raw):
+    queries, kept, d_mixed, mixed, id_column, id_row = operands
+    d_queries, d_keys, d_values = results
+    pair, cot, log_sums, out_pair, grad_pair = raw
+    pair_buf, cot_buf, log_buf, out_buf, grad_buf = scratch[:5]
+    here = scratch[5:11]
+    in_sem, out_sem = scratch[11:]
     heads = pair.shape[1]
-    rows, cols = score.shape
-    depth = pair_buf.shape[0]
-    chunk = min(CHUNK, cols)
+    feats = heads * DH
+    depth, rows, cols = pair_buf.shape
+    blocks = kept.shape[0]
+    parts = chunks_of(cols)
     place = lax.broadcasted_iota(jnp.int32, (8, rows), 0)
 
-    def moves(index, sources, targets, sem, outward):
+    def inward(index):
+        slot = lax.rem(index, depth)
+        sources = (pair.at[0, index], cot.at[0, index], log_sums.at[index])
+        return [
+            pltpu.make_async_copy(source, buf.at[slot], in_sem.at[n, slot])
+            for n, (source, buf) in enumerate(zip(sources, (pair_buf, cot_buf, log_buf), strict=True))
+        ]
+
+    def outward(index):
         slot = lax.rem(index, depth)
         return [
-            pltpu.make_async_copy(buf.at[slot], array.at[0, index], sem.at[n, slot])
-            if outward
-            else pltpu.make_async_copy(array.at[0, index], buf.at[slot], sem.at[n, slot])
-            for n, (array, buf) in enumerate(zip(sources, targets, strict=True))
+            pltpu.make_async_copy(buf.at[slot], array.at[0, index], out_sem.at[n, slot])
+            for n, (array, buf) in enumerate([(out_pair, out_buf), (grad_pair, grad_buf)])
         ]
 
-    def inward(index):
-        return moves(index, (pair, cot), (pair_buf, cot_buf), in_sem, False)
-
-    def outward(index):
-        return moves(index, (out_pair, grad_pair), (out_buf, grad_buf), out_sem, True)
-
-    def both(left, high, low, dims):
-        value = dot(left, high, dims) + dot(left, low, dims)
-        return value[0:8] + value[8:16]
-
-    for n in range(min(depth, heads)):
+    for n in range(2):
         for copy in inward(n):
             copy.start()
-
-    def step(index, carry):
-        slot = lax.rem(index, depth)
-        head = pl.ds(pl.multiple_of(index * 8, 8), 8)
-        q_high, q_low = wide_halves(queries[head, :])
-        k_high, k_low = wide_halves(joined(keys[n, head, :] for n in range(keys.shape[0])))
-        v_high, v_low = wide_halves(joined(values[n, head, :] for n in range(keys.shape[0])))
+    for operand in operands:
+        operand.ref
+
+    def rows_of(index):
+        return pl.ds(pl.multiple_of(index * 8, 8), 8)
+
+    def key_rows(index):
+        return joined(kept[n, rows_of(index), :] for n in range(blocks))
+
+    def value_rows(index):
+        some = pl.ds(pl.multiple_of(feats + index * 8, 8), 8)
+        return joined(kept[n, some, :] for n in range(blocks))
+
+    def packs(index):
+        head = rows_of(index)
+        q_pack, k_pack = score_packs(queries[head, :], key_rows(index))
+        v_high, v_low = wide_halves(value_rows(index))
         m_high, m_low = wide_halves(d_mixed[head, :])
         delta_high, rest = wide_halves(-column_sum(mixed[head, :] * d_mixed[head, :]))
         delta_mid, delta_low = wide_halves(rest)
         deltas = jnp.where(
             place == 0, delta_high, jnp.where(place == 1, delta_mid, jnp.where(place == 2, delta_low, 0.0))
         )
-        q_pack = stacked([q_high, q_high, q_low, q_low])
-        k_pack = stacked([k_high, k_low, k_high, k_low])
         m_pack = stacked([m_high, m_high, m_low, deltas])
         v_pack = stacked([v_high, v_low, v_high, jnp.ones_like(v_high)])
-        q_pair = stacked([q_high, q_low])
-        k_pair = stacked([k_high, k_low])
-        m_pair = stacked([m_high, m_low])
+        return q_pack, k_pack, m_pack, v_pack
+
+    def pairs(index):
+        head = rows_of(index)
+        return [stacked(wide_halves(value)) for value in (queries[head, :], key_rows(index), d_mixed[head, :])]
+
+    def before(pack, part, there):
+        q_pack, k_pack, m_pack, v_pack = pack
+        there[0][:, part] = dot(q_pack, k_pack[:, part], TN)
+        there[1][:, part] = dot(m_pack, v_pack[:, part], TN)
+
+    def middle(index, slot, part, here):
+        score, d_prob, p_high, p_low, g_high, g_low = here
+        for s in range(rows // STRIP):
+            line = pl.ds(s * STRIP, STRIP)
+            own = id_column[line, :]
+            log_sum = log_buf[slot, line, :]
+            for j in range(part.start, part.stop, LANES):
+                tile = pl.ds(j, LANES)
+                value = pair_buf[slot, line, tile] + score[line, tile]
+                out_buf[slot, line, tile] = value
+                prob = jnp.exp(jnp.where(own == id_row[:, tile], value - log_sum, MASK_FILL))
+                p_high[line, tile], p_low[line, tile] = halves(prob)
+                grad = prob * d_prob[line, tile] + cot_buf[slot, line, tile]
+                grad_buf[slot, line, tile] = grad
+                g_high[line, tile], g_low[line, tile] = halves(grad)
+
+    def both(left, high, low, dims):
+        value = dot(left, high, dims) + dot(left, low, dims)
+        return value[0:8] + value[8:16]
+
+    def after(index, pair_of, part, there):
+        q_pair, k_pair, m_pair = pair_of
+        _, _, p_high, p_low, g_high, g_low = there
+        head = rows_of(index)
+        d_value = both(m_pair, p_high[:, part], p_low[:, part], NN)
+        d_key = both(q_pair, g_high[:, part], g_low[:, part], NN)
+        for n in range(part.start // rows, part.stop // rows):
+            span = slice(n * rows - part.start, (n + 1) * rows - part.start)
+            d_keys[n // 2, n % 2, head, :] = d_key[:, span]
+            d_values[n // 2, n % 2, head, :] = d_value[:, span]
+        return both(k_pair[:, part], g_high[:, part], g_low[:, part], NT)
+
+    def stage(index, carry):
+        slot = lax.rem(index, depth)
         for copy in inward(index):
             copy.wait()
 
@@ -301,58 +365,37 @@
             for copy in outward(index - depth):
                 copy.wait()
 
-        d_query = [None]
-
-        def before(part):
-            score[:, part] = dot(q_pack, k_pack[:, part], TN)
-            d_prob[:, part] = dot(m_pack, v_pack[:, part], TN)
-
-        def middle(part):
-            for s in range(rows // STRIP):
-                line = pl.ds(s * STRIP, STRIP)
-                own = id_column[line, :]
-                log_sum = log_sums[index, line, :]
-                for j in range(part.start, part.stop, LANES):
-                    tile = pl.ds(j, LANES)
-                    value = pair_buf[slot, line, tile] + score[line, tile]
-                    out_buf[slot, line, tile] = value
-                    prob = jnp.exp(jnp.where(own == id_row[:, tile], value - log_sum, MASK_FILL))
-                    p_high[line, tile], p_low[line, tile] = halves(prob)
-                    grad = prob * d_prob[line, tile] + cot_buf[slot, line, tile]
-                    grad_buf[slot, line, tile] = grad
-                    g_high[line, tile], g_low[line, tile] = halves(grad)
-
-        def after(part):
-            d_value = both(m_pair, p_high[:, part], p_low[:, part], NN)
-            d_key = both(q_pair, g_high[:, part], g_low[:, part], NN)
-            for n in range(part.start // rows, part.stop // rows):
-                span = slice(n * rows - part.start, (n + 1) * rows - part.start)
-                d_keys[n // 2, n % 2, head, :] = d_key[:, span]
-                d_values[n // 2, n % 2, head, :] = d_value[:, span]
-            term = both(k_pair[:, part], g_high[:, part], g_low[:, part], NT)
-            d_query[0] = term if d_query[0] is None else d_query[0] + term
-
-        parts = [slice(start, start + chunk) for start in range(0, cols, chunk)]
-        before(parts[0])
+        @pl.when(index == 0)
+        def _():
+            for n in range(2, depth - 1):
+                for copy in inward(n):
+                    copy.start()
+
+        @pl.when(index + depth - 1 < heads)
+        def _():
+            for copy in inward(index + depth - 1):
+                copy.start()
+
+        next_packs, own_pairs = packs(index), pairs(index)
+        d_query = None
+        before(next_packs, parts[0], here)
         for n, part in enumerate(parts):
             if n + 1 < len(parts):
-                before(parts[n + 1])
-            middle(part)
+                before(next_packs, parts[n + 1], here)
+            middle(index, slot, part, here)
             if n >= 1:
-                after(parts[n - 1])
-        after(parts[-1])
-        d_queries[head, :] = d_query[0] * (DH ** (-0.5))
+                term = after(index, own_pairs, parts[n - 1], here)
+                d_query = term if d_query is None else d_query + term
+        term = after(index, own_pairs, parts[-1], here)
+        d_query = term if d_query is None else d_query + term
+        d_queries[rows_of(index), :] = d_query * (DH ** (-0.5))
         for copy in outward(index):
             copy.start()
-
-        @pl.when(index + depth < heads)
-        def _():
-            for copy in inward(index + depth):
-                copy.start()
-
         return carry
 
-    lax.fori_loop(0, heads, step, 0)
+    lax.fori_loop(0, heads, stage, 0)
+    for result in results:
+        result.flush()
     for n in range(max(0, heads - depth), heads):
         for copy in outward(n):
             copy.wait()
@@ -363,47 +406,43 @@
     feats = heads * DH
     blocks = kept.shape[0]
     depth = 4
-    big = pl.BlockSpec(memory_space=pltpu.HBM)
-    flat = pl.BlockSpec((feats, rows), lambda n: (0, 0))
-    split = pl.BlockSpec((blocks // 2, 2, feats, rows), lambda n: (0, 0, 0, 0))
-    return pl.pallas_call(
+    split = (blocks // 2, 2, feats, rows)
+    wide, thin = pltpu.VMEM((rows, cols), F32), pltpu.VMEM((rows, cols), BF16)
+    return staged_call(
         attend_back_kernel,
-        grid=(1,),
-        in_specs=[
-            big, big, flat,
-            pl.BlockSpec((blocks, feats, rows), lambda n: (0, 0, 0)),
-            pl.BlockSpec((blocks, feats, rows), lambda n: (0, 1, 0)),
-            flat, flat,
-            pl.BlockSpec((heads, rows, LANES), lambda n: (0, 0, 0)),
-            pl.BlockSpec((rows, LANES), lambda n: (0, 0)),
-            pl.BlockSpec((STRIP, cols), lambda n: (0, 0)),
-        ],
-        out_specs=[big, big, flat, split, split],
-        out_shape=[
-            jax.ShapeDtypeStruct(pair.shape, F32),
-            jax.ShapeDtypeStruct(pair.shape, F32),
-            jax.ShapeDtypeStruct((feats, rows), F32),
-            jax.ShapeDtypeStruct((blocks // 2, 2, feats, rows), F32),
-            jax.ShapeDtypeStruct((blocks // 2, 2, feats, rows), F32),
-        ],
-        scratch_shapes=[pltpu.VMEM((depth, rows, cols), F32)] * 4
-        + [pltpu.VMEM((rows, cols), F32)] * 2
-        + [pltpu.VMEM((rows, cols), BF16)] * 4
-        + [pltpu.SemaphoreType.DMA((2, depth))] * 2,
-        compiler_params=pltpu.CompilerParams(vmem_limit_bytes=60 << 20),
-        cost_estimate=pl.CostEstimate(
+        "attend_back",
+        [queries, kept, d_mixed, mixed, id_column, id_row],
+        [(feats, rows), split, split],
+        [pltpu.VMEM((depth, rows, cols), F32)] * 2
+        + [pltpu.VMEM((depth, rows, LANES), F32)]
+        + [pltpu.VMEM((depth, rows, cols), F32)] * 2
+        + [wide] * 2
+        + [thin] * 4
+        + [pltpu.SemaphoreType.DMA((3, depth)), pltpu.SemaphoreType.DMA((2, depth))],
+        60,
+        raw=(pair, cot, log_sums),
+        raw_results=(pair.shape, pair.shape),
+        cost=pl.CostEstimate(
             flops=2 * 400 * heads * rows * cols,
             bytes_accessed=16 * heads * rows * cols,
             transcendentals=heads * rows * cols,
         ),
-        name="attend_back",
-    )(pair, cot, queries, kept, kept, mixed, d_mixed, log_sums, id_column, id_row)
+    )
 
 
 SMALL_LN1_GAIN, SMALL_LN1_BIAS, SMALL_LN2_GAIN, SMALL_LN2_BIAS = 0, 1, 2, 3
 SMALL_B_OUT, SMALL_B_DOWN, SMALL_PENALTY = 4, 5, 6
 SMALL_B_QUERY, SMALL_B_VALUE, SMALL_B_UP = 8, 9, 10
 SMALL_ROWS = 16
+
+
+def side_by_side(count, units, width):
+    beside = width // units
+    height = count // beside
+    return [
+        (slice(n * height, (n + 1) * height), slice(n * units, (n + 1) * units), slice(0, height))
+        for n in range(beside)
+    ]
 
 
 def team_device(team, core, chips):
@@ -417,9 +456,9 @@
     ) = operands
     (pair,) = raw
     (
-        queries, kept, id_column, log_sums, mixed, id_row, d_mixed, out_mine, d_hidden, up_share, down_share, small,
-    ) = results[:12]
-    parcels = results[12:]
+        queries, kept, id_column, log_sums, mixed, id_row, d_mixed, out_mine, d_hidden, shares, small,
+    ) = results[:11]
+    parcels = results[11:]
     (
         pair_buf, score, high, low, q_part, q_land, q_all, k_all, w_all, squares, mixed_all, hidden_two, down, normal_two, rate_two,
         part, landed, back, back_landed, ups_part, ups_sib, ups_go, ups_got, downs_part, downs_sib, downs_go, downs_got,
@@ -604,11 +643,6 @@
     copies.append(send(ups_part.at[:, other_core], ups_sib, sib_send.at[0], sib_recv.at[0], sibling))
     downs_part[...] = dot_halves(halves(act.T), cots).reshape(downs_part.shape)
     copies.append(send(downs_part.at[:, other_core], downs_sib, sib_send.at[1], sib_recv.at[1], sibling))
-    for n, source in enumerate(far):
-        for m, peer in enumerate(peers):
-            ready = k_all.at[source, peer]
-            arrived(ready, k_recv.at[source, peer])
-            copies.append(send(ready, ready, ks_send.at[n, m], k_recv.at[source, peer], sibling))
     down[...] = dot_halves(halves(act), downs)
     out_mine[...] = hidden_two[mine, :] + down[mine, :] + b_down[...]
     out_mine.flush()
@@ -626,6 +660,11 @@
             for n, peer in enumerate(far_teams)
         ]
         got[team] = go[team]
+    for n, source in enumerate(far):
+        for m, peer in enumerate(peers):
+            ready = k_all.at[source, peer]
+            arrived(ready, k_recv.at[source, peer])
+            copies.append(send(ready, ready, ks_send.at[n, m], k_recv.at[source, peer], sibling))
     for peer in peers:
         arrived(q_land.at[peer], q_recv.at[peer])
     for n in range(zs):
@@ -693,15 +732,20 @@
     small[SMALL_LN2_BIAS : SMALL_LN2_BIAS + 1, :] = column_sum(d_normed)
     small[SMALL_B_OUT : SMALL_B_OUT + 1, :] = column_sum(d_rows)
     small.flush()
+    for kind, got in enumerate([ups_got, downs_got]):
+        for peer in far_teams:
+            arrived(got.at[peer], g_recv.at[kind, peer])
+    up_share, down_share = [
+        functools.reduce(jnp.add, [got[n] for n in range(teams)]) for got in (ups_got, downs_got)
+    ]
+    for rows_of, columns_of, there in side_by_side(*up_share.shape, width):
+        shares[there, columns_of] = up_share[rows_of]
+    shares[there.stop :, :] = down_share
+    shares.flush()
     for peer in peers:
         arrived(back_landed.at[peer], back_recv.at[peer])
     d_mixed[...] = back_landed[...].reshape(rows, feats).T
     d_mixed.flush()
-    for kind, (got, result) in enumerate([(ups_got, up_share), (downs_got, down_share)]):
-        for peer in far_teams:
-            arrived(got.at[peer], g_recv.at[kind, peer])
-        result[...] = functools.reduce(jnp.add, [got[n] for n in range(teams)])
-        result.flush()
     for copy in copies:
         copy.wait_send()
 
@@ -731,7 +775,7 @@
         [
             (feats, rows), (blocks, 2 * feats + 8, rows), (rows, LANES), (heads, rows, LANES), (feats, rows),
             (STRIP, cols), (feats, rows), (piece, width), (piece, width),
-            (up_rows, units), (down_rows, width), (SMALL_ROWS, width),
+            (up_rows * units // width + down_rows, width), (SMALL_ROWS, width),
         ]
         + [(2 * piece, width)] * (zs - 1),
         [
@@ -774,9 +818,9 @@
 def finish_kernel(operands, results, scratch, raw):
     (
         d_keys, d_values, out_mine, d_hidden, d_queries, atoms, gain, bias, w_query, mixed, small_in, w_key, w_value,
-        up_share, down_share,
-    ) = operands[:15]
-    parcels = operands[15:]
+    ) = operands[:13]
+    parcels = operands[13 : 12 + lax.axis_size("head")]
+    chip_shares = operands[12 + lax.axis_size("head") :]
     grad_atoms, out_atoms, total_grads, grad_up, grad_down, small, penalty = results
     (
         sib_keys, sib_values, go_keys, go_values, got_keys, got_values,
@@ -812,6 +856,23 @@
         send(out_atoms.at[mine], out_atoms.at[mine], out_send.at[n], out_recv.at[z], {"head": peer})
         for n, peer in enumerate(peers)
     ]
+
+    def big_rows(result, source, kind):
+        count = result.shape[0] // (2 * teams)
+        return result.at[pl.ds(pl.multiple_of((source * 2 + kind) * count, 8), count)]
+
+    partners = others(dp, lax.axis_size("dp"))
+    for n in range(chips):
+        source = dp * chips + lax.rem(chip + chips - n, chips)
+        up_there, down_there = big_rows(grad_up, source, core), big_rows(grad_down, source, core)
+        for rows_of, columns_of, there in side_by_side(*up_there.shape, width):
+            up_there[rows_of, :] = chip_shares[n][there, columns_of]
+        down_there[...] = chip_shares[n][there.stop :, :]
+        for kind, ready in enumerate([up_there, down_there]):
+            copies += [
+                send(ready, ready, b_send.at[kind, n, m], b_recv.at[kind, source, core], {"dp": partner})
+                for m, partner in enumerate(partners)
+            ]
     own_keys, own_values = d_keys.ref, d_values.ref
     for kind, (sib, mine_too, go, got) in enumerate(
         [(sib_keys, own_keys, go_keys, got_keys), (sib_values, own_values, go_values, got_values)]
@@ -865,23 +926,6 @@
         for n, peer in enumerate(far_teams)
     ]
     got_grads[team] = go_grads[team]
-    bigs = [(up_share, grad_up), (down_share, grad_down)]
-
-    def big_rows(result, source, kind):
-        count = result.shape[0] // (2 * teams)
-        return result.at[pl.ds(pl.multiple_of((source * 2 + kind) * count, 8), count)]
-
-    for kind, (share_in, result) in enumerate(bigs):
-        ready = big_rows(result, team, core)
-        ready[...] = share_in[...]
-        copies.append(send(ready, ready, b_send.at[kind, 0], b_recv.at[kind, team, core], sibling))
-        copies += [
-            send(
-                ready, ready, b_send.at[kind, n + 1], b_recv.at[kind, team, core],
-                team_device(peer, core, chips),
-            )
-            for n, peer in enumerate(far_teams)
-        ]
     for peer in peers:
         arrived(landed.at[peer], part_recv.at[peer])
     d_normed = functools.reduce(jnp.add, [landed[n] for n in range(zs)])
@@ -920,11 +964,15 @@
         ready = total_grads.at[peer, core]
         arrived(ready, t_recv.at[peer, core])
         copies.append(send(ready, ready, f_send.at[n], t_recv.at[peer, core], sibling))
-    for kind, (_, result) in enumerate(bigs):
-        for n, peer in enumerate(far_teams):
-            ready = big_rows(result, peer, core)
-            arrived(ready, b_recv.at[kind, peer, core])
-            copies.append(send(ready, ready, bf_send.at[kind, n], b_recv.at[kind, peer, core], sibling))
+    for kind, result in enumerate([grad_up, grad_down]):
+        for n in range(teams):
+            ready = big_rows(result, n, core)
+
+            @pl.when(lax.div(n, chips) != dp)
+            def _(ready=ready, sem=b_recv.at[kind, n, core]):
+                arrived(ready, sem)
+
+            copies.append(send(ready, ready, bf_send.at[kind, n], b_recv.at[kind, n, core], sibling))
     for source in far_places:
         arrived(small_all.at[source], small_recv.at[source])
     summed = functools.reduce(jnp.add, [small_all[n] for n in range(2 * teams)])
@@ -934,9 +982,9 @@
     for peer in [team] + far_teams:
         arrived(total_grads.at[peer, other_core], t_recv.at[peer, other_core])
     total_grads.flush()
-    for kind, (_, result) in enumerate(bigs):
-        for peer in [team] + far_teams:
-            arrived(big_rows(result, peer, other_core), b_recv.at[kind, peer, other_core])
+    for kind, result in enumerate([grad_up, grad_down]):
+        for n in range(teams):
+            arrived(big_rows(result, n, other_core), b_recv.at[kind, n, other_core])
         result.flush()
     for peer in peers:
         there = pl.ds(pl.multiple_of(peer * piece, 8), piece)
@@ -949,9 +997,8 @@
         copy.wait_send()
 
 
-def finish(zs, dps, *operands):
+def finish(zs, dps, units, *operands):
     d_keys, atoms = operands[0], operands[5]
-    units = operands[14].shape[0] * 2 * dps * d_keys.shape[0]
     chips, _, feats, rows = d_keys.shape
     width = atoms.shape[1]
     piece = rows // zs
@@ -985,7 +1032,7 @@
             dma((zs,)), dma((zs,)),
             dma((teams,)), dma((teams,)),
             dma((teams,)), dma((teams, 2)), dma((teams,)),
-            dma((2, teams)), dma((2, teams, 2)), dma((2, teams)),
+            dma((2, chips, dps)), dma((2, teams, 2)), dma((2, teams)),
             dma((zs,)), dma((zs,)),
             dma((zs,)), dma((zs,)),
             dma((2 * teams,)), dma((2 * teams,)),
@@ -1046,8 +1093,7 @@
         return value.reshape(1, -1)
 
     (
-        queries, kept, id_column, log_sums, mixed, id_row, d_mixed, out_mine, d_hidden, up_share, down_share, small,
-        *parcels,
+        queries, kept, id_column, log_sums, mixed, id_row, d_mixed, out_mine, d_hidden, shares, small, *parcels,
     ) = front(
         zs, dps, dps * blocks // 2, pair,
         inputs, mol_ids, line(ln1_gain), line(ln1_bias), w_key, w_value, line(b_value), w_query, line(b_query),
@@ -1058,13 +1104,18 @@
         lax.ppermute(parcel, "head", [(source, (source + n + 1) % zs) for source in range(zs)])
         for n, parcel in enumerate(parcels)
     ]
+    chips = blocks // 2
+    chip_shares = [shares] + [
+        lax.ppermute(shares, "blk", [(2 * c + core, 2 * ((c + n) % chips) + core) for c in range(chips) for core in range(2)])
+        for n in range(1, chips)
+    ]
     out_pair, grad_pair, d_queries, d_keys, d_values = attend_back(
         pair, cot_pair, queries, kept, mixed, d_mixed, log_sums, id_column, id_row
     )
     grad_atoms, out_atoms, total_grads, grad_up, grad_down, small, penalty = finish(
-        zs, dps,
+        zs, dps, w_up.shape[1],
         d_keys, d_values, out_mine, d_hidden, d_queries, inputs, line(ln1_gain), line(ln1_bias), w_query, mixed,
-        small, w_key, w_value, up_share, down_share, *parcels,
+        small, w_key, w_value, *parcels, *chip_shares,
     )
     placed = place(
         w_query.shape[1], w_up.shape[1],

time: 144 us -> 139 us (0.965)
  Pallas kernels: 137 us -> 130 us
    pallas_call x1 -> x0, Pallas kernels: 28.3 us -> none  [attend_back(): pl.pallas_call(attend_back_kernel, grid=(1,), in_specs=[big, big, flat, p...]
    pallas_call x3 -> x4, Pallas kernels: 108 us -> 130 us  [staged_call(): pl.pallas_call(body, out_shape=[jax.ShapeDtypeStruct(value.shape, value.d...]
  transfers between devices with their start and end apart: 3 -> 4, of which waited for: 0 -> 0; matrix products, arithmetic and copies ran while one was open for 0% -> 0% of each run, Pallas kernels for 20% -> 19%
where the time goes in v6:
time: 139 us; the launch traced here: 138 us
  Pallas kernels  130 us (94%)
  starting transfers between devices  4.76 us (3%)
  between operations  2.52 us (2%)
    pallas_call x4, Pallas kernels, staged_call(): pl.pallas_call(body, out_shape=[jax.ShapeDtypeStruct(value.shape, value.d...  130 us
    ppermute x3, starting transfers between devices, local(): lax.ppermute(parcel, 'head', [(source, (source + n + 1) % zs) for source...  4.28 us
  transfers between devices with their start and end apart: 4, of which 0 were waited for; matrix products, arithmetic and copies ran while one was open for 0% of the time, Pallas kernels for 19%

profile of v6, /device:TPU:0, one launch (start us, length us, event | category | flops | bytes accessed | tf_op | source)
XLA Modules:
  0.0 138.4 jit_solution(3026815423988251980)
XLA Ops:
  0.7 60.4 %front.1 = (f32[128,256]{1,0:T(8,128)}, f32[4,264,256]{2,1,0:T(8,128)}, f32[256,128]{1,0:T(8,128)}, f32[16,256,128]{2,1,0:T(8,128)}, f32[128,256]{1,0:T(8,128)},...) custom-call(f32[256,512]{1,0:T(8,128)} %bitcast.23, ...), custom_call_target="tpu_custom_call" | custom-call | tf_op jit(solution)/shard_map/front/pallas_call | solution.py:164
  61.1 0.8 collective-permute-start
  61.9 2.3 %collective-permute-start.1 = (f32[128,512]{1,0:T(8,128)}, f32[128,512]{1,0:T(8,128)S(1)}, u32[]{:S(2)}, u32[]{:S(2)}) collective-permute-start(f32[128,512]{1,0:T(8,128)} %get-tuple-element.77), channel_id=1, source_target_pairs={{0,4},{2,6},{4,0},{6,2},{1,5},{3,7},{5,1},{7,3},{8,12},{10,14},{12... | collective-permute-start | bytes 786440 | tf_op jit(solution)/shard_map/ppermute | solution.py:1104
  64.2 1.1 collective-permute-start.2
  65.4 0.5 collective-permute-start.3
  65.8 26.5 %attend_back.1 = (f32[1,16,256,1024]{3,2,1,0:T(8,128)}, f32[1,16,256,1024]{3,2,1,0:T(8,128)}, f32[128,256]{1,0:T(8,128)}, f32[2,2,128,256]{3,2,1,0:T(8,128)}, f32[2,2,128,256]{3,2,1,0:T(8,128)}) custom-call(f32[128,256]{1,0:T(8,128)} %get-tuple-element.63.refs_0_, f32[4,264,256]{2,1,0:T(8,128)} %get-tuple-element.64.refs_1_, ...), custom_call_target="tpu_custom_call" | custom-call | flops 3355443200 | bytes 67108864 | tf_op jit(solution)/shard_map/attend_back/pallas_call | solution.py:164
  92.4 0.0 collective-permute-done.refs_13_
  92.4 0.0 copy-start
  92.4 0.0 collective-permute-done.1.refs_14_
  92.4 0.0 copy-start.1
  92.4 0.0 collective-permute-done.2.refs_15_
  92.4 0.0 copy-start.2
  92.4 0.0 collective-permute-done.3.refs_17_
  92.4 0.0 copy-start.3
  92.4 0.6 copy-done
  93.1 0.1 copy-done.1
  93.2 0.1 copy-done.2
  93.2 0.1 copy-done.3
  93.3 39.1 %finish.1 = (f32[256,512]{1,0:T(8,128)}, f32[256,512]{1,0:T(8,128)}, f32[4,2,64,512]{3,2,1,0:T(8,128)}, f32[512,512]{1,0:T(8,128)}, f32[512,512]{1,0:T(8,128)}, /*index=5*/f32[16,512]{1,0:T(8,128)}, f32[1,1]{1,0:T(1,128)}) custom-call(f32[2,2,128,256]{3,2,1,0:T(8,128)} %get-tuple-element.70.refs_0_, f32[2,2,128,256]{3,2,1,0:T(8,128)} %get-tuple-element.71.refs_1_, ...), custom_call_target="tpu_custom_call" | custom-call | tf_op jit(solution)/shard_map/finish/pallas_call | solution.py:164
  132.5 4.2 %place.1 = (f32[256,512]{1,0:T(8,128)}, f32[256,512]{1,0:T(8,128)}, f32[512,512]{1,0:T(8,128)}, f32[512,512]{1,0:T(8,128)}, f32[512,128]{1,0:T(8,128)}, /*index=...) custom-call(f32[4,2,64,512]{3,2,1,0:T(8,128)} %get-tuple-element.80., ...), custom_call_target="tpu_custom_call" | custom-call | tf_op jit(solution)/shard_map/place/pallas_call | solution.py:164
Async XLA Ops:
  61.1 31.3 %collective-permute-start = (f32[128,512]{1,0:T(8,128)}, f32[128,512]{1,0:T(8,128)S(1)}, u32[]{:S(2)}, u32[]{:S(2)}) collective-permute-start(f32[128,512]{1,0:T(8,128)} %get-tuple-element.76), channel_id=1, source_target_pairs={{0,2},{2,4},{4,6},{6,0},{1,3},{3,5},{5,7},{7,1},{8,10},{10,12},{12... | collective-permute-start | bytes 786440 | tf_op jit(solution)/shard_map/ppermute | solution.py:1104
  61.9 30.5 %collective-permute-start.1 = (f32[128,512]{1,0:T(8,128)}, f32[128,512]{1,0:T(8,128)S(1)}, u32[]{:S(2)}, u32[]{:S(2)}) collective-permute-start(f32[128,512]{1,0:T(8,128)} %get-tuple-element.77), channel_id=1, source_target_pairs={{0,4},{2,6},{4,0},{6,2},{1,5},{3,7},{5,1},{7,3},{8,12},{10,14},{12... | collective-permute-start | bytes 786440 | tf_op jit(solution)/shard_map/ppermute | solution.py:1104
  64.2 28.2 %collective-permute-start.2 = (f32[128,512]{1,0:T(8,128)}, f32[128,512]{1,0:T(8,128)S(1)}, u32[]{:S(2)}, u32[]{:S(2)}) collective-permute-start(f32[128,512]{1,0:T(8,128)} %get-tuple-element.78), channel_id=1, source_target_pairs={{0,6},{2,0},{4,2},{6,4},{1,7},{3,1},{5,3},{7,5},{8,14},{10,8},{12,... | collective-permute-start | bytes 786440 | tf_op jit(solution)/shard_map/ppermute | solution.py:1104
  65.4 27.1 %collective-permute-start.3 = (f32[128,512]{1,0:T(8,128)}, f32[128,512]{1,0:T(8,128)S(1)}, u32[]{:S(2)}, u32[]{:S(2)}) collective-permute-start(f32[128,512]{1,0:T(8,128)} %get-tuple-element.79.refs_16_), channel_id=1, source_target_pairs={{0,16},{8,24},{16,0},{24,8},{1,17},{9,25},{17,1},{25,9},{2,18},{10... | collective-permute-start | bytes 786440 | tf_op jit(solution)/shard_map/ppermute | solution.py:1109
  92.4 0.7 copy-start
  92.4 0.8 copy-start.1
  92.4 0.8 copy-start.2
  92.4 0.9 copy-start.3

commit v7 on v6

--- a/solution.py
+++ b/solution.py
@@ -13,6 +13,7 @@
 STRIP = 16
 CHUNK = 256
 GROUP = 2
+FRONT_MB, BACK_MB, FINISH_MB, PLACE_MB = 58, 60, 40, 32
 NORM_EPS = 1e-05
 MASK_FILL = -1e30
 F32 = jnp.float32
@@ -97,8 +98,9 @@
 class Operand:
     def __init__(self, source, slot, sem):
         self.source, self.slot, self.shape = source, slot, slot.shape
-        self.copy = pltpu.make_async_copy(source, slot, sem)
-        self.copy.start()
+        self.copy = None if sem is None else pltpu.make_async_copy(source, slot, sem)
+        if self.copy is not None:
+            self.copy.start()
 
     @property
     def ref(self):
@@ -114,8 +116,8 @@
 class Result:
     def __init__(self, target, slot, sem):
         self.slot, self.shape, self.at = slot, slot.shape, slot.at
-        self.copy = pltpu.make_async_copy(slot, target, sem)
-        self.begun = False
+        self.copy = None if sem is None else pltpu.make_async_copy(slot, target, sem)
+        self.begun = self.copy is None
 
     def __setitem__(self, index, value):
         self.slot[index] = value
@@ -129,9 +131,14 @@
             self.begun = True
 
 
-def staged_call(kernel, name, operands, results, scratch, megabytes, remote=None, raw=(), straight=(), raw_results=(), cost=None):
+def staged_call(
+    kernel, name, operands, results, scratch, megabytes,
+    remote=None, raw=(), straight=(), raw_results=(), cost=None, near_in=(), near_out=(), near_straight=False,
+):
     n_in, n_out, n_raw, n_straight = len(operands), len(results), len(raw), len(straight)
     n_left = len(raw_results)
+    far_in = [n for n in range(n_in) if n not in near_in]
+    far_out = [n for n in range(n_out) if n not in near_out]
 
     def body(*refs):
         sources, left, refs = refs[:n_in], refs[n_in : n_in + n_raw], refs[n_in + n_raw :]
@@ -139,39 +146,51 @@
         arrays, refs = refs[:n_straight], refs[n_straight:]
         left, refs = left + refs[:n_left], refs[n_left:]
         targets, refs = refs[:n_out], refs[n_out:]
-        slots, made, refs = refs[:n_in], refs[n_in : n_in + n_out], refs[n_in + n_out :]
+        in_slots, refs = dict(zip(far_in, refs)), refs[len(far_in) :]
+        out_slots, refs = dict(zip(far_out, refs)), refs[len(far_out) :]
         in_sem, out_sem, move_sem, refs = refs[0], refs[1], refs[2], refs[3:]
-        through, refs = refs[:n_straight], refs[n_straight:]
-        loads = [pltpu.make_async_copy(moved[n], through[n], move_sem.at[n]) for n in range(n_straight)]
+        through, loads = moved, []
+        if not near_straight:
+            through, refs = refs[:n_straight], refs[n_straight:]
+            loads = [pltpu.make_async_copy(moved[n], through[n], move_sem.at[n]) for n in range(n_straight)]
         moves = [pltpu.make_async_copy(through[n], arrays[n], move_sem.at[n]) for n in range(n_straight)]
         for load in loads:
             load.start()
-        ins = [Operand(sources[n], slots[n], in_sem.at[n]) for n in range(n_in)]
-        outs = [Result(targets[n], made[n], out_sem.at[n]) for n in range(n_out)]
-        for load, move in zip(loads, moves, strict=True):
+        ins = [
+            Operand(sources[n], in_slots.get(n, sources[n]), in_sem.at[n] if n in in_slots else None)
+            for n in range(n_in)
+        ]
+        outs = [
+            Result(targets[n], out_slots.get(n, targets[n]), out_sem.at[n] if n in out_slots else None)
+            for n in range(n_out)
+        ]
+        for load in loads:
             load.wait()
+        for move in moves:
             move.start()
         kernel(ins, outs, refs, left)
         for operand in ins:
             operand.ref
         for result in outs:
             result.flush()
-        for copy in moves + [result.copy for result in outs]:
+        for copy in moves + [result.copy for result in outs if result.copy is not None]:
             copy.wait()
 
-    anywhere = pl.BlockSpec(memory_space=pltpu.HBM)
+    hbm, vmem = pl.BlockSpec(memory_space=pltpu.HBM), pl.BlockSpec(memory_space=pltpu.VMEM)
     extra = {} if remote is None else {"collective_id": remote, "has_side_effects": True}
     return pl.pallas_call(
         body,
         out_shape=[jax.ShapeDtypeStruct(value.shape, value.dtype) for value in straight]
         + [jax.ShapeDtypeStruct(shape, F32) for shape in raw_results]
         + [jax.ShapeDtypeStruct(shape, F32) for shape in results],
-        in_specs=[anywhere] * (n_in + n_raw + n_straight),
-        out_specs=[anywhere] * (n_straight + n_left + n_out),
-        scratch_shapes=[pltpu.VMEM(value.shape, value.dtype) for value in operands]
-        + [pltpu.VMEM(shape, F32) for shape in results]
-        + [pltpu.SemaphoreType.DMA((n,)) for n in (n_in, n_out, max(1, n_straight))]
-        + [pltpu.VMEM(value.shape, value.dtype) for value in straight]
+        in_specs=[vmem if n in near_in else hbm for n in range(n_in)]
+        + [hbm] * n_raw
+        + [vmem if near_straight else hbm] * n_straight,
+        out_specs=[hbm] * (n_straight + n_left) + [vmem if n in near_out else hbm for n in range(n_out)],
+        scratch_shapes=[pltpu.VMEM(operands[n].shape, operands[n].dtype) for n in far_in]
+        + [pltpu.VMEM(results[n], F32) for n in far_out]
+        + [pltpu.SemaphoreType.DMA((max(1, n),)) for n in (n_in, n_out, n_straight)]
+        + ([] if near_straight else [pltpu.VMEM(value.shape, value.dtype) for value in straight])
         + list(scratch),
         compiler_params=pltpu.CompilerParams(vmem_limit_bytes=megabytes << 20, **extra),
         cost_estimate=cost,
@@ -257,7 +276,7 @@
 
 def attend_back_kernel(operands, results, scratch, raw):
     queries, kept, d_mixed, mixed, id_column, id_row = operands
-    d_queries, d_keys, d_values = results
+    (d_heads,) = results
     pair, cot, log_sums, out_pair, grad_pair = raw
     pair_buf, cot_buf, log_buf, out_buf, grad_buf = scratch[:5]
     here = scratch[5:11]
@@ -296,9 +315,11 @@
     def key_rows(index):
         return joined(kept[n, rows_of(index), :] for n in range(blocks))
 
+    def value_row(index):
+        return pl.ds(pl.multiple_of(feats + index * 8, 8), 8)
+
     def value_rows(index):
-        some = pl.ds(pl.multiple_of(feats + index * 8, 8), 8)
-        return joined(kept[n, some, :] for n in range(blocks))
+        return joined(kept[n, value_row(index), :] for n in range(blocks))
 
     def packs(index):
         head = rows_of(index)
@@ -351,8 +372,8 @@
         d_key = both(q_pair, g_high[:, part], g_low[:, part], NN)
         for n in range(part.start // rows, part.stop // rows):
             span = slice(n * rows - part.start, (n + 1) * rows - part.start)
-            d_keys[n // 2, n % 2, head, :] = d_key[:, span]
-            d_values[n // 2, n % 2, head, :] = d_value[:, span]
+            d_heads[n // 2, n % 2, head, :] = d_key[:, span]
+            d_heads[n // 2, n % 2, value_row(index), :] = d_value[:, span]
         return both(k_pair[:, part], g_high[:, part], g_low[:, part], NT)
 
     def stage(index, carry):
@@ -388,7 +409,7 @@
                 d_query = term if d_query is None else d_query + term
         term = after(index, own_pairs, parts[-1], here)
         d_query = term if d_query is None else d_query + term
-        d_queries[rows_of(index), :] = d_query * (DH ** (-0.5))
+        d_heads[blocks // 2, 0, rows_of(index), :] = d_query * (DH ** (-0.5))
         for copy in outward(index):
             copy.start()
         return carry
@@ -406,20 +427,19 @@
     feats = heads * DH
     blocks = kept.shape[0]
     depth = 4
-    split = (blocks // 2, 2, feats, rows)
     wide, thin = pltpu.VMEM((rows, cols), F32), pltpu.VMEM((rows, cols), BF16)
     return staged_call(
         attend_back_kernel,
         "attend_back",
         [queries, kept, d_mixed, mixed, id_column, id_row],
-        [(feats, rows), split, split],
+        [(blocks // 2 + 1, 2, 2 * feats, rows)],
         [pltpu.VMEM((depth, rows, cols), F32)] * 2
         + [pltpu.VMEM((depth, rows, LANES), F32)]
         + [pltpu.VMEM((depth, rows, cols), F32)] * 2
         + [wide] * 2
         + [thin] * 4
         + [pltpu.SemaphoreType.DMA((3, depth)), pltpu.SemaphoreType.DMA((2, depth))],
-        60,
+        BACK_MB,
         raw=(pair, cot, log_sums),
         raw_results=(pair.shape, pair.shape),
         cost=pl.CostEstimate(
@@ -809,7 +829,7 @@
             dma((2,)), dma((2,)),
             dma((2, teams)), dma((2, teams)),
         ],
-        58,
+        FRONT_MB,
         remote=0,
         raw=(pair,),
     )
@@ -817,10 +837,10 @@
 
 def finish_kernel(operands, results, scratch, raw):
     (
-        d_keys, d_values, out_mine, d_hidden, d_queries, atoms, gain, bias, w_query, mixed, small_in, w_key, w_value,
-    ) = operands[:13]
-    parcels = operands[13 : 12 + lax.axis_size("head")]
-    chip_shares = operands[12 + lax.axis_size("head") :]
+        d_heads, out_mine, d_hidden, atoms, gain, bias, w_query, mixed, small_in, w_key, w_value,
+    ) = operands[:11]
+    parcels = operands[11 : 10 + lax.axis_size("head")]
+    chip_shares = operands[10 + lax.axis_size("head") :]
     grad_atoms, out_atoms, total_grads, grad_up, grad_down, small, penalty = results
     (
         sib_keys, sib_values, go_keys, go_values, got_keys, got_values,
@@ -829,7 +849,7 @@
         g_send, g_recv, t_send, t_recv, f_send, b_send, b_recv, bf_send, out_send, out_recv,
         small_z_send, small_z_recv, small_send, small_recv,
     ) = scratch
-    chips, _, feats, rows = d_keys.shape
+    chips, feats, rows = d_heads.shape[0] - 1, d_heads.shape[2] // 2, d_heads.shape[3]
     zs, piece, width = part.shape
     teams, _, share, _ = grads.shape
     blk, z, dp = lax.axis_index("blk"), lax.axis_index("head"), lax.axis_index("dp")
@@ -847,8 +867,11 @@
     greet(meeting)
     meet(meeting)
     copies = [
-        send(d_keys.source.at[:, other_core], sib_keys, sib_send.at[0], sib_recv.at[0], sibling),
-        send(d_values.source.at[:, other_core], sib_values, sib_send.at[1], sib_recv.at[1], sibling),
+        send(
+            d_heads.source.at[pl.ds(0, chips), other_core, pl.ds(kind * feats, feats)],
+            sib, sib_send.at[kind], sib_recv.at[kind], sibling,
+        )
+        for kind, sib in enumerate([sib_keys, sib_values])
     ]
     mine = pl.ds(pl.multiple_of(z * piece, 8), piece)
     out_atoms[mine, :] = functools.reduce(jnp.add, [parcel[0:piece, :] for parcel in parcels], out_mine[...])
@@ -873,12 +896,11 @@
                 send(ready, ready, b_send.at[kind, n, m], b_recv.at[kind, source, core], {"dp": partner})
                 for m, partner in enumerate(partners)
             ]
-    own_keys, own_values = d_keys.ref, d_values.ref
-    for kind, (sib, mine_too, go, got) in enumerate(
-        [(sib_keys, own_keys, go_keys, got_keys), (sib_values, own_values, go_values, got_values)]
-    ):
+    own_heads = d_heads.ref
+    d_queries = own_heads[chips, 0, 0:feats, :]
+    for kind, (sib, go, got) in enumerate([(sib_keys, go_keys, got_keys), (sib_values, go_values, got_values)]):
         arrived(sib, sib_recv.at[kind])
-        go[...] = sib[...] + mine_too[:, core]
+        go[...] = sib[...] + own_heads[0:chips, core, kind * feats : (kind + 1) * feats, :]
         copies += [
             send(
                 go.at[peer], got.at[chip], kv_send.at[kind, n], kv_recv.at[kind, chip],
@@ -890,9 +912,9 @@
     got_values[chip] = go_values[chip]
     normal, rate = normalize(atoms[...])
     normed = halves(normal * gain[...] + bias[...])
-    dq_rows = d_queries[...].T
+    dq_rows = d_queries.T
     d_normed = dot_full(dq_rows, w_query[...], NT)
-    grad_q = dot_halves(halves(d_queries[...]), normed)
+    grad_q = dot_halves(halves(d_queries), normed)
     small_z[z] = small_in[0:8, :]
     hidden_all[z] = d_hidden[...]
     for n, parcel in enumerate(parcels):
@@ -998,8 +1020,8 @@
 
 
 def finish(zs, dps, units, *operands):
-    d_keys, atoms = operands[0], operands[5]
-    chips, _, feats, rows = d_keys.shape
+    d_heads, atoms = operands[0], operands[3]
+    chips, feats, rows = d_heads.shape[0] - 1, d_heads.shape[2] // 2, d_heads.shape[3]
     width = atoms.shape[1]
     piece = rows // zs
     teams = dps * chips
@@ -1037,14 +1059,17 @@
             dma((zs,)), dma((zs,)),
             dma((2 * teams,)), dma((2 * teams,)),
         ],
-        58,
+        FINISH_MB,
         remote=2,
+        near_in=[0] + list(range(11, len(operands))),
+        near_out=range(7),
     )
 
 
 def place_kernel(operands, results, scratch, raw):
-    total_grads, small = operands
-    grad_query, grad_key, grad_value, grad_out = results[:4]
+    total_grads, small, penalty_in = operands
+    penalty, grad_query, grad_key, grad_value, grad_out = results[:5]
+    penalty[...] = penalty_in[...]
     feats, width = grad_out.shape
     done = total_grads[...].reshape(4 * feats, width)
     grad_query[...] = done[0:feats].T
@@ -1055,7 +1080,7 @@
     grad_value.flush()
     grad_out[...] = done[3 * feats :]
     grad_out.flush()
-    for result, row in zip(results[4:], SMALL_OUTPUTS, strict=True):
+    for result, row in zip(results[5:], SMALL_OUTPUTS, strict=True):
         result[...] = small[row : row + 1, 0 : result.shape[1]]
 
 
@@ -1072,12 +1097,15 @@
         place_kernel,
         "place",
         operands,
-        [(width, feats)] * 3
+        [(1, 1)]
+        + [(width, feats)] * 3
         + [(feats, width)]
         + [(1, lengths.get(row, width)) for row in SMALL_OUTPUTS],
         [],
-        58,
+        PLACE_MB,
         straight=straight,
+        near_in=(0, 1, 2),
+        near_straight=True,
     )
 
 
@@ -1109,24 +1137,24 @@
         lax.ppermute(shares, "blk", [(2 * c + core, 2 * ((c + n) % chips) + core) for c in range(chips) for core in range(2)])
         for n in range(1, chips)
     ]
-    out_pair, grad_pair, d_queries, d_keys, d_values = attend_back(
+    out_pair, grad_pair, d_heads = attend_back(
         pair, cot_pair, queries, kept, mixed, d_mixed, log_sums, id_column, id_row
     )
     grad_atoms, out_atoms, total_grads, grad_up, grad_down, small, penalty = finish(
         zs, dps, w_up.shape[1],
-        d_keys, d_values, out_mine, d_hidden, d_queries, inputs, line(ln1_gain), line(ln1_bias), w_query, mixed,
+        d_heads, out_mine, d_hidden, inputs, line(ln1_gain), line(ln1_bias), w_query, mixed,
         small, w_key, w_value, *parcels, *chip_shares,
     )
     placed = place(
         w_query.shape[1], w_up.shape[1],
         [grad_atoms, out_atoms, grad_up, grad_down],
-        total_grads, small,
-    )
-    grad_atoms, out_atoms, grad_up, grad_down, grad_query, grad_key, grad_value, grad_out = placed[:8]
+        total_grads, small, penalty,
+    )
+    grad_atoms, out_atoms, grad_up, grad_down, penalty, grad_query, grad_key, grad_value, grad_out = placed[:9]
     (
         grad_ln1_gain, grad_ln1_bias, grad_b_query, grad_b_value, grad_b_out, grad_ln2_gain, grad_ln2_bias,
         grad_b_up, grad_b_down,
-    ) = [value.reshape(-1) for value in placed[8:]]
+    ) = [value.reshape(-1) for value in placed[9:]]
     return (
         out_atoms[None],
         out_pair,

time: 139 us -> 138 us (level)
  between operations: 2.52 us -> 1.03 us
where the time goes in v7:
time: 138 us; the launch traced here: 137 us
  Pallas kernels  130 us (94%)
  starting transfers between devices  4.76 us (3%)
  local copies, waits for them, and re-layouts  1.45 us (1%)
    pallas_call x4, Pallas kernels, staged_call(): pl.pallas_call(body, out_shape=[jax.ShapeDtypeStruct(value.shape, value.d...  130 us
    ppermute x3, starting transfers between devices, local(): lax.ppermute(parcel, 'head', [(source, (source + n + 1) % zs) for source...  4.28 us
  transfers between devices with their start and end apart: 4, of which 0 were waited for; matrix products, arithmetic and copies ran while one was open for 0% of the time, Pallas kernels for 19%

profile of v7, /device:TPU:0, one launch (start us, length us, event | category | flops | bytes accessed | tf_op | source)
XLA Modules:
  0.0 136.9 jit_solution(11274479869137363932)
XLA Ops:
  0.7 60.4 %front.1 = (f32[128,256]{1,0:T(8,128)}, f32[4,264,256]{2,1,0:T(8,128)}, f32[256,128]{1,0:T(8,128)}, f32[16,256,128]{2,1,0:T(8,128)}, f32[128,256]{1,0:T(8,128)},...) custom-call(f32[256,512]{1,0:T(8,128)} %bitcast.23, ...), custom_call_target="tpu_custom_call" | custom-call | tf_op jit(solution)/shard_map/front/pallas_call | solution.py:181
  61.1 0.9 collective-permute-start
  61.9 2.3 %collective-permute-start.1 = (f32[128,512]{1,0:T(8,128)}, f32[128,512]{1,0:T(8,128)S(1)}, u32[]{:S(2)}, u32[]{:S(2)}) collective-permute-start(f32[128,512]{1,0:T(8,128)} %get-tuple-element.74), channel_id=1, source_target_pairs={{0,4},{2,6},{4,0},{6,2},{1,5},{3,7},{5,1},{7,3},{8,12},{10,14},{12... | collective-permute-start | bytes 786440 | tf_op jit(solution)/shard_map/ppermute | solution.py:1132
  64.2 1.1 collective-permute-start.2
  65.3 0.5 collective-permute-start.3
  65.8 0.0 copy-start
  65.8 0.0 copy-start.2
  65.8 0.0 copy-start.3
  65.8 0.0 copy-start.4
  65.8 0.0 copy-start.5
  65.8 0.0 copy-start.6
  65.8 0.0 copy-start.7
  65.9 0.0 copy-start.8
  65.9 0.0 copy-start.9
  65.9 0.0 copy-start.10
  65.9 0.0 copy-start.11
  65.9 26.7 %attend_back.1 = (f32[1,16,256,1024]{3,2,1,0:T(8,128)}, f32[1,16,256,1024]{3,2,1,0:T(8,128)}, f32[3,2,256,256]{3,2,1,0:T(8,128)}) custom-call(f32[128,256]{1,0:T(8,128)} %get-tuple-element.62.refs_0_, f32[4,264,256]{2,1,0:T(8,128)} %get-tuple-element.63.refs_1_, f32[128,256]{1,0:T(8,128)} %get-tuple-element.64.refs_2_, ...), custom_call_target="tpu_custom_call" | custom-call | flops 3355443200 | bytes 67108864 | tf_op jit(solution)/shard_map/attend_back/pallas_call | solution.py:181
  92.6 0.0 collective-permute-done.refs_11_
  92.6 0.0 collective-permute-done.1.refs_12_
  92.6 0.0 collective-permute-done.2.refs_13_
  92.6 0.0 collective-permute-done.3.refs_15_
  92.6 0.0 copy-done
  92.6 0.0 copy-done.2
  92.7 0.0 copy-done.3
  92.7 0.0 copy-done.4
  92.7 0.0 copy-done.5
  92.7 0.0 copy-done.6
  92.7 0.0 copy-done.7
  92.7 0.0 copy-done.8
  92.7 0.0 copy-done.9
  92.7 0.0 copy-done.10
  92.7 0.0 copy-done.11
  92.7 0.0 copy-start.1
  92.8 1.4 %copy-done.1 = f32[3,2,256,256]{3,2,1,0:T(8,128)S(1)} copy-done((f32[3,2,256,256]{3,2,1,0:T(8,128)S(1)}, f32[3,2,256,256]{3,2,1,0:T(8,128)}, u32[]{:S(2)}) %copy-start.1) | copy-done | bytes 1572888
  94.2 39.6 %finish.1 = (f32[256,512]{1,0:T(8,128)S(1)}, f32[256,512]{1,0:T(8,128)S(1)}, f32[4,2,64,512]{3,2,1,0:T(8,128)S(1)}, f32[512,512]{1,0:T(8,128)S(1)}, f32[512,512]...) custom-call(f32[3,2,256,256]{3,2,1,0:T(8,128)S(1)} %copy-done.1, f32[64,512]{1,0:T(8,128)S(1)} %copy-done.7, ...), custom_call_target="tpu_custom_call" | custom-call | tf_op jit(solution)/shard_map/finish/pallas_call | solution.py:181
  133.8 3.0 %place.1 = (f32[256,512]{1,0:T(8,128)}, f32[256,512]{1,0:T(8,128)}, f32[512,512]{1,0:T(8,128)}, f32[512,512]{1,0:T(8,128)}, f32[1,1]{1,0:T(1,128)}, /*index=5*/f...) custom-call(f32[4,2,64,512]{3,2,1,0:T(8,128)S(1)} %get-tuple-element, ...), custom_call_target="tpu_custom_call" | custom-call | tf_op jit(solution)/shard_map/place/pallas_call | solution.py:181
Async XLA Ops:
  61.1 31.5 %collective-permute-start = (f32[128,512]{1,0:T(8,128)}, f32[128,512]{1,0:T(8,128)S(1)}, u32[]{:S(2)}, u32[]{:S(2)}) collective-permute-start(f32[128,512]{1,0:T(8,128)} %get-tuple-element.73), channel_id=1, source_target_pairs={{0,2},{2,4},{4,6},{6,0},{1,3},{3,5},{5,7},{7,1},{8,10},{10,12},{12... | collective-permute-start | bytes 786440 | tf_op jit(solution)/shard_map/ppermute | solution.py:1132
  61.9 30.7 %collective-permute-start.1 = (f32[128,512]{1,0:T(8,128)}, f32[128,512]{1,0:T(8,128)S(1)}, u32[]{:S(2)}, u32[]{:S(2)}) collective-permute-start(f32[128,512]{1,0:T(8,128)} %get-tuple-element.74), channel_id=1, source_target_pairs={{0,4},{2,6},{4,0},{6,2},{1,5},{3,7},{5,1},{7,3},{8,12},{10,14},{12... | collective-permute-start | bytes 786440 | tf_op jit(solution)/shard_map/ppermute | solution.py:1132
  64.2 28.4 %collective-permute-start.2 = (f32[128,512]{1,0:T(8,128)}, f32[128,512]{1,0:T(8,128)S(1)}, u32[]{:S(2)}, u32[]{:S(2)}) collective-permute-start(f32[128,512]{1,0:T(8,128)} %get-tuple-element.75), channel_id=1, source_target_pairs={{0,6},{2,0},{4,2},{6,4},{1,7},{3,1},{5,3},{7,5},{8,14},{10,8},{12,... | collective-permute-start | bytes 786440 | tf_op jit(solution)/shard_map/ppermute | solution.py:1132
  65.3 27.3 %collective-permute-start.3 = (f32[128,512]{1,0:T(8,128)}, f32[128,512]{1,0:T(8,128)S(1)}, u32[]{:S(2)}, u32[]{:S(2)}) collective-permute-start(f32[128,512]{1,0:T(8,128)} %get-tuple-element.76.refs_14_), channel_id=1, source_target_pairs={{0,16},{8,24},{16,0},{24,8},{1,17},{9,25},{17,1},{25,9},{2,18},{10... | collective-permute-start | bytes 786440 | tf_op jit(solution)/shard_map/ppermute | solution.py:1137
  65.8 26.8 %copy-start = (f32[1,256,512]{2,1,0:T(8,128)S(1)}, f32[1,256,512]{2,1,0:T(8,128)}, u32[]{:S(2)}) copy-start(f32[1,256,512]{2,1,0:T(8,128)} %param.20) | copy-start | bytes 1572868
  65.8 26.8 %copy-start.2 = (f32[512,128]{1,0:T(8,128)S(1)}, f32[512,128]{1,0:T(8,128)}, u32[]{:S(2)}) copy-start(f32[512,128]{1,0:T(8,128)} %refs_9_.3) | copy-start | bytes 786436
  65.8 26.8 %copy-start.3 = (f32[512,128]{1,0:T(8,128)S(1)}, f32[512,128]{1,0:T(8,128)}, u32[]{:S(2)}) copy-start(f32[512,128]{1,0:T(8,128)} %refs_10_.1) | copy-start | bytes 786436
  65.8 26.8 %copy-start.4 = (f32[512,128]{1,0:T(8,128)S(1)}, f32[512,128]{1,0:T(8,128)}, u32[]{:S(2)}) copy-start(f32[512,128]{1,0:T(8,128)} %refs_6_.3) | copy-start | bytes 786436
  65.8 26.9 %copy-start.5 = (f32[128,256]{1,0:T(8,128)S(1)}, f32[128,256]{1,0:T(8,128)}, u32[]{:S(2)}) copy-start(f32[128,256]{1,0:T(8,128)} %get-tuple-element.65.refs_3_.refs_7_) | copy-start | bytes 393220
  65.8 26.9 %copy-start.6 = (f32[128,512]{1,0:T(8,128)S(1)}, f32[128,512]{1,0:T(8,128)}, u32[]{:S(2)}) copy-start(f32[128,512]{1,0:T(8,128)} %get-tuple-element.76.refs_14_) | copy-start | bytes 786436
  65.8 26.9 %copy-start.7 = (f32[64,512]{1,0:T(8,128)S(1)}, f32[64,512]{1,0:T(8,128)}, u32[]{:S(2)}) copy-start(f32[64,512]{1,0:T(8,128)} %get-tuple-element.70.refs_1_) | copy-start | bytes 393220
  65.9 26.9 %copy-start.8 = (f32[64,512]{1,0:T(8,128)S(1)}, f32[64,512]{1,0:T(8,128)}, u32[]{:S(2)}) copy-start(f32[64,512]{1,0:T(8,128)} %get-tuple-element.71.refs_2_) | copy-start | bytes 393220
  65.9 26.9 %copy-start.9 = (f32[16,512]{1,0:T(8,128)S(1)}, f32[16,512]{1,0:T(8,128)}, u32[]{:S(2)}) copy-start(f32[16,512]{1,0:T(8,128)} %get-tuple-element.72.refs_8_) | copy-start | bytes 98308
  65.9 26.9 %copy-start.10 = (f32[512]{0:T(512)S(1)}, f32[512]{0:T(512)}, u32[]{:S(2)}) copy-start(f32[512]{0:T(512)} %param.23) | copy-start | bytes 6148
  65.9 26.8 %copy-start.11 = (f32[512]{0:T(512)S(1)}, f32[512]{0:T(512)}, u32[]{:S(2)}) copy-start(f32[512]{0:T(512)} %param.24) | copy-start | bytes 6148
  92.7 1.4 %copy-start.1 = (f32[3,2,256,256]{3,2,1,0:T(8,128)S(1)}, f32[3,2,256,256]{3,2,1,0:T(8,128)}, u32[]{:S(2)}) copy-start(f32[3,2,256,256]{3,2,1,0:T(8,128)} %get-tuple-element.69.refs_0_) | copy-start | bytes 4718596

commit v8 on v7

--- a/solution.py
+++ b/solution.py
@@ -157,11 +157,11 @@
         for load in loads:
             load.start()
         ins = [
-            Operand(sources[n], in_slots.get(n, sources[n]), in_sem.at[n] if n in in_slots else None)
+            Operand(sources[n], in_slots.get(n, sources[n]), in_sem.at[far_in.index(n)] if n in in_slots else None)
             for n in range(n_in)
         ]
         outs = [
-            Result(targets[n], out_slots.get(n, targets[n]), out_sem.at[n] if n in out_slots else None)
+            Result(targets[n], out_slots.get(n, targets[n]), out_sem.at[far_out.index(n)] if n in out_slots else None)
             for n in range(n_out)
         ]
         for load in loads:
@@ -189,7 +189,7 @@
         out_specs=[hbm] * (n_straight + n_left) + [vmem if n in near_out else hbm for n in range(n_out)],
         scratch_shapes=[pltpu.VMEM(operands[n].shape, operands[n].dtype) for n in far_in]
         + [pltpu.VMEM(results[n], F32) for n in far_out]
-        + [pltpu.SemaphoreType.DMA((max(1, n),)) for n in (n_in, n_out, n_straight)]
+        + [pltpu.SemaphoreType.DMA((max(1, n),)) for n in (len(far_in), len(far_out), n_straight)]
         + ([] if near_straight else [pltpu.VMEM(value.shape, value.dtype) for value in straight])
         + list(scratch),
         compiler_params=pltpu.CompilerParams(vmem_limit_bytes=megabytes << 20, **extra),
@@ -482,7 +482,7 @@
     (
         pair_buf, score, high, low, q_part, q_land, q_all, k_all, w_all, squares, mixed_all, hidden_two, down, normal_two, rate_two,
         part, landed, back, back_landed, ups_part, ups_sib, ups_go, ups_got, downs_part, downs_sib, downs_go, downs_got,
-        pair_sem, kept_send, kept_recv, kz_send, kf_send, ks_send, k_recv, q_send, q_recv, w_send, wx_send, wf_send, w_recv,
+        pair_sem, kept_send, kept_recv, kz_send, kf_send, ks_send, k_recv, q_send, q_recv, w_send, w_recv, wx_send, wx_recv, wf_send, wf_recv,
         mix_send, mix_recv, part_send, part_recv, back_send, back_recv, sib_send, sib_recv, g_send, g_recv,
     ) = scratch
     zs, feats, rows = mixed_all.shape
@@ -496,12 +496,12 @@
     z, blk = lax.axis_index("head"), lax.axis_index("blk")
     core, chip = lax.rem(blk, 2), lax.div(blk, 2)
     dp, dps = lax.axis_index("dp"), lax.axis_size("dp")
-    partners = others(dp, dps)
     team = dp * chips + chip
     other_core = 1 - core
     sib_blk = blk + 1 - 2 * core
     sibling = {"blk": sib_blk}
     peers, far_teams = others(z, zs), others(team, teams)
+    sources = [lax.rem(z + zs - n, zs) for n in range(1, zs)]
     far = [step * 2 + core for step in others(chip, chips)]
     far_siblings = [step * 2 + other_core for step in others(chip, chips)]
     mine = pl.ds(pl.multiple_of(z * piece, 8), piece)
@@ -521,10 +521,13 @@
     normed = halves(normal * gain_one[...] + bias_one[...])
     meet(meeting)
     copies = []
-    fewer = feats // (2 * dps)
-    w_mine = w_out.source.at[pl.ds(pl.multiple_of((dp * 2 + core) * fewer, 8), fewer)]
+    squads, _, _, fewer, _ = w_all.shape
+    close = squads // dps
+    base = chip - lax.rem(chip, close)
+    squad = dp * close + chip - base
+    w_mine = w_out.source.at[pl.ds(pl.multiple_of((squad * 2 + core) * fewer, 8), fewer)]
     copies += [
-        send(w_mine, w_all.at[z, dp, core], w_send.at[n], w_recv.at[z, dp, core], {"head": peer})
+        send(w_mine, w_all.at[squad, core, z], w_send.at[n], w_recv.at[n], {"head": peer})
         for n, peer in enumerate(peers)
     ]
     kept[blk, 0:feats, :] = dot_halves(normed, halves(w_key[...])).T
@@ -544,17 +547,10 @@
     queries[...] = q_rows.T
     queries.flush()
     q_land[z] = q_part[z]
-    w_all[z] = w_out[...].reshape(dps, 2, fewer, width)
+    w_all[squad, core, z] = w_out[pl.ds(pl.multiple_of((squad * 2 + core) * fewer, 8), fewer), :]
     id_column[...] = jnp.broadcast_to(id_line, (LANES, rows)).T
     id_column.flush()
     small[...] = jnp.zeros(small.shape, F32)
-    for n, peer in enumerate(peers):
-        ready = w_all.at[peer, dp, core]
-        arrived(ready, w_recv.at[peer, dp, core])
-        copies += [
-            send(ready, ready, wx_send.at[n, m], w_recv.at[peer, dp, core], {"dp": partner})
-            for m, partner in enumerate(partners)
-        ]
     for n, source in enumerate(far):
         arrived(kept.at[source], kept_recv.at[source])
         copies.append(
@@ -574,12 +570,40 @@
                 src_ref=mixed.at[some],
                 dst_ref=mixed_all.at[z, some],
                 send_sem=mix_send.at[n, index],
-                recv_sem=mix_recv.at[z, index],
+                recv_sem=mix_recv.at[n, index],
                 device_id={"head": peer},
                 device_id_type=MESH,
             )
             for n, peer in enumerate(peers)
         ]
+
+    squad_copies = [
+        pltpu.make_async_remote_copy(
+            src_ref=w_all.at[squad, core],
+            dst_ref=w_all.at[squad, core],
+            send_sem=wx_send.at[n - 1],
+            recv_sem=wx_recv.at[n - 1],
+            device_id={
+                "dp": lax.div(lax.rem(squad + n, squads), close),
+                "blk": (base + lax.rem(lax.rem(squad + n, squads), close)) * 2 + core,
+            },
+            device_id_type=MESH,
+        )
+        for n in range(1, squads)
+    ]
+
+    key_copies = [
+        pltpu.make_async_remote_copy(
+            src_ref=k_all.at[blk, peer],
+            dst_ref=k_all.at[blk, peer],
+            send_sem=kf_send.at[n, m],
+            recv_sem=k_recv.at[blk, peer],
+            device_id={"blk": target},
+            device_id_type=MESH,
+        )
+        for n, peer in enumerate(peers)
+        for m, target in enumerate([sib_blk] + far)
+    ]
 
     def step(index, carry):
         slot = lax.rem(index, 2)
@@ -597,6 +621,20 @@
         for copy in mix_copies(index):
             copy.start()
 
+        @pl.when(index == groups // 2)
+        def _():
+            for n, source in enumerate(sources):
+                arrived(w_all.at[squad, core, source], w_recv.at[n])
+            for copy in squad_copies:
+                copy.start()
+
+        @pl.when(index == max(0, groups - 2))
+        def _():
+            for peer in peers:
+                arrived(k_all.at[blk, peer], k_recv.at[blk, peer])
+            for copy in key_copies:
+                copy.start()
+
         @pl.when(index + 2 < groups)
         def _():
             pair_copy(index + 2, slot).start()
@@ -606,39 +644,29 @@
     lax.fori_loop(0, groups, step, 0)
     mixed.flush()
     log_sums.flush()
-    for n, peer in enumerate(peers):
-        for kind in range(dps):
-            ready = w_all.at[peer, kind, core]
-
-            @pl.when(dp != kind)
-            def _(ready=ready, sem=w_recv.at[peer, kind, core]):
-                arrived(ready, sem)
-
-            copies.append(send(ready, ready, wf_send.at[n, kind], w_recv.at[peer, kind, core], sibling))
-    for n, peer in enumerate(peers):
-        ready = k_all.at[blk, peer]
-        arrived(ready, k_recv.at[blk, peer])
-        copies += [
-            send(ready, ready, kf_send.at[n, m], k_recv.at[blk, peer], {"blk": target})
-            for m, target in enumerate([sib_blk] + far)
-        ]
-
+    squad_sources = [lax.rem(squad + squads - n, squads) for n in range(squads)]
+    for n, source in enumerate(squad_sources):
+        ready = w_all.at[source, core]
+        if n >= 1:
+            arrived(ready, wx_recv.at[n - 1])
+        copies.append(send(ready, ready, wf_send.at[n], wf_recv.at[n], sibling))
     small[SMALL_B_DOWN : SMALL_B_DOWN + 1, :] = column_sum(cot[mine, :])
     cots = halves(cot[...])
     downs = halves(w_down[...])
     d_act = dot_halves(cots, downs, NT)
     ups = halves(w_up[...])
-    for peer in peers:
-        for kind in range(dps):
-            arrived(w_all.at[peer, kind, other_core], w_recv.at[peer, kind, other_core])
-    outs = halves(w_all[...].reshape(zs * feats, width))
+    for n, source in enumerate(squad_sources):
+        arrived(w_all.at[source, other_core], wf_recv.at[n])
+    outs = halves(
+        jnp.concatenate([w_all[s, kind, n] for n in range(zs) for s in range(squads) for kind in range(2)], axis=0)
+    )
     mixed_all[z] = mixed[...]
-    for peer in peers:
+    for n, source in enumerate(sources):
         for index in range(groups):
             some = pl.ds(index * (8 * group), 8 * group)
-            arrived(mixed_all.at[peer, some], mix_recv.at[peer, index])
+            arrived(mixed_all.at[source, some], mix_recv.at[n, index])
     copies += [
-        send(q_part.at[peer], q_land.at[z], q_send.at[n], q_recv.at[z], {"head": peer})
+        send(q_part.at[peer], q_land.at[z], q_send.at[n], q_recv.at[n], {"head": peer})
         for n, peer in enumerate(peers)
     ]
     mixed_rows = mixed_all[...].reshape(zs * feats, rows).T
@@ -655,7 +683,7 @@
     d_pres = halves(d_pre)
     part[...] = dot_halves(d_pres, ups, NT).reshape(zs, piece, width)
     copies += [
-        send(part.at[peer], landed.at[z], part_send.at[n], part_recv.at[z], {"head": peer})
+        send(part.at[peer], landed.at[z], part_send.at[n], part_recv.at[n], {"head": peer})
         for n, peer in enumerate(peers)
     ]
     landed[z] = part[z]
@@ -685,8 +713,8 @@
             ready = k_all.at[source, peer]
             arrived(ready, k_recv.at[source, peer])
             copies.append(send(ready, ready, ks_send.at[n, m], k_recv.at[source, peer], sibling))
-    for peer in peers:
-        arrived(q_land.at[peer], q_recv.at[peer])
+    for n, source in enumerate(sources):
+        arrived(q_land.at[source], q_recv.at[n])
     for n in range(zs):
         q_all[n] = q_land[n].T
     for n in range(blocks):
@@ -728,8 +756,8 @@
     small[SMALL_PENALTY : SMALL_PENALTY + 1, :] = jnp.where(
         lane == 0, total(terms), jnp.where(lane == 1, total(number), 0.0)
     )
-    for peer in peers:
-        arrived(landed.at[peer], part_recv.at[peer])
+    for n, source in enumerate(sources):
+        arrived(landed.at[source], part_recv.at[n])
     d_normed = functools.reduce(jnp.add, [landed[n] for n in range(zs)])
     normal = normal_two[mine, :]
     d_rows = cot[mine, :] + normalize_back(d_normed, gain[...], normal, rate_two[mine, 0:1])
@@ -738,7 +766,7 @@
         some = slice(n * feats, (n + 1) * feats)
         back[n] = dot_halves(d_halves, (outs[0][some], outs[1][some]), NT)
     copies += [
-        send(back.at[peer], back_landed.at[z], back_send.at[n], back_recv.at[z], {"head": peer})
+        send(back.at[peer], back_landed.at[z], back_send.at[n], back_recv.at[n], {"head": peer})
         for n, peer in enumerate(peers)
     ]
     back_landed[z] = back[z]
@@ -762,11 +790,11 @@
         shares[there, columns_of] = up_share[rows_of]
     shares[there.stop :, :] = down_share
     shares.flush()
-    for peer in peers:
-        arrived(back_landed.at[peer], back_recv.at[peer])
+    for n, source in enumerate(sources):
+        arrived(back_landed.at[source], back_recv.at[n])
     d_mixed[...] = back_landed[...].reshape(rows, feats).T
     d_mixed.flush()
-    for copy in copies:
+    for copy in copies + squad_copies + key_copies:
         copy.wait_send()
 
     def drain(index, carry):
@@ -781,7 +809,8 @@
     _, heads, rows, cols = pair.shape
     feats, blocks = heads * DH, cols // rows
     width, units = operands[0].shape[1], operands[12].shape[1]
-    piece, group = rows // zs, GROUP
+    piece, group, hops = rows // zs, GROUP, zs - 1
+    squads = dps * min(blocks // 2, max(1, feats // (2 * dps * 8)))
     up_rows, down_rows = width // (2 * teams), units // (2 * teams)
     groups = heads // group
     slab = pltpu.VMEM((zs, piece, width), F32)
@@ -806,7 +835,7 @@
             narrow, narrow,
             pltpu.VMEM((zs, feats, piece), F32),
             pltpu.VMEM((blocks, zs, feats, rows), F32),
-            pltpu.VMEM((zs, dps, 2, feats // (2 * dps), width), F32),
+            pltpu.VMEM((squads, 2, zs, feats // (2 * squads), width), F32),
             pltpu.VMEM((piece, cols), F32),
             pltpu.VMEM((zs, feats, rows), F32),
             pltpu.VMEM((rows, width), F32),
@@ -820,12 +849,13 @@
             one_down, one_down, one_down,
             dma((2,)),
             dma((blocks,)), dma((blocks,)),
-            dma((zs,)), dma((zs, blocks // 2)), dma((blocks // 2, zs)), dma((blocks, zs)),
-            dma((zs,)), dma((zs,)),
-            dma((zs,)), dma((zs, dps)), dma((zs, dps)), dma((zs, dps, 2)),
-            dma((zs, groups)), dma((zs, groups)),
-            dma((zs,)), dma((zs,)),
-            dma((zs,)), dma((zs,)),
+            dma((hops,)), dma((hops, blocks // 2)), dma((max(1, blocks // 2 - 1), hops)), dma((blocks, zs)),
+            dma((hops,)), dma((hops,)),
+            dma((hops,)), dma((hops,)), dma((max(1, squads - 1),)), dma((max(1, squads - 1),)),
+            dma((squads,)), dma((squads,)),
+            dma((hops, groups)), dma((hops, groups)),
+            dma((hops,)), dma((hops,)),
+            dma((hops,)), dma((hops,)),
             dma((2,)), dma((2,)),
             dma((2, teams)), dma((2, teams)),
         ],

time: 138 us -> 134 us (0.971)
  Pallas kernels: 130 us -> 124 us
    pallas_call x4, Pallas kernels: 130 us -> 124 us  [staged_call(): pl.pallas_call(body, out_shape=[jax.ShapeDtypeStruct(value.shape, value.d...]
  transfers between devices with their start and end apart: 4 -> 4, of which waited for: 0 -> 0; matrix products, arithmetic and copies ran while one was open for 0% -> 0% of each run, Pallas kernels for 19% -> 20%
where the time goes in v8:
time: 134 us; the launch traced here: 133 us
  Pallas kernels  124 us (93%)
  starting transfers between devices  5.95 us (4%)
  local copies, waits for them, and re-layouts  1.45 us (1%)
    pallas_call x4, Pallas kernels, staged_call(): pl.pallas_call(body, out_shape=[jax.ShapeDtypeStruct(value.shape, value.d...  124 us
    ppermute x3, starting transfers between devices, local(): lax.ppermute(parcel, 'head', [(source, (source + n + 1) % zs) for source...  4.32 us
  transfers between devices with their start and end apart: 4, of which 0 were waited for; matrix products, arithmetic and copies ran while one was open for 0% of the time, Pallas kernels for 20%

profile of v8, /device:TPU:0, one launch (start us, length us, event | category | flops | bytes accessed | tf_op | source)
XLA Modules:
  0.0 132.9 jit_solution(17647001242588893119)
XLA Ops:
  0.7 56.0 %front.1 = (f32[128,256]{1,0:T(8,128)}, f32[4,264,256]{2,1,0:T(8,128)}, f32[256,128]{1,0:T(8,128)}, f32[16,256,128]{2,1,0:T(8,128)}, f32[128,256]{1,0:T(8,128)},...) custom-call(f32[256,512]{1,0:T(8,128)} %bitcast.23, ...), custom_call_target="tpu_custom_call" | custom-call | tf_op jit(solution)/shard_map/front/pallas_call | solution.py:181
  56.7 1.0 collective-permute-start
  57.7 0.7 collective-permute-start.1
  58.4 2.6 %collective-permute-start.2 = (f32[128,512]{1,0:T(8,128)}, f32[128,512]{1,0:T(8,128)S(1)}, u32[]{:S(2)}, u32[]{:S(2)}) collective-permute-start(f32[128,512]{1,0:T(8,128)} %get-tuple-element.75), channel_id=1, source_target_pairs={{0,6},{2,0},{4,2},{6,4},{1,7},{3,1},{5,3},{7,5},{8,14},{10,8},{12,... | collective-permute-start | bytes 786440 | tf_op jit(solution)/shard_map/ppermute | solution.py:1162
  61.0 1.6 %collective-permute-start.3 = (f32[128,512]{1,0:T(8,128)}, f32[128,512]{1,0:T(8,128)S(1)}, u32[]{:S(2)}, u32[]{:S(2)}) collective-permute-start(f32[128,512]{1,0:T(8,128)} %get-tuple-element.76.refs_14_), channel_id=1, source_target_pairs={{0,16},{8,24},{16,0},{24,8},{1,17},{9,25},{17,1},{25,9},{2,18},{10... | collective-permute-start | bytes 786440 | tf_op jit(solution)/shard_map/ppermute | solution.py:1167
  62.6 0.0 copy-start
  62.6 0.0 copy-start.2
  62.6 0.0 copy-start.3
  62.6 0.0 copy-start.4
  62.6 0.0 copy-start.5
  62.6 0.0 copy-start.6
  62.6 0.0 copy-start.7
  62.7 0.0 copy-start.8
  62.7 0.0 copy-start.9
  62.7 0.0 copy-start.10
  62.7 0.0 copy-start.11
  62.7 26.7 %attend_back.1 = (f32[1,16,256,1024]{3,2,1,0:T(8,128)}, f32[1,16,256,1024]{3,2,1,0:T(8,128)}, f32[3,2,256,256]{3,2,1,0:T(8,128)}) custom-call(f32[128,256]{1,0:T(8,128)} %get-tuple-element.62.refs_0_, f32[4,264,256]{2,1,0:T(8,128)} %get-tuple-element.63.refs_1_, f32[128,256]{1,0:T(8,128)} %get-tuple-element.64.refs_2_, ...), custom_call_target="tpu_custom_call" | custom-call | flops 3355443200 | bytes 67108864 | tf_op jit(solution)/shard_map/attend_back/pallas_call | solution.py:181
  89.4 0.0 collective-permute-done.refs_11_
  89.4 0.0 collective-permute-done.1.refs_12_
  89.4 0.0 collective-permute-done.2.refs_13_
  89.4 0.0 collective-permute-done.3.refs_15_
  89.4 0.0 copy-done
  89.4 0.0 copy-done.2
  89.4 0.0 copy-done.3
  89.5 0.0 copy-done.4
  89.5 0.0 copy-done.5
  89.5 0.0 copy-done.6
  89.5 0.0 copy-done.7
  89.5 0.0 copy-done.8
  89.5 0.0 copy-done.9
  89.5 0.0 copy-done.10
  89.5 0.0 copy-done.11
  89.5 0.0 copy-start.1
  89.5 1.4 %copy-done.1 = f32[3,2,256,256]{3,2,1,0:T(8,128)S(1)} copy-done((f32[3,2,256,256]{3,2,1,0:T(8,128)S(1)}, f32[3,2,256,256]{3,2,1,0:T(8,128)}, u32[]{:S(2)}) %copy-start.1) | copy-done | bytes 1572888
  90.9 38.7 %finish.1 = (f32[256,512]{1,0:T(8,128)S(1)}, f32[256,512]{1,0:T(8,128)S(1)}, f32[4,2,64,512]{3,2,1,0:T(8,128)S(1)}, f32[512,512]{1,0:T(8,128)S(1)}, f32[512,512]...) custom-call(f32[3,2,256,256]{3,2,1,0:T(8,128)S(1)} %copy-done.1, f32[64,512]{1,0:T(8,128)S(1)} %copy-done.7, ...), custom_call_target="tpu_custom_call" | custom-call | tf_op jit(solution)/shard_map/finish/pallas_call | solution.py:181
  129.7 3.0 %place.1 = (f32[256,512]{1,0:T(8,128)}, f32[256,512]{1,0:T(8,128)}, f32[512,512]{1,0:T(8,128)}, f32[512,512]{1,0:T(8,128)}, f32[1,1]{1,0:T(1,128)}, /*index=5*/f...) custom-call(f32[4,2,64,512]{3,2,1,0:T(8,128)S(1)} %get-tuple-element, ...), custom_call_target="tpu_custom_call" | custom-call | tf_op jit(solution)/shard_map/place/pallas_call | solution.py:181
Async XLA Ops:
  56.7 32.7 %collective-permute-start = (f32[128,512]{1,0:T(8,128)}, f32[128,512]{1,0:T(8,128)S(1)}, u32[]{:S(2)}, u32[]{:S(2)}) collective-permute-start(f32[128,512]{1,0:T(8,128)} %get-tuple-element.73), channel_id=1, source_target_pairs={{0,2},{2,4},{4,6},{6,0},{1,3},{3,5},{5,7},{7,1},{8,10},{10,12},{12... | collective-permute-start | bytes 786440 | tf_op jit(solution)/shard_map/ppermute | solution.py:1162
  57.7 31.7 %collective-permute-start.1 = (f32[128,512]{1,0:T(8,128)}, f32[128,512]{1,0:T(8,128)S(1)}, u32[]{:S(2)}, u32[]{:S(2)}) collective-permute-start(f32[128,512]{1,0:T(8,128)} %get-tuple-element.74), channel_id=1, source_target_pairs={{0,4},{2,6},{4,0},{6,2},{1,5},{3,7},{5,1},{7,3},{8,12},{10,14},{12... | collective-permute-start | bytes 786440 | tf_op jit(solution)/shard_map/ppermute | solution.py:1162
  58.4 31.0 %collective-permute-start.2 = (f32[128,512]{1,0:T(8,128)}, f32[128,512]{1,0:T(8,128)S(1)}, u32[]{:S(2)}, u32[]{:S(2)}) collective-permute-start(f32[128,512]{1,0:T(8,128)} %get-tuple-element.75), channel_id=1, source_target_pairs={{0,6},{2,0},{4,2},{6,4},{1,7},{3,1},{5,3},{7,5},{8,14},{10,8},{12,... | collective-permute-start | bytes 786440 | tf_op jit(solution)/shard_map/ppermute | solution.py:1162
  61.0 28.4 %collective-permute-start.3 = (f32[128,512]{1,0:T(8,128)}, f32[128,512]{1,0:T(8,128)S(1)}, u32[]{:S(2)}, u32[]{:S(2)}) collective-permute-start(f32[128,512]{1,0:T(8,128)} %get-tuple-element.76.refs_14_), channel_id=1, source_target_pairs={{0,16},{8,24},{16,0},{24,8},{1,17},{9,25},{17,1},{25,9},{2,18},{10... | collective-permute-start | bytes 786440 | tf_op jit(solution)/shard_map/ppermute | solution.py:1167
  62.6 26.8 %copy-start = (f32[1,256,512]{2,1,0:T(8,128)S(1)}, f32[1,256,512]{2,1,0:T(8,128)}, u32[]{:S(2)}) copy-start(f32[1,256,512]{2,1,0:T(8,128)} %param.20) | copy-start | bytes 1572868
  62.6 26.8 %copy-start.2 = (f32[512,128]{1,0:T(8,128)S(1)}, f32[512,128]{1,0:T(8,128)}, u32[]{:S(2)}) copy-start(f32[512,128]{1,0:T(8,128)} %refs_9_.3) | copy-start | bytes 786436
  62.6 26.8 %copy-start.3 = (f32[512,128]{1,0:T(8,128)S(1)}, f32[512,128]{1,0:T(8,128)}, u32[]{:S(2)}) copy-start(f32[512,128]{1,0:T(8,128)} %refs_10_.1) | copy-start | bytes 786436
  62.6 26.8 %copy-start.4 = (f32[512,128]{1,0:T(8,128)S(1)}, f32[512,128]{1,0:T(8,128)}, u32[]{:S(2)}) copy-start(f32[512,128]{1,0:T(8,128)} %refs_6_.3) | copy-start | bytes 786436
  62.6 26.9 %copy-start.5 = (f32[128,256]{1,0:T(8,128)S(1)}, f32[128,256]{1,0:T(8,128)}, u32[]{:S(2)}) copy-start(f32[128,256]{1,0:T(8,128)} %get-tuple-element.65.refs_3_.refs_7_) | copy-start | bytes 393220
  62.6 26.9 %copy-start.6 = (f32[128,512]{1,0:T(8,128)S(1)}, f32[128,512]{1,0:T(8,128)}, u32[]{:S(2)}) copy-start(f32[128,512]{1,0:T(8,128)} %get-tuple-element.76.refs_14_) | copy-start | bytes 786436
  62.6 26.9 %copy-start.7 = (f32[64,512]{1,0:T(8,128)S(1)}, f32[64,512]{1,0:T(8,128)}, u32[]{:S(2)}) copy-start(f32[64,512]{1,0:T(8,128)} %get-tuple-element.70.refs_1_) | copy-start | bytes 393220
  62.7 26.9 %copy-start.8 = (f32[64,512]{1,0:T(8,128)S(1)}, f32[64,512]{1,0:T(8,128)}, u32[]{:S(2)}) copy-start(f32[64,512]{1,0:T(8,128)} %get-tuple-element.71.refs_2_) | copy-start | bytes 393220
  62.7 26.9 %copy-start.9 = (f32[16,512]{1,0:T(8,128)S(1)}, f32[16,512]{1,0:T(8,128)}, u32[]{:S(2)}) copy-start(f32[16,512]{1,0:T(8,128)} %get-tuple-element.72.refs_8_) | copy-start | bytes 98308
  62.7 26.9 %copy-start.10 = (f32[512]{0:T(512)S(1)}, f32[512]{0:T(512)}, u32[]{:S(2)}) copy-start(f32[512]{0:T(512)} %param.23) | copy-start | bytes 6148
  62.7 26.8 %copy-start.11 = (f32[512]{0:T(512)S(1)}, f32[512]{0:T(512)}, u32[]{:S(2)}) copy-start(f32[512]{0:T(512)} %param.24) | copy-start | bytes 6148
  89.5 1.4 %copy-start.1 = (f32[3,2,256,256]{3,2,1,0:T(8,128)S(1)}, f32[3,2,256,256]{3,2,1,0:T(8,128)}, u32[]{:S(2)}) copy-start(f32[3,2,256,256]{3,2,1,0:T(8,128)} %get-tuple-element.69.refs_0_) | copy-start | bytes 4718596

commit v9 on v8

--- a/solution.py
+++ b/solution.py
@@ -276,11 +276,10 @@
 
 def attend_back_kernel(operands, results, scratch, raw):
     queries, kept, d_mixed, mixed, id_column, id_row = operands
-    (d_heads,) = results
-    pair, cot, log_sums, out_pair, grad_pair = raw
+    pair, cot, log_sums, out_pair, grad_pair, heads_out = raw
     pair_buf, cot_buf, log_buf, out_buf, grad_buf = scratch[:5]
     here = scratch[5:11]
-    in_sem, out_sem = scratch[11:]
+    d_heads, in_sem, out_sem, heads_sem = scratch[11:]
     heads = pair.shape[1]
     feats = heads * DH
     depth, rows, cols = pair_buf.shape
@@ -415,33 +414,37 @@
         return carry
 
     lax.fori_loop(0, heads, stage, 0)
-    for result in results:
-        result.flush()
+    last = pltpu.make_async_copy(d_heads, heads_out.at[pl.ds(0, d_heads.shape[0])], heads_sem.at[0])
+    last.start()
     for n in range(max(0, heads - depth), heads):
         for copy in outward(n):
             copy.wait()
+    last.wait()
 
 
 def attend_back(pair, cot, queries, kept, mixed, d_mixed, log_sums, id_column, id_row):
     _, heads, rows, cols = pair.shape
     feats = heads * DH
     blocks = kept.shape[0]
-    depth = 4
+    depth = 6
+    entries = max(blocks // 2 + 1, (26 << 20) // (16 * feats * rows))
     wide, thin = pltpu.VMEM((rows, cols), F32), pltpu.VMEM((rows, cols), BF16)
     return staged_call(
         attend_back_kernel,
         "attend_back",
         [queries, kept, d_mixed, mixed, id_column, id_row],
-        [(blocks // 2 + 1, 2, 2 * feats, rows)],
+        [],
         [pltpu.VMEM((depth, rows, cols), F32)] * 2
         + [pltpu.VMEM((depth, rows, LANES), F32)]
         + [pltpu.VMEM((depth, rows, cols), F32)] * 2
         + [wide] * 2
         + [thin] * 4
-        + [pltpu.SemaphoreType.DMA((3, depth)), pltpu.SemaphoreType.DMA((2, depth))],
+        + [pltpu.VMEM((blocks // 2 + 1, 2, 2 * feats, rows), F32)]
+        + [pltpu.SemaphoreType.DMA((n, depth)) for n in (3, 2)]
+        + [pltpu.SemaphoreType.DMA((1,))],
         BACK_MB,
         raw=(pair, cot, log_sums),
-        raw_results=(pair.shape, pair.shape),
+        raw_results=(pair.shape, pair.shape, (entries, 2, 2 * feats, rows)),
         cost=pl.CostEstimate(
             flops=2 * 400 * heads * rows * cols,
             bytes_accessed=16 * heads * rows * cols,
@@ -480,7 +483,7 @@
     ) = results[:11]
     parcels = results[11:]
     (
-        pair_buf, score, high, low, q_part, q_land, q_all, k_all, w_all, squares, mixed_all, hidden_two, down, normal_two, rate_two,
+        pair_buf, score, high, low, q_part, q_land, q_all, k_all, w_all, squares, mixed_all, hidden_two, down, d_act, up_high, up_low, normal_two, rate_two,
         part, landed, back, back_landed, ups_part, ups_sib, ups_go, ups_got, downs_part, downs_sib, downs_go, downs_got,
         pair_sem, kept_send, kept_recv, kz_send, kf_send, ks_send, k_recv, q_send, q_recv, w_send, w_recv, wx_send, wx_recv, wf_send, wf_recv,
         mix_send, mix_recv, part_send, part_recv, back_send, back_recv, sib_send, sib_recv, g_send, g_recv,
@@ -551,6 +554,9 @@
     id_column[...] = jnp.broadcast_to(id_line, (LANES, rows)).T
     id_column.flush()
     small[...] = jnp.zeros(small.shape, F32)
+    small[SMALL_B_DOWN : SMALL_B_DOWN + 1, :] = column_sum(cot[mine, :])
+    d_act[...] = dot_full(cot[...], w_down[...], NT)
+    up_high[...], up_low[...] = halves(w_up[...])
     for n, source in enumerate(far):
         arrived(kept.at[source], kept_recv.at[source])
         copies.append(
@@ -650,11 +656,6 @@
         if n >= 1:
             arrived(ready, wx_recv.at[n - 1])
         copies.append(send(ready, ready, wf_send.at[n], wf_recv.at[n], sibling))
-    small[SMALL_B_DOWN : SMALL_B_DOWN + 1, :] = column_sum(cot[mine, :])
-    cots = halves(cot[...])
-    downs = halves(w_down[...])
-    d_act = dot_halves(cots, downs, NT)
-    ups = halves(w_up[...])
     for n, source in enumerate(squad_sources):
         arrived(w_all.at[source, other_core], wf_recv.at[n])
     outs = halves(
@@ -669,6 +670,7 @@
         send(q_part.at[peer], q_land.at[z], q_send.at[n], q_recv.at[n], {"head": peer})
         for n, peer in enumerate(peers)
     ]
+    ups = up_high[...], up_low[...]
     mixed_rows = mixed_all[...].reshape(zs * feats, rows).T
     hidden_rows = atoms[...] + dot_halves(halves(mixed_rows), outs) + b_out[...]
     hidden_two[...] = hidden_rows
@@ -679,8 +681,9 @@
     pre = dot_halves(halves(normed), ups) + b_up[...]
     phi = 0.5 * (1.0 + lax.erf(pre * math.sqrt(0.5)))
     act = pre * phi
-    d_pre = d_act * (phi + pre * jnp.exp(-0.5 * pre * pre) * (1.0 / math.sqrt(2.0 * math.pi)))
+    d_pre = d_act[...] * (phi + pre * jnp.exp(-0.5 * pre * pre) * (1.0 / math.sqrt(2.0 * math.pi)))
     d_pres = halves(d_pre)
+    cots, downs = halves(cot[...]), halves(w_down[...])
     part[...] = dot_halves(d_pres, ups, NT).reshape(zs, piece, width)
     copies += [
         send(part.at[peer], landed.at[z], part_send.at[n], part_recv.at[n], {"head": peer})
@@ -840,6 +843,9 @@
             pltpu.VMEM((zs, feats, rows), F32),
             pltpu.VMEM((rows, width), F32),
             pltpu.VMEM((rows, width), F32),
+            pltpu.VMEM((rows, units), F32),
+            pltpu.VMEM((width, units), BF16),
+            pltpu.VMEM((width, units), BF16),
             pltpu.VMEM((rows, width), F32),
             pltpu.VMEM((rows, LANES), F32),
             slab, slab, narrow, narrow,
@@ -867,19 +873,22 @@
 
 def finish_kernel(operands, results, scratch, raw):
     (
-        d_heads, out_mine, d_hidden, atoms, gain, bias, w_query, mixed, small_in, w_key, w_value,
-    ) = operands[:11]
-    parcels = operands[11 : 10 + lax.axis_size("head")]
-    chip_shares = operands[10 + lax.axis_size("head") :]
+        out_mine, d_hidden, atoms, gain, bias, w_query, mixed, small_in, w_key, w_value,
+    ) = operands[:10]
+    parcels = operands[10 : 9 + lax.axis_size("head")]
+    chip_shares = operands[9 + lax.axis_size("head") :]
     grad_atoms, out_atoms, total_grads, grad_up, grad_down, small, penalty = results
     (
         sib_keys, sib_values, go_keys, go_values, got_keys, got_values,
         part, landed, grads, sib_grads, go_grads, got_grads, hidden_all, small_z, small_all,
         sib_send, sib_recv, kv_send, kv_recv, part_send, part_recv, back_send, back_recv,
         g_send, g_recv, t_send, t_recv, f_send, b_send, b_recv, bf_send, out_send, out_recv,
-        small_z_send, small_z_recv, small_send, small_recv,
+        small_z_send, small_z_recv, small_send, small_recv, own_heads, heads_sem,
     ) = scratch
-    chips, feats, rows = d_heads.shape[0] - 1, d_heads.shape[2] // 2, d_heads.shape[3]
+    (d_heads,) = raw
+    chips, feats, rows = own_heads.shape[0] - 1, d_heads.shape[2] // 2, d_heads.shape[3]
+    heads_copy = pltpu.make_async_copy(d_heads.at[pl.ds(0, chips + 1)], own_heads, heads_sem.at[0])
+    heads_copy.start()
     zs, piece, width = part.shape
     teams, _, share, _ = grads.shape
     blk, z, dp = lax.axis_index("blk"), lax.axis_index("head"), lax.axis_index("dp")
@@ -898,7 +907,7 @@
     meet(meeting)
     copies = [
         send(
-            d_heads.source.at[pl.ds(0, chips), other_core, pl.ds(kind * feats, feats)],
+            d_heads.at[pl.ds(0, chips), other_core, pl.ds(kind * feats, feats)],
             sib, sib_send.at[kind], sib_recv.at[kind], sibling,
         )
         for kind, sib in enumerate([sib_keys, sib_values])
@@ -926,7 +935,7 @@
                 send(ready, ready, b_send.at[kind, n, m], b_recv.at[kind, source, core], {"dp": partner})
                 for m, partner in enumerate(partners)
             ]
-    own_heads = d_heads.ref
+    heads_copy.wait()
     d_queries = own_heads[chips, 0, 0:feats, :]
     for kind, (sib, go, got) in enumerate([(sib_keys, go_keys, got_keys), (sib_values, go_values, got_values)]):
         arrived(sib, sib_recv.at[kind])
@@ -1049,9 +1058,9 @@
         copy.wait_send()
 
 
-def finish(zs, dps, units, *operands):
-    d_heads, atoms = operands[0], operands[3]
-    chips, feats, rows = d_heads.shape[0] - 1, d_heads.shape[2] // 2, d_heads.shape[3]
+def finish(zs, dps, units, d_heads, *operands):
+    atoms = operands[2]
+    chips, feats, rows = lax.axis_size("blk") // 2, d_heads.shape[2] // 2, d_heads.shape[3]
     width = atoms.shape[1]
     piece = rows // zs
     teams = dps * chips
@@ -1088,10 +1097,12 @@
             dma((zs,)), dma((zs,)),
             dma((zs,)), dma((zs,)),
             dma((2 * teams,)), dma((2 * teams,)),
+            pltpu.VMEM((chips + 1, 2, 2 * feats, rows), F32), dma((1,)),
         ],
         FINISH_MB,
         remote=2,
-        near_in=[0] + list(range(11, len(operands))),
+        near_in=range(10, len(operands)),
+        raw=(d_heads,),
         near_out=range(7),
     )
 

time: 134 us -> 132 us (0.985)
  local copies, waits for them, and re-layouts: 1.45 us -> 0.05 us
    unnamed x24 -> x22, local copies, waits for them, and re-layouts: 1.45 us -> 0.05 us
where the time goes in v9:
time: 132 us; the launch traced here: 131 us
  Pallas kernels  124 us (94%)
  starting transfers between devices  5.78 us (4%)
    pallas_call x4, Pallas kernels, staged_call(): pl.pallas_call(body, out_shape=[jax.ShapeDtypeStruct(value.shape, value.d...  124 us
    ppermute x3, starting transfers between devices, local(): lax.ppermute(parcel, 'head', [(source, (source + n + 1) % zs) for source...  4.24 us
  transfers between devices with their start and end apart: 4, of which 0 were waited for; matrix products, arithmetic and copies ran while one was open for 0% of the time, Pallas kernels for 20%

profile of v9, /device:TPU:0, one launch (start us, length us, event | category | flops | bytes accessed | tf_op | source)
XLA Modules:
  0.0 131.3 jit_solution(14365986713557425523)
XLA Ops:
  0.7 55.4 %front.1 = (f32[128,256]{1,0:T(8,128)}, f32[4,264,256]{2,1,0:T(8,128)}, f32[256,128]{1,0:T(8,128)}, f32[16,256,128]{2,1,0:T(8,128)}, f32[128,256]{1,0:T(8,128)},...) custom-call(f32[256,512]{1,0:T(8,128)} %bitcast.23, ...), custom_call_target="tpu_custom_call" | custom-call | tf_op jit(solution)/shard_map/front/pallas_call | solution.py:181
  56.1 1.0 collective-permute-start
  57.0 1.6 %collective-permute-start.1 = (f32[128,512]{1,0:T(8,128)}, f32[128,512]{1,0:T(8,128)S(1)}, u32[]{:S(2)}, u32[]{:S(2)}) collective-permute-start(f32[128,512]{1,0:T(8,128)} %get-tuple-element.67), channel_id=1, source_target_pairs={{0,4},{2,6},{4,0},{6,2},{1,5},{3,7},{5,1},{7,3},{8,12},{10,14},{12... | collective-permute-start | bytes 786440 | tf_op jit(solution)/shard_map/ppermute | solution.py:1173
  58.6 1.7 %collective-permute-start.2 = (f32[128,512]{1,0:T(8,128)}, f32[128,512]{1,0:T(8,128)S(1)}, u32[]{:S(2)}, u32[]{:S(2)}) collective-permute-start(f32[128,512]{1,0:T(8,128)} %get-tuple-element.68), channel_id=1, source_target_pairs={{0,6},{2,0},{4,2},{6,4},{1,7},{3,1},{5,3},{7,5},{8,14},{10,8},{12,... | collective-permute-start | bytes 786440 | tf_op jit(solution)/shard_map/ppermute | solution.py:1173
  60.3 1.5 %collective-permute-start.3 = (f32[128,512]{1,0:T(8,128)}, f32[128,512]{1,0:T(8,128)S(1)}, u32[]{:S(2)}, u32[]{:S(2)}) collective-permute-start(f32[128,512]{1,0:T(8,128)} %get-tuple-element.69.refs_13_), channel_id=1, source_target_pairs={{0,16},{8,24},{16,0},{24,8},{1,17},{9,25},{17,1},{25,9},{2,18},{10... | collective-permute-start | bytes 786440 | tf_op jit(solution)/shard_map/ppermute | solution.py:1178
  61.9 0.0 copy-start
  61.9 0.0 copy-start.1
  61.9 0.0 copy-start.2
  61.9 0.0 copy-start.3
  61.9 0.0 copy-start.4
  61.9 0.0 copy-start.5
  61.9 0.0 copy-start.6
  61.9 0.0 copy-start.7
  61.9 0.0 copy-start.8
  61.9 0.0 copy-start.9
  61.9 0.0 copy-start.10
  61.9 26.8 %attend_back.1 = (f32[1,16,256,1024]{3,2,1,0:T(8,128)}, f32[1,16,256,1024]{3,2,1,0:T(8,128)}, f32[52,2,256,256]{3,2,1,0:T(8,128)}) custom-call(f32[128,256]{1,0:T(8,128)} %get-tuple-element.70.refs_0_, f32[4,264,256]{2,1,0:T(8,128)} %get-tuple-element.71.refs_1_, f32[128,256]{1,0:T(8,128)} %get-tuple-element.72.refs_2_, ...), custom_call_target="tpu_custom_call" | custom-call | flops 3355443200 | bytes 67108864 | tf_op jit(solution)/shard_map/attend_back/pallas_call | solution.py:181
  88.8 0.0 collective-permute-done.refs_10_
  88.8 0.0 collective-permute-done.1.refs_11_
  88.8 0.0 collective-permute-done.2.refs_12_
  88.8 0.0 collective-permute-done.3.refs_14_
  88.8 0.0 copy-done
  88.8 0.0 copy-done.1
  88.8 0.0 copy-done.2
  88.8 0.0 copy-done.3
  88.8 0.0 copy-done.4
  88.8 0.0 copy-done.5
  88.9 0.0 copy-done.6
  88.9 0.0 copy-done.7
  88.9 0.0 copy-done.8
  88.9 0.0 copy-done.9
  88.9 0.0 copy-done.10
  88.9 39.3 %finish.1 = (f32[256,512]{1,0:T(8,128)S(1)}, f32[256,512]{1,0:T(8,128)S(1)}, f32[4,2,64,512]{3,2,1,0:T(8,128)S(1)}, f32[512,512]{1,0:T(8,128)S(1)}, f32[512,512]...) custom-call(f32[64,512]{1,0:T(8,128)S(1)} %copy-done.6, f32[64,512]{1,0:T(8,128)S(1)} %copy-done.7, ...), custom_call_target="tpu_custom_call" | custom-call | tf_op jit(solution)/shard_map/finish/pallas_call | solution.py:181
  128.2 2.9 %place.1 = (f32[256,512]{1,0:T(8,128)}, f32[256,512]{1,0:T(8,128)}, f32[512,512]{1,0:T(8,128)}, f32[512,512]{1,0:T(8,128)}, f32[1,1]{1,0:T(1,128)}, /*index=5*/f...) custom-call(f32[4,2,64,512]{3,2,1,0:T(8,128)S(1)} %get-tuple-element, ...), custom_call_target="tpu_custom_call" | custom-call | tf_op jit(solution)/shard_map/place/pallas_call | solution.py:181
Async XLA Ops:
  56.1 32.7 %collective-permute-start = (f32[128,512]{1,0:T(8,128)}, f32[128,512]{1,0:T(8,128)S(1)}, u32[]{:S(2)}, u32[]{:S(2)}) collective-permute-start(f32[128,512]{1,0:T(8,128)} %get-tuple-element.66), channel_id=1, source_target_pairs={{0,2},{2,4},{4,6},{6,0},{1,3},{3,5},{5,7},{7,1},{8,10},{10,12},{12... | collective-permute-start | bytes 786440 | tf_op jit(solution)/shard_map/ppermute | solution.py:1173
  57.0 31.7 %collective-permute-start.1 = (f32[128,512]{1,0:T(8,128)}, f32[128,512]{1,0:T(8,128)S(1)}, u32[]{:S(2)}, u32[]{:S(2)}) collective-permute-start(f32[128,512]{1,0:T(8,128)} %get-tuple-element.67), channel_id=1, source_target_pairs={{0,4},{2,6},{4,0},{6,2},{1,5},{3,7},{5,1},{7,3},{8,12},{10,14},{12... | collective-permute-start | bytes 786440 | tf_op jit(solution)/shard_map/ppermute | solution.py:1173
  58.6 30.2 %collective-permute-start.2 = (f32[128,512]{1,0:T(8,128)}, f32[128,512]{1,0:T(8,128)S(1)}, u32[]{:S(2)}, u32[]{:S(2)}) collective-permute-start(f32[128,512]{1,0:T(8,128)} %get-tuple-element.68), channel_id=1, source_target_pairs={{0,6},{2,0},{4,2},{6,4},{1,7},{3,1},{5,3},{7,5},{8,14},{10,8},{12,... | collective-permute-start | bytes 786440 | tf_op jit(solution)/shard_map/ppermute | solution.py:1173
  60.3 28.5 %collective-permute-start.3 = (f32[128,512]{1,0:T(8,128)}, f32[128,512]{1,0:T(8,128)S(1)}, u32[]{:S(2)}, u32[]{:S(2)}) collective-permute-start(f32[128,512]{1,0:T(8,128)} %get-tuple-element.69.refs_13_), channel_id=1, source_target_pairs={{0,16},{8,24},{16,0},{24,8},{1,17},{9,25},{17,1},{25,9},{2,18},{10... | collective-permute-start | bytes 786440 | tf_op jit(solution)/shard_map/ppermute | solution.py:1178
  61.9 26.9 %copy-start = (f32[1,256,512]{2,1,0:T(8,128)S(1)}, f32[1,256,512]{2,1,0:T(8,128)}, u32[]{:S(2)}) copy-start(f32[1,256,512]{2,1,0:T(8,128)} %param.20) | copy-start | bytes 1572868
  61.9 26.9 %copy-start.1 = (f32[512,128]{1,0:T(8,128)S(1)}, f32[512,128]{1,0:T(8,128)}, u32[]{:S(2)}) copy-start(f32[512,128]{1,0:T(8,128)} %refs_8_.1) | copy-start | bytes 786436
  61.9 27.0 %copy-start.2 = (f32[512,128]{1,0:T(8,128)S(1)}, f32[512,128]{1,0:T(8,128)}, u32[]{:S(2)}) copy-start(f32[512,128]{1,0:T(8,128)} %refs_9_.3) | copy-start | bytes 786436
  61.9 27.0 %copy-start.3 = (f32[512,128]{1,0:T(8,128)S(1)}, f32[512,128]{1,0:T(8,128)}, u32[]{:S(2)}) copy-start(f32[512,128]{1,0:T(8,128)} %refs_5_.3) | copy-start | bytes 786436
  61.9 27.0 %copy-start.4 = (f32[128,256]{1,0:T(8,128)S(1)}, f32[128,256]{1,0:T(8,128)}, u32[]{:S(2)}) copy-start(f32[128,256]{1,0:T(8,128)} %get-tuple-element.64.refs_3_.refs_6_) | copy-start | bytes 393220
  61.9 27.0 %copy-start.5 = (f32[128,512]{1,0:T(8,128)S(1)}, f32[128,512]{1,0:T(8,128)}, u32[]{:S(2)}) copy-start(f32[128,512]{1,0:T(8,128)} %get-tuple-element.69.refs_13_) | copy-start | bytes 786436
  61.9 27.0 %copy-start.6 = (f32[64,512]{1,0:T(8,128)S(1)}, f32[64,512]{1,0:T(8,128)}, u32[]{:S(2)}) copy-start(f32[64,512]{1,0:T(8,128)} %get-tuple-element.62.refs_0_) | copy-start | bytes 393220
  61.9 27.0 %copy-start.7 = (f32[64,512]{1,0:T(8,128)S(1)}, f32[64,512]{1,0:T(8,128)}, u32[]{:S(2)}) copy-start(f32[64,512]{1,0:T(8,128)} %get-tuple-element.63.refs_1_) | copy-start | bytes 393220
  61.9 27.0 %copy-start.8 = (f32[16,512]{1,0:T(8,128)S(1)}, f32[16,512]{1,0:T(8,128)}, u32[]{:S(2)}) copy-start(f32[16,512]{1,0:T(8,128)} %get-tuple-element.65.refs_7_) | copy-start | bytes 98308
  61.9 27.0 %copy-start.9 = (f32[512]{0:T(512)S(1)}, f32[512]{0:T(512)}, u32[]{:S(2)}) copy-start(f32[512]{0:T(512)} %param.23) | copy-start | bytes 6148
  61.9 27.0 %copy-start.10 = (f32[512]{0:T(512)S(1)}, f32[512]{0:T(512)}, u32[]{:S(2)}) copy-start(f32[512]{0:T(512)} %param.24) | copy-start | bytes 6148

commit v10 on v9

--- a/solution.py
+++ b/solution.py
@@ -399,9 +399,11 @@
         next_packs, own_pairs = packs(index), pairs(index)
         d_query = None
         before(next_packs, parts[0], here)
+        if len(parts) > 1:
+            before(next_packs, parts[1], here)
         for n, part in enumerate(parts):
-            if n + 1 < len(parts):
-                before(next_packs, parts[n + 1], here)
+            if n + 2 < len(parts):
+                before(next_packs, parts[n + 2], here)
             middle(index, slot, part, here)
             if n >= 1:
                 term = after(index, own_pairs, parts[n - 1], here)
@@ -509,20 +511,22 @@
     far_siblings = [step * 2 + other_core for step in others(chip, chips)]
     mine = pl.ds(pl.multiple_of(z * piece, 8), piece)
 
-    def pair_copy(index, slot):
-        return pltpu.make_async_copy(
-            pair.at[0, pl.ds(index * group, group)], pair_buf.at[slot], pair_sem.at[slot]
-        )
+    def pair_copies(index, slot):
+        return [
+            pltpu.make_async_copy(pair.at[0, index * group + n], pair_buf.at[slot, n], pair_sem.at[slot, n])
+            for n in range(group)
+        ]
 
     meeting = [{"head": peer} for peer in peers] + [sibling]
     meeting += [team_device(peer, core, chips) for peer in far_teams]
     greet(meeting)
-    for n in range(2):
-        pair_copy(n, n).start()
 
     normal, _ = normalize(atoms[...])
     normed = halves(normal * gain_one[...] + bias_one[...])
     meet(meeting)
+    for n in range(2):
+        for copy in pair_copies(n, n):
+            copy.start()
     copies = []
     squads, _, _, fewer, _ = w_all.shape
     close = squads // dps
@@ -613,7 +617,8 @@
 
     def step(index, carry):
         slot = lax.rem(index, 2)
-        pair_copy(index, slot).wait()
+        for copy in pair_copies(index, slot):
+            copy.wait()
         low_row = pl.multiple_of(index * (8 * group), 8 * group)
         some = pl.ds(low_row, 8 * group)
         values = pl.ds(pl.multiple_of(feats + low_row, 8), 8 * group)
@@ -643,7 +648,8 @@
 
         @pl.when(index + 2 < groups)
         def _():
-            pair_copy(index + 2, slot).start()
+            for copy in pair_copies(index + 2, slot):
+                copy.start()
 
         return carry
 
@@ -853,7 +859,7 @@
             one_up, one_up, one_up,
             pltpu.VMEM((teams, 2, down_rows, width), F32),
             one_down, one_down, one_down,
-            dma((2,)),
+            dma((2, group)),
             dma((blocks,)), dma((blocks,)),
             dma((hops,)), dma((hops, blocks // 2)), dma((max(1, blocks // 2 - 1), hops)), dma((blocks, zs)),
             dma((hops,)), dma((hops,)),

time: 132 us -> 132 us (level)
  no operation moved by 1% of the time
where the time goes in v10:
time: 132 us; the launch traced here: 131 us
  Pallas kernels  124 us (94%)
  starting transfers between devices  5.92 us (4%)
    pallas_call x4, Pallas kernels, staged_call(): pl.pallas_call(body, out_shape=[jax.ShapeDtypeStruct(value.shape, value.d...  124 us
    ppermute x3, starting transfers between devices, local(): lax.ppermute(parcel, 'head', [(source, (source + n + 1) % zs) for source...  4.24 us
  transfers between devices with their start and end apart: 4, of which 0 were waited for; matrix products, arithmetic and copies ran while one was open for 0% of the time, Pallas kernels for 20%

profile of v10, /device:TPU:0, one launch (start us, length us, event | category | flops | bytes accessed | tf_op | source)
XLA Modules:
  0.0 130.9 jit_solution(15208526755912701238)
XLA Ops:
  0.7 55.5 %front.1 = (f32[128,256]{1,0:T(8,128)}, f32[4,264,256]{2,1,0:T(8,128)}, f32[256,128]{1,0:T(8,128)}, f32[16,256,128]{2,1,0:T(8,128)}, f32[128,256]{1,0:T(8,128)},...) custom-call(f32[256,512]{1,0:T(8,128)} %bitcast.23, ...), custom_call_target="tpu_custom_call" | custom-call | tf_op jit(solution)/shard_map/front/pallas_call | solution.py:181
  56.1 1.0 collective-permute-start
  57.1 1.5 %collective-permute-start.1 = (f32[128,512]{1,0:T(8,128)}, f32[128,512]{1,0:T(8,128)S(1)}, u32[]{:S(2)}, u32[]{:S(2)}) collective-permute-start(f32[128,512]{1,0:T(8,128)} %get-tuple-element.67), channel_id=1, source_target_pairs={{0,4},{2,6},{4,0},{6,2},{1,5},{3,7},{5,1},{7,3},{8,12},{10,14},{12... | collective-permute-start | bytes 786440 | tf_op jit(solution)/shard_map/ppermute | solution.py:1179
  58.6 1.8 %collective-permute-start.2 = (f32[128,512]{1,0:T(8,128)}, f32[128,512]{1,0:T(8,128)S(1)}, u32[]{:S(2)}, u32[]{:S(2)}) collective-permute-start(f32[128,512]{1,0:T(8,128)} %get-tuple-element.68), channel_id=1, source_target_pairs={{0,6},{2,0},{4,2},{6,4},{1,7},{3,1},{5,3},{7,5},{8,14},{10,8},{12,... | collective-permute-start | bytes 786440 | tf_op jit(solution)/shard_map/ppermute | solution.py:1179
  60.4 1.7 %collective-permute-start.3 = (f32[128,512]{1,0:T(8,128)}, f32[128,512]{1,0:T(8,128)S(1)}, u32[]{:S(2)}, u32[]{:S(2)}) collective-permute-start(f32[128,512]{1,0:T(8,128)} %get-tuple-element.69.refs_13_), channel_id=1, source_target_pairs={{0,16},{8,24},{16,0},{24,8},{1,17},{9,25},{17,1},{25,9},{2,18},{10... | collective-permute-start | bytes 786440 | tf_op jit(solution)/shard_map/ppermute | solution.py:1184
  62.1 0.0 copy-start
  62.1 0.0 copy-start.1
  62.1 0.0 copy-start.2
  62.1 0.0 copy-start.3
  62.1 0.0 copy-start.4
  62.1 0.0 copy-start.5
  62.1 0.0 copy-start.6
  62.1 0.0 copy-start.7
  62.1 0.0 copy-start.8
  62.1 0.0 copy-start.9
  62.1 0.0 copy-start.10
  62.1 26.2 %attend_back.1 = (f32[1,16,256,1024]{3,2,1,0:T(8,128)}, f32[1,16,256,1024]{3,2,1,0:T(8,128)}, f32[52,2,256,256]{3,2,1,0:T(8,128)}) custom-call(f32[128,256]{1,0:T(8,128)} %get-tuple-element.70.refs_0_, f32[4,264,256]{2,1,0:T(8,128)} %get-tuple-element.71.refs_1_, f32[128,256]{1,0:T(8,128)} %get-tuple-element.72.refs_2_, ...), custom_call_target="tpu_custom_call" | custom-call | flops 3355443200 | bytes 67108864 | tf_op jit(solution)/shard_map/attend_back/pallas_call | solution.py:181
  88.3 0.0 collective-permute-done.refs_10_
  88.3 0.0 collective-permute-done.1.refs_11_
  88.3 0.0 collective-permute-done.2.refs_12_
  88.4 0.0 collective-permute-done.3.refs_14_
  88.4 0.0 copy-done
  88.4 0.0 copy-done.1
  88.4 0.0 copy-done.2
  88.4 0.0 copy-done.3
  88.4 0.0 copy-done.4
  88.4 0.0 copy-done.5
  88.4 0.0 copy-done.6
  88.4 0.0 copy-done.7
  88.5 0.0 copy-done.8
  88.5 0.0 copy-done.9
  88.5 0.0 copy-done.10
  88.5 39.3 %finish.1 = (f32[256,512]{1,0:T(8,128)S(1)}, f32[256,512]{1,0:T(8,128)S(1)}, f32[4,2,64,512]{3,2,1,0:T(8,128)S(1)}, f32[512,512]{1,0:T(8,128)S(1)}, f32[512,512]...) custom-call(f32[64,512]{1,0:T(8,128)S(1)} %copy-done.6, f32[64,512]{1,0:T(8,128)S(1)} %copy-done.7, ...), custom_call_target="tpu_custom_call" | custom-call | tf_op jit(solution)/shard_map/finish/pallas_call | solution.py:181
  127.8 2.9 %place.1 = (f32[256,512]{1,0:T(8,128)}, f32[256,512]{1,0:T(8,128)}, f32[512,512]{1,0:T(8,128)}, f32[512,512]{1,0:T(8,128)}, f32[1,1]{1,0:T(1,128)}, /*index=5*/f...) custom-call(f32[4,2,64,512]{3,2,1,0:T(8,128)S(1)} %get-tuple-element, ...), custom_call_target="tpu_custom_call" | custom-call | tf_op jit(solution)/shard_map/place/pallas_call | solution.py:181
Async XLA Ops:
  56.1 32.2 %collective-permute-start = (f32[128,512]{1,0:T(8,128)}, f32[128,512]{1,0:T(8,128)S(1)}, u32[]{:S(2)}, u32[]{:S(2)}) collective-permute-start(f32[128,512]{1,0:T(8,128)} %get-tuple-element.66), channel_id=1, source_target_pairs={{0,2},{2,4},{4,6},{6,0},{1,3},{3,5},{5,7},{7,1},{8,10},{10,12},{12... | collective-permute-start | bytes 786440 | tf_op jit(solution)/shard_map/ppermute | solution.py:1179
  57.1 31.2 %collective-permute-start.1 = (f32[128,512]{1,0:T(8,128)}, f32[128,512]{1,0:T(8,128)S(1)}, u32[]{:S(2)}, u32[]{:S(2)}) collective-permute-start(f32[128,512]{1,0:T(8,128)} %get-tuple-element.67), channel_id=1, source_target_pairs={{0,4},{2,6},{4,0},{6,2},{1,5},{3,7},{5,1},{7,3},{8,12},{10,14},{12... | collective-permute-start | bytes 786440 | tf_op jit(solution)/shard_map/ppermute | solution.py:1179
  58.6 29.7 %collective-permute-start.2 = (f32[128,512]{1,0:T(8,128)}, f32[128,512]{1,0:T(8,128)S(1)}, u32[]{:S(2)}, u32[]{:S(2)}) collective-permute-start(f32[128,512]{1,0:T(8,128)} %get-tuple-element.68), channel_id=1, source_target_pairs={{0,6},{2,0},{4,2},{6,4},{1,7},{3,1},{5,3},{7,5},{8,14},{10,8},{12,... | collective-permute-start | bytes 786440 | tf_op jit(solution)/shard_map/ppermute | solution.py:1179
  60.4 28.0 %collective-permute-start.3 = (f32[128,512]{1,0:T(8,128)}, f32[128,512]{1,0:T(8,128)S(1)}, u32[]{:S(2)}, u32[]{:S(2)}) collective-permute-start(f32[128,512]{1,0:T(8,128)} %get-tuple-element.69.refs_13_), channel_id=1, source_target_pairs={{0,16},{8,24},{16,0},{24,8},{1,17},{9,25},{17,1},{25,9},{2,18},{10... | collective-permute-start | bytes 786440 | tf_op jit(solution)/shard_map/ppermute | solution.py:1184
  62.1 26.3 %copy-start = (f32[1,256,512]{2,1,0:T(8,128)S(1)}, f32[1,256,512]{2,1,0:T(8,128)}, u32[]{:S(2)}) copy-start(f32[1,256,512]{2,1,0:T(8,128)} %param.20) | copy-start | bytes 1572868
  62.1 26.3 %copy-start.1 = (f32[512,128]{1,0:T(8,128)S(1)}, f32[512,128]{1,0:T(8,128)}, u32[]{:S(2)}) copy-start(f32[512,128]{1,0:T(8,128)} %refs_8_.1) | copy-start | bytes 786436
  62.1 26.3 %copy-start.2 = (f32[512,128]{1,0:T(8,128)S(1)}, f32[512,128]{1,0:T(8,128)}, u32[]{:S(2)}) copy-start(f32[512,128]{1,0:T(8,128)} %refs_9_.3) | copy-start | bytes 786436
  62.1 26.3 %copy-start.3 = (f32[512,128]{1,0:T(8,128)S(1)}, f32[512,128]{1,0:T(8,128)}, u32[]{:S(2)}) copy-start(f32[512,128]{1,0:T(8,128)} %refs_5_.3) | copy-start | bytes 786436
  62.1 26.3 %copy-start.4 = (f32[128,256]{1,0:T(8,128)S(1)}, f32[128,256]{1,0:T(8,128)}, u32[]{:S(2)}) copy-start(f32[128,256]{1,0:T(8,128)} %get-tuple-element.64.refs_3_.refs_6_) | copy-start | bytes 393220
  62.1 26.3 %copy-start.5 = (f32[128,512]{1,0:T(8,128)S(1)}, f32[128,512]{1,0:T(8,128)}, u32[]{:S(2)}) copy-start(f32[128,512]{1,0:T(8,128)} %get-tuple-element.69.refs_13_) | copy-start | bytes 786436
  62.1 26.3 %copy-start.6 = (f32[64,512]{1,0:T(8,128)S(1)}, f32[64,512]{1,0:T(8,128)}, u32[]{:S(2)}) copy-start(f32[64,512]{1,0:T(8,128)} %get-tuple-element.62.refs_0_) | copy-start | bytes 393220
  62.1 26.3 %copy-start.7 = (f32[64,512]{1,0:T(8,128)S(1)}, f32[64,512]{1,0:T(8,128)}, u32[]{:S(2)}) copy-start(f32[64,512]{1,0:T(8,128)} %get-tuple-element.63.refs_1_) | copy-start | bytes 393220
  62.1 26.3 %copy-start.8 = (f32[16,512]{1,0:T(8,128)S(1)}, f32[16,512]{1,0:T(8,128)}, u32[]{:S(2)}) copy-start(f32[16,512]{1,0:T(8,128)} %get-tuple-element.65.refs_7_) | copy-start | bytes 98308
  62.1 26.3 %copy-start.9 = (f32[512]{0:T(512)S(1)}, f32[512]{0:T(512)}, u32[]{:S(2)}) copy-start(f32[512]{0:T(512)} %param.23) | copy-start | bytes 6148
  62.1 26.3 %copy-start.10 = (f32[512]{0:T(512)S(1)}, f32[512]{0:T(512)}, u32[]{:S(2)}) copy-start(f32[512]{0:T(512)} %param.24) | copy-start | bytes 6148

commit v11 on v10

--- a/solution.py
+++ b/solution.py
@@ -774,6 +774,7 @@
     for n in range(zs):
         some = slice(n * feats, (n + 1) * feats)
         back[n] = dot_halves(d_halves, (outs[0][some], outs[1][some]), NT)
+    settled = len(copies)
     copies += [
         send(back.at[peer], back_landed.at[z], back_send.at[n], back_recv.at[n], {"head": peer})
         for n, peer in enumerate(peers)
@@ -799,19 +800,21 @@
         shares[there, columns_of] = up_share[rows_of]
     shares[there.stop :, :] = down_share
     shares.flush()
+    for copy in copies[:settled] + squad_copies + key_copies:
+        copy.wait_send()
+
+    def drain(index, carry):
+        for copy in mix_copies(index):
+            copy.wait_send()
+        return carry
+
+    lax.fori_loop(0, groups, drain, 0)
     for n, source in enumerate(sources):
         arrived(back_landed.at[source], back_recv.at[n])
     d_mixed[...] = back_landed[...].reshape(rows, feats).T
     d_mixed.flush()
-    for copy in copies + squad_copies + key_copies:
+    for copy in copies[settled:]:
         copy.wait_send()
-
-    def drain(index, carry):
-        for copy in mix_copies(index):
-            copy.wait_send()
-        return carry
-
-    lax.fori_loop(0, groups, drain, 0)
 
 
 def front(zs, dps, teams, pair, *operands):
@@ -1000,6 +1003,7 @@
     grad_atoms[mine, :] = d_hidden[...] + normalize_back(d_normed, gain[...], normal, rate)
     small_z[z, SMALL_LN1_GAIN : SMALL_LN1_GAIN + 1, :] = column_sum(d_normed * normal)
     small_z[z, SMALL_LN1_BIAS : SMALL_LN1_BIAS + 1, :] = column_sum(d_normed)
+    settled = len(copies)
     copies += [
         send(small_z.at[z], small_z.at[z], small_z_send.at[n], small_z_recv.at[z], {"head": peer})
         for n, peer in enumerate(peers)
@@ -1040,6 +1044,8 @@
                 arrived(ready, sem)
 
             copies.append(send(ready, ready, bf_send.at[kind, n], b_recv.at[kind, n, core], sibling))
+    for copy in copies[:settled]:
+        copy.wait_send()
     for source in far_places:
         arrived(small_all.at[source], small_recv.at[source])
     summed = functools.reduce(jnp.add, [small_all[n] for n in range(2 * teams)])
@@ -1060,7 +1066,7 @@
     for peer in peers:
         there = pl.ds(pl.multiple_of(peer * piece, 8), piece)
         arrived(grad_atoms.at[there], back_recv.at[peer])
-    for copy in copies:
+    for copy in copies[settled:]:
         copy.wait_send()
 
 

time: 132 us -> 132 us (level)
  no operation moved by 1% of the time
where the time goes in v11:
time: 132 us; the launch traced here: 131 us
  Pallas kernels  124 us (94%)
  starting transfers between devices  5.92 us (4%)
    pallas_call x4, Pallas kernels, staged_call(): pl.pallas_call(body, out_shape=[jax.ShapeDtypeStruct(value.shape, value.d...  124 us
    ppermute x3, starting transfers between devices, local(): lax.ppermute(parcel, 'head', [(source, (source + n + 1) % zs) for source...  4.24 us
  transfers between devices with their start and end apart: 4, of which 0 were waited for; matrix products, arithmetic and copies ran while one was open for 0% of the time, Pallas kernels for 20%

profile of v11, /device:TPU:0, one launch (start us, length us, event | category | flops | bytes accessed | tf_op | source)
XLA Modules:
  0.0 130.9 jit_solution(7224065887926207391)
XLA Ops:
  0.7 55.5 %front.1 = (f32[128,256]{1,0:T(8,128)}, f32[4,264,256]{2,1,0:T(8,128)}, f32[256,128]{1,0:T(8,128)}, f32[16,256,128]{2,1,0:T(8,128)}, f32[128,256]{1,0:T(8,128)},...) custom-call(f32[256,512]{1,0:T(8,128)} %bitcast.23, ...), custom_call_target="tpu_custom_call" | custom-call | tf_op jit(solution)/shard_map/front/pallas_call | solution.py:181
  56.1 1.0 collective-permute-start
  57.1 1.5 %collective-permute-start.1 = (f32[128,512]{1,0:T(8,128)}, f32[128,512]{1,0:T(8,128)S(1)}, u32[]{:S(2)}, u32[]{:S(2)}) collective-permute-start(f32[128,512]{1,0:T(8,128)} %get-tuple-element.67), channel_id=1, source_target_pairs={{0,4},{2,6},{4,0},{6,2},{1,5},{3,7},{5,1},{7,3},{8,12},{10,14},{12... | collective-permute-start | bytes 786440 | tf_op jit(solution)/shard_map/ppermute | solution.py:1185
  58.6 1.8 %collective-permute-start.2 = (f32[128,512]{1,0:T(8,128)}, f32[128,512]{1,0:T(8,128)S(1)}, u32[]{:S(2)}, u32[]{:S(2)}) collective-permute-start(f32[128,512]{1,0:T(8,128)} %get-tuple-element.68), channel_id=1, source_target_pairs={{0,6},{2,0},{4,2},{6,4},{1,7},{3,1},{5,3},{7,5},{8,14},{10,8},{12,... | collective-permute-start | bytes 786440 | tf_op jit(solution)/shard_map/ppermute | solution.py:1185
  60.4 1.7 %collective-permute-start.3 = (f32[128,512]{1,0:T(8,128)}, f32[128,512]{1,0:T(8,128)S(1)}, u32[]{:S(2)}, u32[]{:S(2)}) collective-permute-start(f32[128,512]{1,0:T(8,128)} %get-tuple-element.69.refs_13_), channel_id=1, source_target_pairs={{0,16},{8,24},{16,0},{24,8},{1,17},{9,25},{17,1},{25,9},{2,18},{10... | collective-permute-start | bytes 786440 | tf_op jit(solution)/shard_map/ppermute | solution.py:1190
  62.1 0.0 copy-start
  62.1 0.0 copy-start.1
  62.1 0.0 copy-start.2
  62.1 0.0 copy-start.3
  62.1 0.0 copy-start.4
  62.1 0.0 copy-start.5
  62.1 0.0 copy-start.6
  62.1 0.0 copy-start.7
  62.1 0.0 copy-start.8
  62.1 0.0 copy-start.9
  62.1 0.0 copy-start.10
  62.1 26.2 %attend_back.1 = (f32[1,16,256,1024]{3,2,1,0:T(8,128)}, f32[1,16,256,1024]{3,2,1,0:T(8,128)}, f32[52,2,256,256]{3,2,1,0:T(8,128)}) custom-call(f32[128,256]{1,0:T(8,128)} %get-tuple-element.70.refs_0_, f32[4,264,256]{2,1,0:T(8,128)} %get-tuple-element.71.refs_1_, f32[128,256]{1,0:T(8,128)} %get-tuple-element.72.refs_2_, ...), custom_call_target="tpu_custom_call" | custom-call | flops 3355443200 | bytes 67108864 | tf_op jit(solution)/shard_map/attend_back/pallas_call | solution.py:181
  88.3 0.0 collective-permute-done.refs_10_
  88.3 0.0 collective-permute-done.1.refs_11_
  88.3 0.0 collective-permute-done.2.refs_12_
  88.4 0.0 collective-permute-done.3.refs_14_
  88.4 0.0 copy-done
  88.4 0.0 copy-done.1
  88.4 0.0 copy-done.2
  88.4 0.0 copy-done.3
  88.4 0.0 copy-done.4
  88.4 0.0 copy-done.5
  88.4 0.0 copy-done.6
  88.4 0.0 copy-done.7
  88.5 0.0 copy-done.8
  88.5 0.0 copy-done.9
  88.5 0.0 copy-done.10
  88.5 39.3 %finish.1 = (f32[256,512]{1,0:T(8,128)S(1)}, f32[256,512]{1,0:T(8,128)S(1)}, f32[4,2,64,512]{3,2,1,0:T(8,128)S(1)}, f32[512,512]{1,0:T(8,128)S(1)}, f32[512,512]...) custom-call(f32[64,512]{1,0:T(8,128)S(1)} %copy-done.6, f32[64,512]{1,0:T(8,128)S(1)} %copy-done.7, ...), custom_call_target="tpu_custom_call" | custom-call | tf_op jit(solution)/shard_map/finish/pallas_call | solution.py:181
  127.8 2.9 %place.1 = (f32[256,512]{1,0:T(8,128)}, f32[256,512]{1,0:T(8,128)}, f32[512,512]{1,0:T(8,128)}, f32[512,512]{1,0:T(8,128)}, f32[1,1]{1,0:T(1,128)}, /*index=5*/f...) custom-call(f32[4,2,64,512]{3,2,1,0:T(8,128)S(1)} %get-tuple-element, ...), custom_call_target="tpu_custom_call" | custom-call | tf_op jit(solution)/shard_map/place/pallas_call | solution.py:181
Async XLA Ops:
  56.1 32.2 %collective-permute-start = (f32[128,512]{1,0:T(8,128)}, f32[128,512]{1,0:T(8,128)S(1)}, u32[]{:S(2)}, u32[]{:S(2)}) collective-permute-start(f32[128,512]{1,0:T(8,128)} %get-tuple-element.66), channel_id=1, source_target_pairs={{0,2},{2,4},{4,6},{6,0},{1,3},{3,5},{5,7},{7,1},{8,10},{10,12},{12... | collective-permute-start | bytes 786440 | tf_op jit(solution)/shard_map/ppermute | solution.py:1185
  57.1 31.2 %collective-permute-start.1 = (f32[128,512]{1,0:T(8,128)}, f32[128,512]{1,0:T(8,128)S(1)}, u32[]{:S(2)}, u32[]{:S(2)}) collective-permute-start(f32[128,512]{1,0:T(8,128)} %get-tuple-element.67), channel_id=1, source_target_pairs={{0,4},{2,6},{4,0},{6,2},{1,5},{3,7},{5,1},{7,3},{8,12},{10,14},{12... | collective-permute-start | bytes 786440 | tf_op jit(solution)/shard_map/ppermute | solution.py:1185
  58.6 29.7 %collective-permute-start.2 = (f32[128,512]{1,0:T(8,128)}, f32[128,512]{1,0:T(8,128)S(1)}, u32[]{:S(2)}, u32[]{:S(2)}) collective-permute-start(f32[128,512]{1,0:T(8,128)} %get-tuple-element.68), channel_id=1, source_target_pairs={{0,6},{2,0},{4,2},{6,4},{1,7},{3,1},{5,3},{7,5},{8,14},{10,8},{12,... | collective-permute-start | bytes 786440 | tf_op jit(solution)/shard_map/ppermute | solution.py:1185
  60.4 28.0 %collective-permute-start.3 = (f32[128,512]{1,0:T(8,128)}, f32[128,512]{1,0:T(8,128)S(1)}, u32[]{:S(2)}, u32[]{:S(2)}) collective-permute-start(f32[128,512]{1,0:T(8,128)} %get-tuple-element.69.refs_13_), channel_id=1, source_target_pairs={{0,16},{8,24},{16,0},{24,8},{1,17},{9,25},{17,1},{25,9},{2,18},{10... | collective-permute-start | bytes 786440 | tf_op jit(solution)/shard_map/ppermute | solution.py:1190
  62.1 26.3 %copy-start = (f32[1,256,512]{2,1,0:T(8,128)S(1)}, f32[1,256,512]{2,1,0:T(8,128)}, u32[]{:S(2)}) copy-start(f32[1,256,512]{2,1,0:T(8,128)} %param.20) | copy-start | bytes 1572868
  62.1 26.3 %copy-start.1 = (f32[512,128]{1,0:T(8,128)S(1)}, f32[512,128]{1,0:T(8,128)}, u32[]{:S(2)}) copy-start(f32[512,128]{1,0:T(8,128)} %refs_8_.1) | copy-start | bytes 786436
  62.1 26.3 %copy-start.2 = (f32[512,128]{1,0:T(8,128)S(1)}, f32[512,128]{1,0:T(8,128)}, u32[]{:S(2)}) copy-start(f32[512,128]{1,0:T(8,128)} %refs_9_.3) | copy-start | bytes 786436
  62.1 26.3 %copy-start.3 = (f32[512,128]{1,0:T(8,128)S(1)}, f32[512,128]{1,0:T(8,128)}, u32[]{:S(2)}) copy-start(f32[512,128]{1,0:T(8,128)} %refs_5_.3) | copy-start | bytes 786436
  62.1 26.3 %copy-start.4 = (f32[128,256]{1,0:T(8,128)S(1)}, f32[128,256]{1,0:T(8,128)}, u32[]{:S(2)}) copy-start(f32[128,256]{1,0:T(8,128)} %get-tuple-element.64.refs_3_.refs_6_) | copy-start | bytes 393220
  62.1 26.3 %copy-start.5 = (f32[128,512]{1,0:T(8,128)S(1)}, f32[128,512]{1,0:T(8,128)}, u32[]{:S(2)}) copy-start(f32[128,512]{1,0:T(8,128)} %get-tuple-element.69.refs_13_) | copy-start | bytes 786436
  62.1 26.3 %copy-start.6 = (f32[64,512]{1,0:T(8,128)S(1)}, f32[64,512]{1,0:T(8,128)}, u32[]{:S(2)}) copy-start(f32[64,512]{1,0:T(8,128)} %get-tuple-element.62.refs_0_) | copy-start | bytes 393220
  62.1 26.3 %copy-start.7 = (f32[64,512]{1,0:T(8,128)S(1)}, f32[64,512]{1,0:T(8,128)}, u32[]{:S(2)}) copy-start(f32[64,512]{1,0:T(8,128)} %get-tuple-element.63.refs_1_) | copy-start | bytes 393220
  62.1 26.3 %copy-start.8 = (f32[16,512]{1,0:T(8,128)S(1)}, f32[16,512]{1,0:T(8,128)}, u32[]{:S(2)}) copy-start(f32[16,512]{1,0:T(8,128)} %get-tuple-element.65.refs_7_) | copy-start | bytes 98308
  62.1 26.3 %copy-start.9 = (f32[512]{0:T(512)S(1)}, f32[512]{0:T(512)}, u32[]{:S(2)}) copy-start(f32[512]{0:T(512)} %param.23) | copy-start | bytes 6148
  62.1 26.3 %copy-start.10 = (f32[512]{0:T(512)S(1)}, f32[512]{0:T(512)}, u32[]{:S(2)}) copy-start(f32[512]{0:T(512)} %param.24) | copy-start | bytes 6148

commit v12 on v10

--- a/solution.py
+++ b/solution.py
@@ -398,18 +398,15 @@
 
         next_packs, own_pairs = packs(index), pairs(index)
         d_query = None
-        before(next_packs, parts[0], here)
-        if len(parts) > 1:
-            before(next_packs, parts[1], here)
-        for n, part in enumerate(parts):
-            if n + 2 < len(parts):
-                before(next_packs, parts[n + 2], here)
-            middle(index, slot, part, here)
-            if n >= 1:
-                term = after(index, own_pairs, parts[n - 1], here)
+        ahead, behind = 3, 1
+        for n in range(-ahead, len(parts) + behind):
+            if 0 <= n + ahead < len(parts):
+                before(next_packs, parts[n + ahead], here)
+            if 0 <= n < len(parts):
+                middle(index, slot, parts[n], here)
+            if 0 <= n - behind < len(parts):
+                term = after(index, own_pairs, parts[n - behind], here)
                 d_query = term if d_query is None else d_query + term
-        term = after(index, own_pairs, parts[-1], here)
-        d_query = term if d_query is None else d_query + term
         d_heads[blocks // 2, 0, rows_of(index), :] = d_query * (DH ** (-0.5))
         for copy in outward(index):
             copy.start()

time: 132 us -> 132 us (level)
  no operation moved by 1% of the time
where the time goes in v12:
time: 132 us; the launch traced here: 131 us
  Pallas kernels  124 us (94%)
  starting transfers between devices  5.92 us (4%)
    pallas_call x4, Pallas kernels, staged_call(): pl.pallas_call(body, out_shape=[jax.ShapeDtypeStruct(value.shape, value.d...  124 us
    ppermute x3, starting transfers between devices, local(): lax.ppermute(parcel, 'head', [(source, (source + n + 1) % zs) for source...  4.24 us
  transfers between devices with their start and end apart: 4, of which 0 were waited for; matrix products, arithmetic and copies ran while one was open for 0% of the time, Pallas kernels for 20%

profile of v12, /device:TPU:0, one launch (start us, length us, event | category | flops | bytes accessed | tf_op | source)
XLA Modules:
  0.0 130.9 jit_solution(15208526755912701238)
XLA Ops:
  0.7 55.5 %front.1 = (f32[128,256]{1,0:T(8,128)}, f32[4,264,256]{2,1,0:T(8,128)}, f32[256,128]{1,0:T(8,128)}, f32[16,256,128]{2,1,0:T(8,128)}, f32[128,256]{1,0:T(8,128)},...) custom-call(f32[256,512]{1,0:T(8,128)} %bitcast.23, ...), custom_call_target="tpu_custom_call" | custom-call | tf_op jit(solution)/shard_map/front/pallas_call | solution.py:181
  56.1 1.0 collective-permute-start
  57.1 1.5 %collective-permute-start.1 = (f32[128,512]{1,0:T(8,128)}, f32[128,512]{1,0:T(8,128)S(1)}, u32[]{:S(2)}, u32[]{:S(2)}) collective-permute-start(f32[128,512]{1,0:T(8,128)} %get-tuple-element.67), channel_id=1, source_target_pairs={{0,4},{2,6},{4,0},{6,2},{1,5},{3,7},{5,1},{7,3},{8,12},{10,14},{12... | collective-permute-start | bytes 786440 | tf_op jit(solution)/shard_map/ppermute | solution.py:1176
  58.6 1.8 %collective-permute-start.2 = (f32[128,512]{1,0:T(8,128)}, f32[128,512]{1,0:T(8,128)S(1)}, u32[]{:S(2)}, u32[]{:S(2)}) collective-permute-start(f32[128,512]{1,0:T(8,128)} %get-tuple-element.68), channel_id=1, source_target_pairs={{0,6},{2,0},{4,2},{6,4},{1,7},{3,1},{5,3},{7,5},{8,14},{10,8},{12,... | collective-permute-start | bytes 786440 | tf_op jit(solution)/shard_map/ppermute | solution.py:1176
  60.4 1.7 %collective-permute-start.3 = (f32[128,512]{1,0:T(8,128)}, f32[128,512]{1,0:T(8,128)S(1)}, u32[]{:S(2)}, u32[]{:S(2)}) collective-permute-start(f32[128,512]{1,0:T(8,128)} %get-tuple-element.69.refs_13_), channel_id=1, source_target_pairs={{0,16},{8,24},{16,0},{24,8},{1,17},{9,25},{17,1},{25,9},{2,18},{10... | collective-permute-start | bytes 786440 | tf_op jit(solution)/shard_map/ppermute | solution.py:1181
  62.1 0.0 copy-start
  62.1 0.0 copy-start.1
  62.1 0.0 copy-start.2
  62.1 0.0 copy-start.3
  62.1 0.0 copy-start.4
  62.1 0.0 copy-start.5
  62.1 0.0 copy-start.6
  62.1 0.0 copy-start.7
  62.1 0.0 copy-start.8
  62.1 0.0 copy-start.9
  62.1 0.0 copy-start.10
  62.1 26.2 %attend_back.1 = (f32[1,16,256,1024]{3,2,1,0:T(8,128)}, f32[1,16,256,1024]{3,2,1,0:T(8,128)}, f32[52,2,256,256]{3,2,1,0:T(8,128)}) custom-call(f32[128,256]{1,0:T(8,128)} %get-tuple-element.70.refs_0_, f32[4,264,256]{2,1,0:T(8,128)} %get-tuple-element.71.refs_1_, f32[128,256]{1,0:T(8,128)} %get-tuple-element.72.refs_2_, ...), custom_call_target="tpu_custom_call" | custom-call | flops 3355443200 | bytes 67108864 | tf_op jit(solution)/shard_map/attend_back/pallas_call | solution.py:181
  88.3 0.0 collective-permute-done.refs_10_
  88.3 0.0 collective-permute-done.1.refs_11_
  88.3 0.0 collective-permute-done.2.refs_12_
  88.4 0.0 collective-permute-done.3.refs_14_
  88.4 0.0 copy-done
  88.4 0.0 copy-done.1
  88.4 0.0 copy-done.2
  88.4 0.0 copy-done.3
  88.4 0.0 copy-done.4
  88.4 0.0 copy-done.5
  88.4 0.0 copy-done.6
  88.4 0.0 copy-done.7
  88.5 0.0 copy-done.8
  88.5 0.0 copy-done.9
  88.5 0.0 copy-done.10
  88.5 39.3 %finish.1 = (f32[256,512]{1,0:T(8,128)S(1)}, f32[256,512]{1,0:T(8,128)S(1)}, f32[4,2,64,512]{3,2,1,0:T(8,128)S(1)}, f32[512,512]{1,0:T(8,128)S(1)}, f32[512,512]...) custom-call(f32[64,512]{1,0:T(8,128)S(1)} %copy-done.6, f32[64,512]{1,0:T(8,128)S(1)} %copy-done.7, ...), custom_call_target="tpu_custom_call" | custom-call | tf_op jit(solution)/shard_map/finish/pallas_call | solution.py:181
  127.8 2.9 %place.1 = (f32[256,512]{1,0:T(8,128)}, f32[256,512]{1,0:T(8,128)}, f32[512,512]{1,0:T(8,128)}, f32[512,512]{1,0:T(8,128)}, f32[1,1]{1,0:T(1,128)}, /*index=5*/f...) custom-call(f32[4,2,64,512]{3,2,1,0:T(8,128)S(1)} %get-tuple-element, ...), custom_call_target="tpu_custom_call" | custom-call | tf_op jit(solution)/shard_map/place/pallas_call | solution.py:181
Async XLA Ops:
  56.1 32.2 %collective-permute-start = (f32[128,512]{1,0:T(8,128)}, f32[128,512]{1,0:T(8,128)S(1)}, u32[]{:S(2)}, u32[]{:S(2)}) collective-permute-start(f32[128,512]{1,0:T(8,128)} %get-tuple-element.66), channel_id=1, source_target_pairs={{0,2},{2,4},{4,6},{6,0},{1,3},{3,5},{5,7},{7,1},{8,10},{10,12},{12... | collective-permute-start | bytes 786440 | tf_op jit(solution)/shard_map/ppermute | solution.py:1176
  57.1 31.2 %collective-permute-start.1 = (f32[128,512]{1,0:T(8,128)}, f32[128,512]{1,0:T(8,128)S(1)}, u32[]{:S(2)}, u32[]{:S(2)}) collective-permute-start(f32[128,512]{1,0:T(8,128)} %get-tuple-element.67), channel_id=1, source_target_pairs={{0,4},{2,6},{4,0},{6,2},{1,5},{3,7},{5,1},{7,3},{8,12},{10,14},{12... | collective-permute-start | bytes 786440 | tf_op jit(solution)/shard_map/ppermute | solution.py:1176
  58.6 29.7 %collective-permute-start.2 = (f32[128,512]{1,0:T(8,128)}, f32[128,512]{1,0:T(8,128)S(1)}, u32[]{:S(2)}, u32[]{:S(2)}) collective-permute-start(f32[128,512]{1,0:T(8,128)} %get-tuple-element.68), channel_id=1, source_target_pairs={{0,6},{2,0},{4,2},{6,4},{1,7},{3,1},{5,3},{7,5},{8,14},{10,8},{12,... | collective-permute-start | bytes 786440 | tf_op jit(solution)/shard_map/ppermute | solution.py:1176
  60.4 28.0 %collective-permute-start.3 = (f32[128,512]{1,0:T(8,128)}, f32[128,512]{1,0:T(8,128)S(1)}, u32[]{:S(2)}, u32[]{:S(2)}) collective-permute-start(f32[128,512]{1,0:T(8,128)} %get-tuple-element.69.refs_13_), channel_id=1, source_target_pairs={{0,16},{8,24},{16,0},{24,8},{1,17},{9,25},{17,1},{25,9},{2,18},{10... | collective-permute-start | bytes 786440 | tf_op jit(solution)/shard_map/ppermute | solution.py:1181
  62.1 26.3 %copy-start = (f32[1,256,512]{2,1,0:T(8,128)S(1)}, f32[1,256,512]{2,1,0:T(8,128)}, u32[]{:S(2)}) copy-start(f32[1,256,512]{2,1,0:T(8,128)} %param.20) | copy-start | bytes 1572868
  62.1 26.3 %copy-start.1 = (f32[512,128]{1,0:T(8,128)S(1)}, f32[512,128]{1,0:T(8,128)}, u32[]{:S(2)}) copy-start(f32[512,128]{1,0:T(8,128)} %refs_8_.1) | copy-start | bytes 786436
  62.1 26.3 %copy-start.2 = (f32[512,128]{1,0:T(8,128)S(1)}, f32[512,128]{1,0:T(8,128)}, u32[]{:S(2)}) copy-start(f32[512,128]{1,0:T(8,128)} %refs_9_.3) | copy-start | bytes 786436
  62.1 26.3 %copy-start.3 = (f32[512,128]{1,0:T(8,128)S(1)}, f32[512,128]{1,0:T(8,128)}, u32[]{:S(2)}) copy-start(f32[512,128]{1,0:T(8,128)} %refs_5_.3) | copy-start | bytes 786436
  62.1 26.3 %copy-start.4 = (f32[128,256]{1,0:T(8,128)S(1)}, f32[128,256]{1,0:T(8,128)}, u32[]{:S(2)}) copy-start(f32[128,256]{1,0:T(8,128)} %get-tuple-element.64.refs_3_.refs_6_) | copy-start | bytes 393220
  62.1 26.3 %copy-start.5 = (f32[128,512]{1,0:T(8,128)S(1)}, f32[128,512]{1,0:T(8,128)}, u32[]{:S(2)}) copy-start(f32[128,512]{1,0:T(8,128)} %get-tuple-element.69.refs_13_) | copy-start | bytes 786436
  62.1 26.3 %copy-start.6 = (f32[64,512]{1,0:T(8,128)S(1)}, f32[64,512]{1,0:T(8,128)}, u32[]{:S(2)}) copy-start(f32[64,512]{1,0:T(8,128)} %get-tuple-element.62.refs_0_) | copy-start | bytes 393220
  62.1 26.3 %copy-start.7 = (f32[64,512]{1,0:T(8,128)S(1)}, f32[64,512]{1,0:T(8,128)}, u32[]{:S(2)}) copy-start(f32[64,512]{1,0:T(8,128)} %get-tuple-element.63.refs_1_) | copy-start | bytes 393220
  62.1 26.3 %copy-start.8 = (f32[16,512]{1,0:T(8,128)S(1)}, f32[16,512]{1,0:T(8,128)}, u32[]{:S(2)}) copy-start(f32[16,512]{1,0:T(8,128)} %get-tuple-element.65.refs_7_) | copy-start | bytes 98308
  62.1 26.3 %copy-start.9 = (f32[512]{0:T(512)S(1)}, f32[512]{0:T(512)}, u32[]{:S(2)}) copy-start(f32[512]{0:T(512)} %param.23) | copy-start | bytes 6148
  62.1 26.3 %copy-start.10 = (f32[512]{0:T(512)S(1)}, f32[512]{0:T(512)}, u32[]{:S(2)}) copy-start(f32[512]{0:T(512)} %param.24) | copy-start | bytes 6148
